TPU v7x, 256 devices: a whole 4x4x8 slice. The times are simulated.
256 devices in a mesh: seq: 32 (over y, x, core), chan: 8 (over z).
Axes of the slice: x: 4, y: 4, z: 8, core: 2. Of those that a mesh axis runs over, the one named last changes fastest.
Arguments:
- tokens: bfloat16 [8192, 4096], P('seq', 'chan'), may hold values from -6 to 6
- input_weight: bfloat16 [3, 4096, 4096], P(None, 'seq', 'chan'), may hold values from -0.09375 to 0.09375
- short_taps: float32 [3, 3, 4096], P(None, None, 'chan'), may hold values from -3 to 3
- residue: float32 [16, 4096], P(None, 'chan'), may hold values from -1.5 to 1.5
- decay_rate: float32 [16, 4096], P(None, 'chan'), may hold values from 0.1 to 409
- out_weight: bfloat16 [4096, 4096], P('chan'), may hold values from -0.125 to 0.125
Outputs:
- hyena_out: bfloat16 [8192, 4096], P('seq', 'chan')
All inputs are finite; a program needn't handle non-finite values.
Results may differ from a plain program's by a relative error of at most 0.025.
Values may be sent and summed in bfloat16 or wider, within the bound.
No kernel may reach another device: no remote copies, remote signals or barrier semaphores. Data moves between devices by JAX's collectives and lax.ppermute only.
A program may use at most 128 MiB of HBM per device.

v0:
```python
import functools

import jax
import jax.numpy as jnp
from jax import lax
from jax.experimental import pallas as pl
from jax.experimental.pallas import tpu as pltpu
from jax.sharding import Mesh, PartitionSpec as P

HALO = 16
VMEM_LIMIT = 40 * 1024 * 1024


def shift(block, axis, distance):
    n = lax.axis_size(axis)
    return lax.ppermute(block, axis, [(i, (i + distance) % n) for i in range(n)])


def shift_open(block, axis, distance):
    n = lax.axis_size(axis)
    return lax.ppermute(block, axis, [(i, i + distance) for i in range(n - distance)])


def swap_cores(block):
    return lax.ppermute(block, "core", [(0, 1), (1, 0)])


def tokens_around(tokens):
    half = tokens.shape[1] // 2
    parts = [(0, 0, tokens)]
    right = left = tokens
    for step in (1, 2, 3):
        right = shift(right, "chan", 1)
        left = shift(left, "chan", -1)
        parts.append((-step, 0, right))
        parts.append((step, 0, left))
    parts.append((4, 0, shift(right[:, :half], "chan", 1)))
    parts.append((4, half, shift(left[:, half:], "chan", -1)))
    return parts


def accumulate(layout, groups, place, mine, partner, weight, sum_mine, sum_partner):
    group_rows = weight.shape[0] // groups
    for number, (offset, first) in enumerate(layout):
        depth = mine[number].shape[1]
        group = lax.rem(place[0] + offset + groups, groups)
        start = pl.multiple_of(group * group_rows + first, 128)
        rows = weight[pl.ds(start, depth), :]
        for tokens, total in ((mine[number], sum_mine), (partner[number], sum_partner)):
            product = jnp.dot(tokens[...], rows, preferred_element_type=jnp.float32)
            if number == 0:
                total[...] = product
            else:
                total[...] += product


def in_order(place, sum_mine, sum_partner, projected):
    rows = sum_mine.shape[0]
    step = rows - HALO
    mine = pl.multiple_of(place[1] * step, 16)
    partner = pl.multiple_of((1 - place[1]) * step, 16)
    projected[pl.ds(mine, rows), :] = sum_mine[...].astype(jnp.bfloat16).astype(jnp.float32)
    projected[pl.ds(partner, rows), :] = sum_partner[...].astype(jnp.bfloat16).astype(jnp.float32)


def filtered(projected, taps, group, channels, columns):
    rows = projected.shape[0] - HALO
    return sum(
        taps[group, lag : lag + 1, channels] * projected[pl.ds(HALO - lag, rows), columns]
        for lag in range(taps.shape[1])
    )


def key_value_kernel(layout, groups, place, *refs):
    n = len(layout)
    mine, partner = refs[:n], refs[n : 2 * n]
    weight, taps, rates, signal, block_ends, end_state, sum_mine, sum_partner, projected = refs[2 * n :]
    accumulate(layout, groups, place, mine, partner, weight, sum_mine, sum_partner)
    in_order(place, sum_mine, sum_partner, projected)
    modes, blocks, width = block_ends.shape
    steps = signal.shape[1] // blocks
    for part in range(width // 128):
        lanes = pl.ds(part * 128, 128)
        key = filtered(projected, taps, 1, lanes, lanes)
        value = filtered(projected, taps, 2, lanes, pl.ds(width + part * 128, 128))
        signal[part] = key * value
        decay = [
            jnp.broadcast_to(jnp.exp(-rates[m : m + 1, lanes]), (blocks, 128)) for m in range(modes)
        ]

        def step(s, states):
            u = signal[part, pl.ds(s, blocks, steps), :]
            return tuple(decay[m] * states[m] + u for m in range(modes))

        zero = jnp.zeros((blocks, 128), jnp.float32)
        states = lax.fori_loop(0, steps, step, (zero,) * modes, unroll=8)
        for m in range(modes):
            block_ends[m, :, lanes] = states[m]
    block_decay = jnp.exp(-rates[...] * float(steps))
    state = block_ends[:, 0, :]
    for b in range(1, blocks):
        state = block_decay * state + block_ends[:, b, :]
    end_state[...] = state


def query_kernel(layout, groups, place, *refs):
    n = len(layout)
    mine, partner = refs[:n], refs[n : 2 * n]
    weight, taps, query, sum_mine, sum_partner, projected = refs[2 * n :]
    accumulate(layout, groups, place, mine, partner, weight, sum_mine, sum_partner)
    in_order(place, sum_mine, sum_partner, projected)
    query[...] = filtered(projected, taps, 0, slice(None), slice(None))


def scan_kernel(signal, query, block_ends, start_state, rates, amplitude, gated, block_starts, result):
    modes, blocks, width = block_ends.shape
    steps = signal.shape[1] // blocks
    block_decay = jnp.exp(-rates[...] * float(steps))
    state = start_state[...]
    for b in range(blocks):
        block_starts[:, b, :] = state
        state = block_decay * state + block_ends[:, b, :]
    for part in range(width // 128):
        lanes = pl.ds(part * 128, 128)
        decay = [
            jnp.broadcast_to(jnp.exp(-rates[m : m + 1, lanes]), (blocks, 128)) for m in range(modes)
        ]
        scale = [jnp.broadcast_to(amplitude[m : m + 1, lanes], (blocks, 128)) for m in range(modes)]

        def step(s, states):
            u = signal[part, pl.ds(s, blocks, steps), :]
            states = tuple(decay[m] * states[m] + u for m in range(modes))
            terms = [scale[m] * states[m] for m in range(modes)]
            while len(terms) > 1:
                terms = [a + b for a, b in zip(terms[::2], terms[1::2])]
            result[part, pl.ds(s, blocks, steps), :] = terms[0]
            return states

        states = tuple(block_starts[m, :, lanes] for m in range(modes))
        lax.fori_loop(0, steps, step, states, unroll=4)
        gated[:, lanes] = (query[:, lanes] * result[part]).astype(jnp.bfloat16)


def on_device(kernel, outs, scratch, cost, *arrays):
    smem = pl.BlockSpec(memory_space=pltpu.SMEM)
    vmem = pl.BlockSpec(memory_space=pltpu.VMEM)
    return pl.pallas_call(
        kernel,
        out_shape=outs,
        in_specs=[smem if a.dtype == jnp.int32 else vmem for a in arrays],
        out_specs=jax.tree.map(lambda _: vmem, outs),
        scratch_shapes=[pltpu.VMEM(s, jnp.float32) for s in scratch],
        compiler_params=pltpu.CompilerParams(vmem_limit_bytes=VMEM_LIMIT),
        cost_estimate=pl.CostEstimate(flops=cost, bytes_accessed=cost // 400, transcendentals=0),
    )(*arrays)


def carried_in(end_state, rates, positions):
    nx, ny = lax.axis_size("x"), lax.axis_size("y")
    x, y = lax.axis_index("x"), lax.axis_index("y")
    from_x = [end_state] + [shift(end_state, "x", d) for d in range(1, nx)]
    prefix = jnp.zeros_like(end_state)
    row_total = jnp.zeros_like(end_state)
    for d, state in enumerate(from_x):
        source = (x - d) % nx
        row_total += jnp.exp(-rates * (positions * (nx - 1 - source)).astype(jnp.float32)) * state
        if d:
            weight = jnp.exp(-rates * float(positions * (d - 1)))
            prefix += jnp.where(d <= x, weight * state, 0.0)
    from_y = [shift_open(row_total, "y", d) for d in range(1, ny)]
    above = jnp.zeros_like(end_state)
    for d, state in enumerate(from_y, 1):
        above += jnp.exp(-rates * float(positions * nx * (d - 1))) * state
    return prefix + jnp.exp(-rates * (positions * x).astype(jnp.float32)) * above


def shards(tokens, input_weight, short_taps, residue, decay_rate, out_weight):
    f32, bf16 = jnp.float32, jnp.bfloat16
    rows, _ = tokens.shape
    width = input_weight.shape[2] // 2
    groups = lax.axis_size("chan")
    core = lax.axis_index("core")
    chips = lax.axis_size("x") * lax.axis_size("y")
    positions = 2 * rows
    sequence = positions * chips
    place = jnp.stack([lax.axis_index("chan"), core]).astype(jnp.int32)

    def own_columns(array, owner):
        return lax.dynamic_slice_in_dim(array, owner * width, width, axis=array.ndim - 1)

    kept = own_columns(input_weight, core)
    got = swap_cores(own_columns(input_weight, 1 - core))
    both = jnp.where(core == 0, jnp.stack([kept, got]), jnp.stack([got, kept]))
    query_part = both[:, 0].reshape(-1, width)
    key_value_part = jnp.concatenate([both[:, 1], both[:, 2]], axis=-1).reshape(-1, 2 * width)
    key_value_weight = lax.all_gather(key_value_part, ("y", "x"), axis=0, tiled=True)
    query_part, _ = lax.optimization_barrier((query_part, key_value_weight[:16, :128]))
    query_weight = lax.all_gather(query_part, ("y", "x"), axis=0, tiled=True)

    last_rows = tokens[-HALO:]
    devices = range(2 * chips)
    earlier = lax.ppermute(last_rows, ("y", "x", "core"), [(i, i + 1) for i in devices[:-1]])
    parts = tokens_around(jnp.concatenate([earlier, tokens], axis=0))
    layout = tuple((offset, first) for offset, first, _ in parts)
    mine = [block for _, _, block in parts]
    partner = [swap_cores(block) for block in mine]

    rates_all = decay_rate / float(sequence)
    rates = own_columns(rates_all, core)
    amplitude = own_columns(residue * jnp.sqrt(-jnp.expm1(-2.0 * rates_all)), core)
    taps = own_columns(short_taps, core)
    modes = rates.shape[0]
    blocks = 8

    ext = rows + HALO
    signal, block_ends, end_state = on_device(
        functools.partial(key_value_kernel, layout, groups),
        (
            jax.ShapeDtypeStruct((width // 128, positions, 128), f32),
            jax.ShapeDtypeStruct((modes, blocks, width), f32),
            jax.ShapeDtypeStruct((modes, width), f32),
        ),
        ((ext, 2 * width), (ext, 2 * width), (positions + HALO, 2 * width)),
        2 * positions * key_value_weight.size,
        place, *mine, *partner, key_value_weight, taps, rates,
    )
    start_state = carried_in(end_state, rates, positions)
    query = on_device(
        functools.partial(query_kernel, layout, groups),
        jax.ShapeDtypeStruct((positions, width), f32),
        ((ext, width), (ext, width), (positions + HALO, width)),
        2 * positions * query_weight.size,
        place, *mine, *partner, query_weight, taps,
    )
    gated = on_device(
        scan_kernel,
        jax.ShapeDtypeStruct((positions, width), bf16),
        ((modes, blocks, width), (width // 128, positions, 128)),
        4 * modes * positions * width,
        signal, query, block_ends, start_state, rates, amplitude,
    )

    own = lax.dynamic_slice_in_dim(gated, core * rows, rows, axis=0)
    other = swap_cores(lax.dynamic_slice_in_dim(gated, (1 - core) * rows, rows, axis=0))
    ordered = jnp.where(
        core == 0, jnp.concatenate([own, other], axis=1), jnp.concatenate([other, own], axis=1)
    )
    partial_sum = jnp.dot(ordered, out_weight, preferred_element_type=f32)
    return lax.psum_scatter(
        partial_sum.astype(bf16), "chan", scatter_dimension=1, tiled=True
    )


def solution(mesh):
    devices = mesh.devices.reshape(4, 4, 2, 8)
    chips = Mesh(devices, ("y", "x", "core", "chan"))
    seq = ("y", "x", "core")
    placed = (
        P(seq, "chan"),
        P(None, seq, "chan"),
        P(None, None, "chan"),
        P(None, "chan"),
        P(None, "chan"),
        P("chan", None),
    )
    return jax.shard_map(
        shards, mesh=chips, in_specs=placed, out_specs=P(seq, "chan"), check_vma=False
    )
```

profile of v0, /device:TPU:2, one launch (start us, length us, event | category | flops | bytes accessed | tf_op | source)
XLA Modules:
  0.0 183.6 jit_solution(2789524689683328252)
XLA Ops:
  6.5 1.1 dynamic-slice_bitcast_fusion
  7.7 1.4 collective-permute-done.18
  9.2 0.7 fusion.7
  9.9 0.7 pad_maximum_fusion
  10.7 0.7 all-gather.5.cloned.1.call-update
  11.4 0.7 slice.19
  12.1 2.0 %collective-permute-start = (bf16[16,512]{1,0:T(8,128)(2,1)S(1)}, bf16[16,512]{1,0:T(8,128)(2,1)S(1)}, u32[]{:S(2)}, u32[]{:S(2)}) collective-permute-start(bf16[16,512]{1,0:T(8,128)(2,1)S(1)} %slice.19), channel_id=1, source_target_pairs={{0,8},{8,16},{16,24},{24,32},{32,40},{40,48},{48,56},{56,64},{64,7... | collective-permute-start | bytes 49160 | tf_op jit(solution)/shard_map/ppermute | solution.py:202
  14.2 3.3 %collective-permute-done = bf16[16,512]{1,0:T(8,128)(2,1)S(1)} collective-permute-done((bf16[16,512]{1,0:T(8,128)(2,1)S(1)}, bf16[16,512]{1,0:T(8,128)(2,1)S(1)}, u32[]{:S(2)}, u32[]{:S(2)}) %collective-permute-start) | collective-permute-done | bytes 16416 | tf_op jit(solution)/shard_map/ppermute | solution.py:202
  17.5 1.0 constant_dynamic-update-slice_fusion.refs_0_
  18.4 1.7 collective-permute-start.1
  20.1 4.0 %collective-permute-start.2 = (bf16[272,512]{1,0:T(8,128)(2,1)S(1)}, bf16[272,512]{1,0:T(8,128)(2,1)S(1)}, u32[]{:S(2)}, u32[]{:S(2)}) collective-permute-start(bf16[272,512]{1,0:T(8,128)(2,1)S(1)} %constant_dynamic-update-slice_fusion.refs_0_), channel_id=1, source_target_pairs={{0,7},{1,0},{2,1},{3,2},{4,3},{5,4},{6,5},{7,6},{8,15},{9,8},{10,9... | collective-permute-start | bytes 835592 | tf_op jit(solution)/shard_map/ppermute | solution.py:16
  24.2 6.0 %collective-permute-done.1.refs_1_ = bf16[272,512]{1,0:T(8,128)(2,1)S(1)} collective-permute-done((bf16[272,512]{1,0:T(8,128)(2,1)S(1)}, bf16[272,512]{1,0:T(8,128)(2,1)S(1)}, u32[]{:S(2)}, u32[]{:S(2)}) %collective-permute-start.1) | collective-permute-done | bytes 278560 | tf_op jit(solution)/shard_map/ppermute | solution.py:16
  30.2 3.2 %collective-permute-start.4 = (bf16[272,512]{1,0:T(8,128)(2,1)S(1)}, bf16[272,512]{1,0:T(8,128)(2,1)S(1)}, u32[]{:S(2)}, u32[]{:S(2)}) collective-permute-start(bf16[272,512]{1,0:T(8,128)(2,1)S(1)} %collective-permute-done.2.refs_2_), channel_id=1, source_target_pairs={{0,7},{1,0},{2,1},{3,2},{4,3},{5,4},{6,5},{7,6},{8,15},{9,8},{10,9... | collective-permute-start | bytes 835592 | tf_op jit(solution)/shard_map/ppermute | solution.py:16
  33.5 5.2 %collective-permute-done.3.refs_3_ = bf16[272,512]{1,0:T(8,128)(2,1)S(1)} collective-permute-done((bf16[272,512]{1,0:T(8,128)(2,1)S(1)}, bf16[272,512]{1,0:T(8,128)(2,1)S(1)}, u32[]{:S(2)}, u32[]{:S(2)}) %collective-permute-start.3) | collective-permute-done | bytes 278560 | tf_op jit(solution)/shard_map/ppermute | solution.py:16
  38.7 3.2 %collective-permute-start.6 = (bf16[272,512]{1,0:T(8,128)(2,1)S(1)}, bf16[272,512]{1,0:T(8,128)(2,1)S(1)}, u32[]{:S(2)}, u32[]{:S(2)}) collective-permute-start(bf16[272,512]{1,0:T(8,128)(2,1)S(1)} %collective-permute-done.4.refs_4_), channel_id=1, source_target_pairs={{0,7},{1,0},{2,1},{3,2},{4,3},{5,4},{6,5},{7,6},{8,15},{9,8},{10,9... | collective-permute-start | bytes 835592 | tf_op jit(solution)/shard_map/ppermute | solution.py:16
  42.4 4.0 %collective-permute-done.5.refs_5_ = bf16[272,512]{1,0:T(8,128)(2,1)S(1)} collective-permute-done((bf16[272,512]{1,0:T(8,128)(2,1)S(1)}, bf16[272,512]{1,0:T(8,128)(2,1)S(1)}, u32[]{:S(2)}, u32[]{:S(2)}) %collective-permute-start.5) | collective-permute-done | bytes 278560 | tf_op jit(solution)/shard_map/ppermute | solution.py:16
  46.4 0.7 slice.25
  47.1 0.7 slice.26
  47.8 3.2 %collective-permute-start.8 = (bf16[272,256]{1,0:T(8,128)(2,1)}, bf16[272,256]{1,0:T(8,128)(2,1)}, u32[]{:S(2)}, u32[]{:S(2)}) collective-permute-start(bf16[272,256]{1,0:T(8,128)(2,1)} %slice.26), channel_id=1, source_target_pairs={{0,7},{1,0},{2,1},{3,2},{4,3},{5,4},{6,5},{7,6},{8,15},{9,8},{10,9... | collective-permute-start | bytes 417800 | tf_op jit(solution)/shard_map/ppermute | solution.py:16
  51.6 3.0 %collective-permute-done.7.refs_7_ = bf16[272,256]{1,0:T(8,128)(2,1)S(1)} collective-permute-done((bf16[272,256]{1,0:T(8,128)(2,1)}, bf16[272,256]{1,0:T(8,128)(2,1)S(1)}, u32[]{:S(2)}, u32[]{:S(2)}) %collective-permute-start.7) | collective-permute-done | bytes 139296 | tf_op jit(solution)/shard_map/ppermute | solution.py:16
  55.2 0.8 dynamic-slice_multiply_fusion
  56.0 0.6 copy-done.3
  56.6 0.6 copy-done.6
  57.3 13.0 %all-gather.3.cloned.1.call-done.refs_18_ = bf16[4096,512]{1,0:T(8,128)(2,1)} async-done(((bf16[256,512]{1,0:T(8,128)(2,1)}), bf16[4096,512]{1,0:T(8,128)(2,1)}) %all-gather.3.cloned.1.call-update) | async-done | bytes 4194320 | tf_op jit(solution)/shard_map/all_gather | solution.py:196
  70.3 2.2 %copy-done.1 = bf16[4096,512]{1,0:T(8,128)(2,1)S(1)} copy-done((bf16[4096,512]{1,0:T(8,128)(2,1)S(1)}, bf16[4096,512]{1,0:T(8,128)(2,1)}, u32[]{:S(2)}) %copy-start.1) | copy-done | bytes 4194328
  72.4 0.9 copy-done.4
  73.4 0.9 copy-done.7
  74.3 5.5 %shard_map.64 = (f32[2,512,128]{2,1,0:T(8,128)S(1)}, f32[16,8,256]{2,1,0:T(8,128)S(1)}, f32[16,256]{1,0:T(8,128)}) custom-call(s32[2]{0:T(128)S(1)} %pad_add_fusion.place, bf16[272,512]{1,0:T(8,128)(2,1)S(1)} %constant_dynamic-update-slice_fusion.refs_0_, bf16[272,512]{1,0:T(8,128)(2,1)S(1)} %collective-permute-done.1.refs_1_, ...), custom_call_target="tpu_custom_call" | custom-call | flops 2147483648 | bytes 5368709 | tf_op jit(solution)/shard_map/pallas_call | solution.py:147
  79.8 0.8 copy-done.9
  80.6 0.7 copy-done.11
  81.2 1.5 collective-permute-start.19
  82.7 1.2 collective-permute-start.20
  83.9 2.1 %collective-permute-start.21 = (f32[16,256]{1,0:T(8,128)}, f32[16,256]{1,0:T(8,128)}, u32[]{:S(2)}, u32[]{:S(2)}) collective-permute-start(f32[16,256]{1,0:T(8,128)} %get-tuple-element.10), channel_id=1, source_target_pairs={{0,48},{16,0},{32,16},{48,32},{1,49},{17,1},{33,17},{49,33},{2,50}... | collective-permute-start | bytes 49160 | tf_op jit(solution)/shard_map/ppermute | solution.py:16
  86.0 2.4 %collective-permute-done.20 = f32[16,256]{1,0:T(8,128)} collective-permute-done((f32[16,256]{1,0:T(8,128)}, f32[16,256]{1,0:T(8,128)}, u32[]{:S(2)}, u32[]{:S(2)}) %collective-permute-start.20) | collective-permute-done | bytes 16416 | tf_op jit(solution)/shard_map/ppermute | solution.py:16
  88.4 1.4 multiply_add_fusion.1
  89.8 3.6 %collective-permute-start.22 = (f32[16,256]{1,0:T(8,128)}, f32[16,256]{1,0:T(8,128)}, u32[]{:S(2)}, u32[]{:S(2)}) collective-permute-start(f32[16,256]{1,0:T(8,128)} %multiply_add_fusion.1), channel_id=1, source_target_pairs={{0,64},{64,128},{128,192},{1,65},{65,129},{129,193},{2,66},{66,130... | collective-permute-start | bytes 49160 | tf_op jit(solution)/shard_map/ppermute | solution.py:21
  93.4 4.6 %collective-permute-start.23 = (f32[16,256]{1,0:T(8,128)}, f32[16,256]{1,0:T(8,128)}, u32[]{:S(2)}, u32[]{:S(2)}) collective-permute-start(f32[16,256]{1,0:T(8,128)} %multiply_add_fusion.1), channel_id=1, source_target_pairs={{0,128},{64,192},{1,129},{65,193},{2,130},{66,194},{3,131},{67,195... | collective-permute-start | bytes 49160 | tf_op jit(solution)/shard_map/ppermute | solution.py:21
  98.0 1.9 %collective-permute-start.24 = (f32[16,256]{1,0:T(8,128)}, f32[16,256]{1,0:T(8,128)}, u32[]{:S(2)}, u32[]{:S(2)}) collective-permute-start(f32[16,256]{1,0:T(8,128)} %multiply_add_fusion.1), channel_id=1, source_target_pairs={{0,192},{1,193},{2,194},{3,195},{4,196},{5,197},{6,198},{7,199},{8... | collective-permute-start | bytes 49160 | tf_op jit(solution)/shard_map/ppermute | solution.py:21
  99.9 22.2 %all-gather.5.cloned.1.call-done.refs_18_ = bf16[4096,256]{1,0:T(8,128)(2,1)} async-done(((bf16[256,256]{1,0:T(8,128)(2,1)}), bf16[4096,256]{1,0:T(8,128)(2,1)}) %all-gather.5.cloned.1.call-update) | async-done | bytes 2097168 | tf_op jit(solution)/shard_map/all_gather | solution.py:198
  122.1 1.6 copy-done.2
  123.7 0.9 copy-done.5
  124.6 0.9 copy-done.8
  125.5 2.8 %shard_map.65.query = f32[512,256]{1,0:T(8,128)S(1)} custom-call(s32[2]{0:T(128)S(1)} %pad_add_fusion.place, bf16[272,512]{1,0:T(8,128)(2,1)S(1)} %constant_dynamic-update-slice_fusion.refs_0_, bf16[272,512]{1,0:T(8,128)(2,1)S(1)} %collective-permute-done.1.refs_1_, bf16[272,512]{1,0:T(8,128)(2,1)S(1)} %collective-permute-done.2.refs_2_, ...), custom_call_target="tpu_custom_call" | custom-call | flops 1073741824 | bytes 2684354 | tf_op jit(solution)/shard_map/pallas_call | solution.py:147
  128.4 0.8 multiply_add_fusion.start_state
  129.2 1.9 %shard_map.66 = bf16[512,256]{1,0:T(8,128)(2,1)S(1)} custom-call(f32[2,512,128]{2,1,0:T(8,128)S(1)} %copy-done.10, f32[512,256]{1,0:T(8,128)S(1)} %shard_map.65.query, f32[16,8,256]{2,1,0:T(8,128)S(1)} %copy-done.12, f32[16,256]{1,0:T(8,128)S(1)} %multiply_add_fusion.start_state, f32[16,256]{1,0:T(8,128)S(1)} %get-tuple-element.19.refs_20_.rates, ...), custom_call_target="tpu_custom_call" | custom-call | flops 8388608 | bytes 20971 | tf_op jit(solution)/shard_map/pallas_call | solution.py:147
  131.3 1.3 collective-permute-done.25
  132.7 2.6 %convolution_convert_fusion = bf16[256,4096]{1,0:T(8,128)(2,1)} fusion(bf16[512,4096]{1,0:T(8,128)(2,1)S(1)} %copy-done.13, bf16[256,256]{1,0:T(8,128)(2,1)S(1)} %collective-permute-done.25, bf16[256,256]{1,0:T(8,128)(2,1)S(1)} %get-tuple-element.16, pred[]{:T(512)S(6)} %eq.9), kind=kOutput, calls=%fused_computation | convolution fusion | flops 1075970048 | bytes 6553601 | tf_op jit(solution)/shard_map/dot_general | solution.py:248
  135.3 41.8 %reduce-scatter.2.cloned.1.call-done = bf16[256,512]{1,0:T(8,128)(2,1)} async-done(((bf16[256,4096]{1,0:T(8,128)(2,1)}), bf16[256,512]{1,0:T(8,128)(2,1)}) %reduce-scatter.2.cloned.1.call-update) | async-done | bytes 262160 | tf_op jit(solution)/shard_map/reduce_scatter | solution.py:249
  (60 shorter events, 2.2 us)
Async XLA Ops:
  6.5 45.1 %copy-start = (f32[3,3,512]{2,1,0:T(4,128)S(1)}, f32[3,3,512]{2,1,0:T(4,128)}, u32[]{:S(2)}) copy-start(f32[3,3,512]{2,1,0:T(4,128)} %param.8) | copy-start | bytes 55300
  6.5 63.7 %all-gather.3.cloned.1.call-start = ((), (), s32[]{:S(2)}) async-start(), calls=%async_computation.1 | async-start | bytes 4456448 | tf_op jit(solution)/shard_map/all_gather | solution.py:196
  7.6 1.5 collective-permute-start.18
  10.6 111.5 %all-gather.5.cloned.1.call-start = ((), (), s32[]{:S(2)}) async-start(), calls=%async_computation.2 | async-start | bytes 2228224 | tf_op jit(solution)/shard_map/all_gather | solution.py:198
  11.4 165.7 %reduce-scatter.2.cloned.1.call-start = ((), (), s32[]{:S(2)}) async-start(), calls=%async_computation.3 | async-start | bytes 2359296 | tf_op jit(solution)/shard_map/reduce_scatter | solution.py:249
  12.1 5.3 %collective-permute-start = (bf16[16,512]{1,0:T(8,128)(2,1)S(1)}, bf16[16,512]{1,0:T(8,128)(2,1)S(1)}, u32[]{:S(2)}, u32[]{:S(2)}) collective-permute-start(bf16[16,512]{1,0:T(8,128)(2,1)S(1)} %slice.19), channel_id=1, source_target_pairs={{0,8},{8,16},{16,24},{24,32},{32,40},{40,48},{48,56},{56,64},{64,7... | collective-permute-start | bytes 49160 | tf_op jit(solution)/shard_map/ppermute | solution.py:202
  18.4 11.8 %collective-permute-start.1 = (bf16[272,512]{1,0:T(8,128)(2,1)S(1)}, bf16[272,512]{1,0:T(8,128)(2,1)S(1)}, u32[]{:S(2)}, u32[]{:S(2)}) collective-permute-start(bf16[272,512]{1,0:T(8,128)(2,1)S(1)} %constant_dynamic-update-slice_fusion.refs_0_), channel_id=1, source_target_pairs={{0,1},{1,2},{2,3},{3,4},{4,5},{5,6},{6,7},{7,0},{8,9},{9,10},{10,1... | collective-permute-start | bytes 835592 | tf_op jit(solution)/shard_map/ppermute | solution.py:16
  20.1 10.1 %collective-permute-start.2 = (bf16[272,512]{1,0:T(8,128)(2,1)S(1)}, bf16[272,512]{1,0:T(8,128)(2,1)S(1)}, u32[]{:S(2)}, u32[]{:S(2)}) collective-permute-start(bf16[272,512]{1,0:T(8,128)(2,1)S(1)} %constant_dynamic-update-slice_fusion.refs_0_), channel_id=1, source_target_pairs={{0,7},{1,0},{2,1},{3,2},{4,3},{5,4},{6,5},{7,6},{8,15},{9,8},{10,9... | collective-permute-start | bytes 835592 | tf_op jit(solution)/shard_map/ppermute | solution.py:16
  30.2 8.5 %collective-permute-start.3 = (bf16[272,512]{1,0:T(8,128)(2,1)S(1)}, bf16[272,512]{1,0:T(8,128)(2,1)S(1)}, u32[]{:S(2)}, u32[]{:S(2)}) collective-permute-start(bf16[272,512]{1,0:T(8,128)(2,1)S(1)} %collective-permute-done.1.refs_1_), channel_id=1, source_target_pairs={{0,1},{1,2},{2,3},{3,4},{4,5},{5,6},{6,7},{7,0},{8,9},{9,10},{10,1... | collective-permute-start | bytes 835592 | tf_op jit(solution)/shard_map/ppermute | solution.py:16
  30.2 8.5 %collective-permute-start.4 = (bf16[272,512]{1,0:T(8,128)(2,1)S(1)}, bf16[272,512]{1,0:T(8,128)(2,1)S(1)}, u32[]{:S(2)}, u32[]{:S(2)}) collective-permute-start(bf16[272,512]{1,0:T(8,128)(2,1)S(1)} %collective-permute-done.2.refs_2_), channel_id=1, source_target_pairs={{0,7},{1,0},{2,1},{3,2},{4,3},{5,4},{6,5},{7,6},{8,15},{9,8},{10,9... | collective-permute-start | bytes 835592 | tf_op jit(solution)/shard_map/ppermute | solution.py:16
  38.7 7.8 %collective-permute-start.5 = (bf16[272,512]{1,0:T(8,128)(2,1)S(1)}, bf16[272,512]{1,0:T(8,128)(2,1)S(1)}, u32[]{:S(2)}, u32[]{:S(2)}) collective-permute-start(bf16[272,512]{1,0:T(8,128)(2,1)S(1)} %collective-permute-done.3.refs_3_), channel_id=1, source_target_pairs={{0,1},{1,2},{2,3},{3,4},{4,5},{5,6},{6,7},{7,0},{8,9},{9,10},{10,1... | collective-permute-start | bytes 835592 | tf_op jit(solution)/shard_map/ppermute | solution.py:16
  38.7 8.4 %collective-permute-start.6 = (bf16[272,512]{1,0:T(8,128)(2,1)S(1)}, bf16[272,512]{1,0:T(8,128)(2,1)S(1)}, u32[]{:S(2)}, u32[]{:S(2)}) collective-permute-start(bf16[272,512]{1,0:T(8,128)(2,1)S(1)} %collective-permute-done.4.refs_4_), channel_id=1, source_target_pairs={{0,7},{1,0},{2,1},{3,2},{4,3},{5,4},{6,5},{7,6},{8,15},{9,8},{10,9... | collective-permute-start | bytes 835592 | tf_op jit(solution)/shard_map/ppermute | solution.py:16
  41.9 5.8 %collective-permute-start.9 = (bf16[272,512]{1,0:T(8,128)(2,1)S(1)}, bf16[272,512]{1,0:T(8,128)(2,1)S(1)}, u32[]{:S(2)}, u32[]{:S(2)}) collective-permute-start(bf16[272,512]{1,0:T(8,128)(2,1)S(1)} %constant_dynamic-update-slice_fusion.refs_0_), channel_id=1, source_target_pairs={{0,8},{8,0},{1,9},{9,1},{2,10},{10,2},{3,11},{11,3},{4,12},{12,4},... | collective-permute-start | bytes 835592 | tf_op jit(solution)/shard_map/ppermute | solution.py:25
  41.9 9.1 %collective-permute-start.10 = (bf16[272,512]{1,0:T(8,128)(2,1)S(1)}, bf16[272,512]{1,0:T(8,128)(2,1)S(1)}, u32[]{:S(2)}, u32[]{:S(2)}) collective-permute-start(bf16[272,512]{1,0:T(8,128)(2,1)S(1)} %collective-permute-done.1.refs_1_), channel_id=1, source_target_pairs={{0,8},{8,0},{1,9},{9,1},{2,10},{10,2},{3,11},{11,3},{4,12},{12,4},... | collective-permute-start | bytes 835592 | tf_op jit(solution)/shard_map/ppermute | solution.py:25
  42.4 8.6 %collective-permute-start.11 = (bf16[272,512]{1,0:T(8,128)(2,1)S(1)}, bf16[272,512]{1,0:T(8,128)(2,1)S(1)}, u32[]{:S(2)}, u32[]{:S(2)}) collective-permute-start(bf16[272,512]{1,0:T(8,128)(2,1)S(1)} %collective-permute-done.2.refs_2_), channel_id=1, source_target_pairs={{0,8},{8,0},{1,9},{9,1},{2,10},{10,2},{3,11},{11,3},{4,12},{12,4},... | collective-permute-start | bytes 835592 | tf_op jit(solution)/shard_map/ppermute | solution.py:25
  46.4 5.1 %collective-permute-start.12 = (bf16[272,512]{1,0:T(8,128)(2,1)S(1)}, bf16[272,512]{1,0:T(8,128)(2,1)S(1)}, u32[]{:S(2)}, u32[]{:S(2)}) collective-permute-start(bf16[272,512]{1,0:T(8,128)(2,1)S(1)} %collective-permute-done.3.refs_3_), channel_id=1, source_target_pairs={{0,8},{8,0},{1,9},{9,1},{2,10},{10,2},{3,11},{11,3},{4,12},{12,4},... | collective-permute-start | bytes 835592 | tf_op jit(solution)/shard_map/ppermute | solution.py:25
  47.1 7.5 %collective-permute-start.7 = (bf16[272,256]{1,0:T(8,128)(2,1)}, bf16[272,256]{1,0:T(8,128)(2,1)S(1)}, u32[]{:S(2)}, u32[]{:S(2)}) collective-permute-start(bf16[272,256]{1,0:T(8,128)(2,1)} %slice.25), channel_id=1, source_target_pairs={{0,1},{1,2},{2,3},{3,4},{4,5},{5,6},{6,7},{7,0},{8,9},{9,10},{10,1... | collective-permute-start | bytes 417800 | tf_op jit(solution)/shard_map/ppermute | solution.py:16
  47.8 6.9 %collective-permute-start.8 = (bf16[272,256]{1,0:T(8,128)(2,1)}, bf16[272,256]{1,0:T(8,128)(2,1)}, u32[]{:S(2)}, u32[]{:S(2)}) collective-permute-start(bf16[272,256]{1,0:T(8,128)(2,1)} %slice.26), channel_id=1, source_target_pairs={{0,7},{1,0},{2,1},{3,2},{4,3},{5,4},{6,5},{7,6},{8,15},{9,8},{10,9... | collective-permute-start | bytes 417800 | tf_op jit(solution)/shard_map/ppermute | solution.py:16
  51.0 5.0 %collective-permute-start.13 = (bf16[272,512]{1,0:T(8,128)(2,1)S(1)}, bf16[272,512]{1,0:T(8,128)(2,1)S(1)}, u32[]{:S(2)}, u32[]{:S(2)}) collective-permute-start(bf16[272,512]{1,0:T(8,128)(2,1)S(1)} %collective-permute-done.4.refs_4_), channel_id=1, source_target_pairs={{0,8},{8,0},{1,9},{9,1},{2,10},{10,2},{3,11},{11,3},{4,12},{12,4},... | collective-permute-start | bytes 835592 | tf_op jit(solution)/shard_map/ppermute | solution.py:25
  51.0 6.3 %collective-permute-start.14 = (bf16[272,512]{1,0:T(8,128)(2,1)S(1)}, bf16[272,512]{1,0:T(8,128)(2,1)}, u32[]{:S(2)}, u32[]{:S(2)}) collective-permute-start(bf16[272,512]{1,0:T(8,128)(2,1)S(1)} %collective-permute-done.5.refs_5_), channel_id=1, source_target_pairs={{0,8},{8,0},{1,9},{9,1},{2,10},{10,2},{3,11},{11,3},{4,12},{12,4},... | collective-permute-start | bytes 835592 | tf_op jit(solution)/shard_map/ppermute | solution.py:25
  51.5 5.8 %collective-permute-start.15 = (bf16[272,512]{1,0:T(8,128)(2,1)S(1)}, bf16[272,512]{1,0:T(8,128)(2,1)}, u32[]{:S(2)}, u32[]{:S(2)}) collective-permute-start(bf16[272,512]{1,0:T(8,128)(2,1)S(1)} %collective-permute-done.6.refs_6_), channel_id=1, source_target_pairs={{0,8},{8,0},{1,9},{9,1},{2,10},{10,2},{3,11},{11,3},{4,12},{12,4},... | collective-permute-start | bytes 835592 | tf_op jit(solution)/shard_map/ppermute | solution.py:25
  54.6 1.4 collective-permute-start.16
  54.6 2.0 %collective-permute-start.17 = (bf16[272,256]{1,0:T(8,128)(2,1)}, bf16[272,256]{1,0:T(8,128)(2,1)S(1)}, u32[]{:S(2)}, u32[]{:S(2)}) collective-permute-start(bf16[272,256]{1,0:T(8,128)(2,1)} %collective-permute-done.8.refs_8_), channel_id=1, source_target_pairs={{0,8},{8,0},{1,9},{9,1},{2,10},{10,2},{3,11},{11,3},{4,12},{12,4},... | collective-permute-start | bytes 417800 | tf_op jit(solution)/shard_map/ppermute | solution.py:25
  56.0 0.6 copy-start.3
  56.6 0.7 copy-start.6
  70.3 2.2 %copy-start.1 = (bf16[4096,512]{1,0:T(8,128)(2,1)S(1)}, bf16[4096,512]{1,0:T(8,128)(2,1)}, u32[]{:S(2)}) copy-start(bf16[4096,512]{1,0:T(8,128)(2,1)} %all-gather.3.cloned.1.call-done.refs_18_) | copy-start | bytes 12582916
  72.4 0.9 copy-start.4
  73.4 0.9 copy-start.7
  79.8 0.8 copy-start.9
  80.6 0.7 copy-start.11
  81.2 4.7 %collective-permute-start.19 = (f32[16,256]{1,0:T(8,128)}, f32[16,256]{1,0:T(8,128)}, u32[]{:S(2)}, u32[]{:S(2)}) collective-permute-start(f32[16,256]{1,0:T(8,128)} %get-tuple-element.10), channel_id=1, source_target_pairs={{0,16},{16,32},{32,48},{48,0},{1,17},{17,33},{33,49},{49,1},{2,18}... | collective-permute-start | bytes 49160 | tf_op jit(solution)/shard_map/ppermute | solution.py:16
  82.7 5.7 %collective-permute-start.20 = (f32[16,256]{1,0:T(8,128)}, f32[16,256]{1,0:T(8,128)}, u32[]{:S(2)}, u32[]{:S(2)}) collective-permute-start(f32[16,256]{1,0:T(8,128)} %get-tuple-element.10), channel_id=1, source_target_pairs={{0,32},{16,48},{32,0},{48,16},{1,33},{17,49},{33,1},{49,17},{2,34}... | collective-permute-start | bytes 49160 | tf_op jit(solution)/shard_map/ppermute | solution.py:16
  83.9 4.5 %collective-permute-start.21 = (f32[16,256]{1,0:T(8,128)}, f32[16,256]{1,0:T(8,128)}, u32[]{:S(2)}, u32[]{:S(2)}) collective-permute-start(f32[16,256]{1,0:T(8,128)} %get-tuple-element.10), channel_id=1, source_target_pairs={{0,48},{16,0},{32,16},{48,32},{1,49},{17,1},{33,17},{49,33},{2,50}... | collective-permute-start | bytes 49160 | tf_op jit(solution)/shard_map/ppermute | solution.py:16
  89.8 38.6 %collective-permute-start.22 = (f32[16,256]{1,0:T(8,128)}, f32[16,256]{1,0:T(8,128)}, u32[]{:S(2)}, u32[]{:S(2)}) collective-permute-start(f32[16,256]{1,0:T(8,128)} %multiply_add_fusion.1), channel_id=1, source_target_pairs={{0,64},{64,128},{128,192},{1,65},{65,129},{129,193},{2,66},{66,130... | collective-permute-start | bytes 49160 | tf_op jit(solution)/shard_map/ppermute | solution.py:21
  93.4 35.0 %collective-permute-start.23 = (f32[16,256]{1,0:T(8,128)}, f32[16,256]{1,0:T(8,128)}, u32[]{:S(2)}, u32[]{:S(2)}) collective-permute-start(f32[16,256]{1,0:T(8,128)} %multiply_add_fusion.1), channel_id=1, source_target_pairs={{0,128},{64,192},{1,129},{65,193},{2,130},{66,194},{3,131},{67,195... | collective-permute-start | bytes 49160 | tf_op jit(solution)/shard_map/ppermute | solution.py:21
  98.0 30.4 %collective-permute-start.24 = (f32[16,256]{1,0:T(8,128)}, f32[16,256]{1,0:T(8,128)}, u32[]{:S(2)}, u32[]{:S(2)}) collective-permute-start(f32[16,256]{1,0:T(8,128)} %multiply_add_fusion.1), channel_id=1, source_target_pairs={{0,192},{1,193},{2,194},{3,195},{4,196},{5,197},{6,198},{7,199},{8... | collective-permute-start | bytes 49160 | tf_op jit(solution)/shard_map/ppermute | solution.py:21
  122.1 1.6 copy-start.2
  123.7 0.9 copy-start.5
  124.6 0.9 copy-start.8
  125.5 3.7 %copy-start.10 = (f32[2,512,128]{2,1,0:T(8,128)S(1)}, f32[2,512,128]{2,1,0:T(8,128)}, u32[]{:S(2)}) copy-start(f32[2,512,128]{2,1,0:T(8,128)} %copy-done.9) | copy-start | bytes 1572868
  125.5 3.7 %copy-start.12 = (f32[16,8,256]{2,1,0:T(8,128)S(1)}, f32[16,8,256]{2,1,0:T(8,128)}, u32[]{:S(2)}) copy-start(f32[16,8,256]{2,1,0:T(8,128)} %copy-done.11) | copy-start | bytes 393220
  125.5 7.2 %copy-start.13 = (bf16[512,4096]{1,0:T(8,128)(2,1)S(1)}, bf16[512,4096]{1,0:T(8,128)(2,1)}, u32[]{:S(2)}) copy-start(bf16[512,4096]{1,0:T(8,128)(2,1)} %param.11) | copy-start | bytes 12582916
  131.2 1.4 collective-permute-start.25
Sparse Core Ops, SparseCore 0:
  10.7 59.4 all-gather.2
  72.7 49.3 all-gather.4
  135.4 41.6 reduce-scatter.1
where the time goes:
time: 184 us
  waiting for transfers between devices  104 us (57%)
  starting transfers between devices  34.2 us (19%)
  local copies, waits for them, and re-layouts  14.9 us (8%)
  between operations  13.3 us (7%)
  Pallas kernels  10.3 us (6%)
  other arithmetic  3.83 us (2%)
  matrix products  2.63 us (1%)
    reduce_scatter x1, waiting for transfers between devices, shards(): lax.psum_scatter(partial_sum.astype(bf16), 'chan', scatter_dimension=1, t...  41.8 us
    all_gather x1, waiting for transfers between devices, shards(): query_weight = lax.all_gather(query_part, ('y', 'x'), axis=0, tiled=True)  22.2 us
    ppermute x11, waiting for transfers between devices, shift(): lax.ppermute(block, axis, [(i, (i + distance) % n) for i in range(n)])  20.7 us
    ppermute x11, starting transfers between devices, shift(): lax.ppermute(block, axis, [(i, (i + distance) % n) for i in range(n)])  20.2 us
    all_gather x1, waiting for transfers between devices, shards(): lax.all_gather(key_value_part, ('y', 'x'), axis=0, tiled=True)  13 us
    pallas_call x3, Pallas kernels, on_device(): pl.pallas_call(kernel, out_shape=outs, in_specs=[smem if a.dtype == jnp.i...  10.3 us
    unnamed x29, local copies, waits for them, and re-layouts  10.2 us
    ppermute x3, starting transfers between devices, shift_open(): lax.ppermute(block, axis, [(i, i + distance) for i in range(n - distance)])  10.1 us
  transfers between devices with their start and end apart: 29, of which 11 were waited for; matrix products, arithmetic and copies ran while one was open for 3% of the time, Pallas kernels for 5%

commit v1 on v0

v1 whole, which is shorter than its diff:
```python
import functools

import jax
import jax.numpy as jnp
from jax import lax
from jax.experimental import pallas as pl
from jax.experimental.pallas import tpu as pltpu
from jax.sharding import Mesh, PartitionSpec as P

HALO = 16
VMEM_LIMIT = 40 * 1024 * 1024


def shift(block, axis, distance):
    n = lax.axis_size(axis)
    return lax.ppermute(block, axis, [(i, (i + distance) % n) for i in range(n)])


def shift_open(block, axis, distance):
    n = lax.axis_size(axis)
    return lax.ppermute(block, axis, [(i, i + distance) for i in range(n - distance)])


def swap_cores(block):
    return lax.ppermute(block, "core", [(0, 1), (1, 0)])


def chip_ring(block, sides, stage, sign):
    ny, nx = sides
    pairs = []
    for y in range(ny):
        for x in range(nx):
            for c in range(2):
                to = (y, (x + sign) % nx) if c == stage else ((y + sign) % ny, x)
                pairs.append(((y * nx + x) * 2 + c, (to[0] * nx + to[1]) * 2 + c))
    return lax.ppermute(block, ("y", "x", "core"), pairs)


def group_ring(block):
    n = lax.axis_size("chan")
    pairs = []
    for c in range(2):
        for z in range(n):
            pairs.append((c * n + z, c * n + (z + 1 - 2 * c) % n))
    return lax.ppermute(block, ("core", "chan"), pairs)


def weights_around(block, sides):
    def ring(own, stage):
        half = own.shape[0] // 2
        before = chip_ring(own, sides, stage, 1)
        behind = chip_ring(own, sides, stage, -1)
        far = chip_ring(before[:half], sides, stage, 1), chip_ring(behind[half:], sides, stage, -1)
        return before, behind, far

    before, behind, far = ring(block, 0)
    near = jnp.concatenate([block, before, *far, behind], axis=0)
    before, behind, far = ring(near, 1)
    return near, before, behind, *far


def tokens_around(block, core):
    blocks = [block]
    for _ in range(3):
        blocks.append(group_ring(blocks[-1]))
    half = block.shape[1] // 2
    blocks.append(group_ring(lax.dynamic_slice_in_dim(blocks[-1], core * half, half, axis=1)))
    return blocks[1:]


def tokens_in_order(place, groups, streams, gathered, semaphores):
    copies = []
    core = place[1]
    ahead = 1 - 2 * core
    row = 0
    for own, mine, partner in streams:
        rows, depth = own.shape
        half = depth // 2
        for distance in range(5):
            for side, blocks in ((-1, mine), (1, partner)):
                if distance == 0 and side == 1:
                    continue
                block = own if distance == 0 else blocks[distance - 1]
                group = lax.rem(place[0] + side * ahead * distance + groups, groups)
                column = group * depth
                if distance == 4:
                    column = column + (core if side == -1 else 1 - core) * half
                column = pl.multiple_of(column, 128)
                copies.append(
                    pltpu.make_async_copy(
                        block,
                        gathered.at[pl.ds(row, rows), pl.ds(column, block.shape[1])],
                        semaphores.at[len(copies)],
                    )
                )
        row += rows
    for copy in copies:
        copy.start()
    return copies


def weights_in_order(place, sides, blocks, gathered, semaphores):
    ny, nx = sides
    core, y, x = place[1], place[2], place[3]
    near, before, behind, far_top, far_bottom = blocks
    rows = near.shape[0] // 4
    order = (0, -1, -2, 1)
    pieces = [(near, i, first, 0) for i, first in enumerate(order)]
    pieces += [(before, i, first, -1) for i, first in enumerate(order)]
    pieces += [(behind, i, first, 1) for i, first in enumerate(order)]
    pieces += [(far_top, i, order[i], -2) for i in range(2)]
    pieces += [(far_bottom, i, order[i + 2], -2) for i in range(2)]
    copies = []
    for block, i, first, second in pieces:
        dx = jnp.where(core == 0, first, second)
        dy = jnp.where(core == 0, second, first)
        chip = lax.rem(y + dy + ny, ny) * nx + lax.rem(x + dx + nx, nx)
        to = pl.multiple_of(chip * rows, 128)
        copies.append(
            pltpu.make_async_copy(
                block.at[pl.ds(i * rows, rows)],
                gathered.at[pl.ds(to, rows)],
                semaphores.at[len(copies)],
            )
        )
    for copy in copies:
        copy.start()
    return copies


def take_tokens(refs):
    return [(refs[i], refs[i + 1 : i + 5], refs[i + 5 : i + 9]) for i in (0, 9)]


def project(tokens, weight, depth, projected):
    total = None
    rows = tokens.shape[0] - HALO
    for first in range(0, tokens.shape[1], depth):
        part = pl.ds(first, depth)
        product = jnp.dot(tokens[:, part], weight[part, :], preferred_element_type=jnp.float32)
        total = product if total is None else total + product
    total = total.astype(jnp.bfloat16).astype(jnp.float32)
    projected[pl.ds(0, HALO), :] = total[rows:]
    projected[pl.ds(HALO, rows), :] = total[:rows]


def filtered(projected, taps, group, channels, columns):
    rows = projected.shape[0] - HALO
    return sum(
        taps[group, lag : lag + 1, channels] * projected[pl.ds(HALO - lag, rows), columns]
        for lag in range(taps.shape[1])
    )


def key_value_kernel(groups, sides, place, *refs):
    streams, weights = take_tokens(refs[:18]), refs[18:23]
    taps, rates, signal, block_ends, end_state, tokens, weight, projected, *semaphores = refs[23:]
    copies = weights_in_order(place, sides, weights, weight, semaphores[0])
    copies += tokens_in_order(place, groups, streams, tokens, semaphores[1])
    for copy in copies:
        copy.wait()
    project(tokens, weight, tokens.shape[1], projected)
    modes, blocks, width = block_ends.shape
    steps = signal.shape[1] // blocks
    for part in range(width // 128):
        lanes = pl.ds(part * 128, 128)
        key = filtered(projected, taps, 1, lanes, lanes)
        value = filtered(projected, taps, 2, lanes, pl.ds(width + part * 128, 128))
        signal[part] = key * value
        decay = [
            jnp.broadcast_to(jnp.exp(-rates[m : m + 1, lanes]), (blocks, 128)) for m in range(modes)
        ]

        def step(s, states):
            u = signal[part, pl.ds(s, blocks, steps), :]
            return tuple(decay[m] * states[m] + u for m in range(modes))

        zero = jnp.zeros((blocks, 128), jnp.float32)
        states = lax.fori_loop(0, steps, step, (zero,) * modes, unroll=8)
        for m in range(modes):
            block_ends[m, :, lanes] = states[m]
    block_decay = jnp.exp(-rates[...] * float(steps))
    state = block_ends[:, 0, :]
    for b in range(1, blocks):
        state = block_decay * state + block_ends[:, b, :]
    end_state[...] = state


def query_kernel(groups, place, *refs):
    streams = take_tokens(refs[:18])
    weight, taps, query, tokens, projected, semaphores = refs[18:]
    for copy in tokens_in_order(place, groups, streams, tokens, semaphores):
        copy.wait()
    project(tokens, weight, tokens.shape[1], projected)
    query[...] = filtered(projected, taps, 0, slice(None), slice(None))


def scan_kernel(signal, query, block_ends, start_state, rates, amplitude, gated, block_starts, result):
    modes, blocks, width = block_ends.shape
    steps = signal.shape[1] // blocks
    block_decay = jnp.exp(-rates[...] * float(steps))
    state = start_state[...]
    for b in range(blocks):
        block_starts[:, b, :] = state
        state = block_decay * state + block_ends[:, b, :]
    for part in range(width // 128):
        lanes = pl.ds(part * 128, 128)
        decay = [
            jnp.broadcast_to(jnp.exp(-rates[m : m + 1, lanes]), (blocks, 128)) for m in range(modes)
        ]
        scale = [jnp.broadcast_to(amplitude[m : m + 1, lanes], (blocks, 128)) for m in range(modes)]

        def step(s, states):
            u = signal[part, pl.ds(s, blocks, steps), :]
            states = tuple(decay[m] * states[m] + u for m in range(modes))
            terms = [scale[m] * states[m] for m in range(modes)]
            while len(terms) > 1:
                terms = [a + b for a, b in zip(terms[::2], terms[1::2])]
            result[part, pl.ds(s, blocks, steps), :] = terms[0]
            return states

        states = tuple(block_starts[m, :, lanes] for m in range(modes))
        lax.fori_loop(0, steps, step, states, unroll=4)
        gated[:, lanes] = (query[:, lanes] * result[part]).astype(jnp.bfloat16)


def on_device(kernel, outs, scratch, cost, places, *arrays):
    smem = pl.BlockSpec(memory_space=pltpu.SMEM)
    vmem = pl.BlockSpec(memory_space=pltpu.VMEM)
    anywhere = pl.BlockSpec(memory_space=pl.ANY)
    specs = [vmem] * len(arrays)
    if places:
        specs[: places + 1] = [smem] + [anywhere] * places
    return pl.pallas_call(
        kernel,
        out_shape=outs,
        in_specs=specs,
        out_specs=jax.tree.map(lambda _: vmem, outs),
        scratch_shapes=scratch,
        compiler_params=pltpu.CompilerParams(vmem_limit_bytes=VMEM_LIMIT),
        cost_estimate=pl.CostEstimate(flops=cost, bytes_accessed=cost // 400, transcendentals=0),
    )(*arrays)


def carried_in(end_state, rates, positions):
    nx, ny = lax.axis_size("x"), lax.axis_size("y")
    x, y = lax.axis_index("x"), lax.axis_index("y")
    from_x = [end_state] + [shift(end_state, "x", d) for d in range(1, nx)]
    prefix = jnp.zeros_like(end_state)
    row_total = jnp.zeros_like(end_state)
    for d, state in enumerate(from_x):
        source = (x - d) % nx
        row_total += jnp.exp(-rates * (positions * (nx - 1 - source)).astype(jnp.float32)) * state
        if d:
            weight = jnp.exp(-rates * float(positions * (d - 1)))
            prefix += jnp.where(d <= x, weight * state, 0.0)
    from_y = [shift_open(row_total, "y", d) for d in range(1, ny)]
    above = jnp.zeros_like(end_state)
    for d, state in enumerate(from_y, 1):
        above += jnp.exp(-rates * float(positions * nx * (d - 1))) * state
    return prefix + jnp.exp(-rates * (positions * x).astype(jnp.float32)) * above


def shards(tokens, input_weight, short_taps, residue, decay_rate, out_weight):
    f32, bf16 = jnp.float32, jnp.bfloat16
    rows, depth = tokens.shape
    width = input_weight.shape[2] // 2
    groups = lax.axis_size("chan")
    sides = lax.axis_size("y"), lax.axis_size("x")
    chips = sides[0] * sides[1]
    core, z = lax.axis_index("core"), lax.axis_index("chan")
    positions = 2 * rows
    sequence = positions * chips
    place = jnp.stack([z, core, lax.axis_index("y"), lax.axis_index("x")]).astype(jnp.int32)

    def own_columns(array, owner):
        return lax.dynamic_slice_in_dim(array, owner * width, width, axis=array.ndim - 1)

    def by_core(own, other, axis):
        return jnp.where(
            core == 0,
            jnp.concatenate([own, other], axis=axis),
            jnp.concatenate([other, own], axis=axis),
        )

    kept = own_columns(input_weight, core)
    got = swap_cores(own_columns(input_weight, 1 - core))
    both = by_core(kept, got, 1)
    query_weight = lax.all_gather(both[0], ("y", "x"), axis=0, tiled=True)
    weights = weights_around(jnp.concatenate([both[1], both[2]], axis=1), sides)

    other = swap_cores(tokens)
    low = jnp.where(core == 0, tokens, other)
    high = jnp.where(core == 0, other, tokens)
    earlier = lax.ppermute(
        high[-HALO:], ("y", "x", "core"), [(i, i + 2) for i in range(2 * chips - 2)]
    )
    gathered = []
    for stream in (low, jnp.concatenate([high, earlier], axis=0)):
        mine = tokens_around(stream, core)
        gathered += [stream, *mine, *[swap_cores(block) for block in mine]]

    rates_all = decay_rate / float(sequence)
    rates = own_columns(rates_all, core)
    amplitude = own_columns(residue * jnp.sqrt(-jnp.expm1(-2.0 * rates_all)), core)
    taps = own_columns(short_taps, core)
    modes = rates.shape[0]
    blocks = 8
    lanes = (width // 128, positions, 128)
    features = depth * groups
    dma = pltpu.SemaphoreType.DMA

    signal, block_ends, end_state = on_device(
        functools.partial(key_value_kernel, groups, sides),
        (
            jax.ShapeDtypeStruct(lanes, f32),
            jax.ShapeDtypeStruct((modes, blocks, width), f32),
            jax.ShapeDtypeStruct((modes, width), f32),
        ),
        [
            pltpu.VMEM((positions + HALO, features), bf16),
            pltpu.VMEM((features, 2 * width), bf16),
            pltpu.VMEM((positions + HALO, 2 * width), f32),
            dma((16,)),
            dma((18,)),
        ],
        4 * positions * features * width,
        23,
        place, *gathered, *weights, taps, rates,
    )
    start_state = carried_in(end_state, rates, positions)
    query = on_device(
        functools.partial(query_kernel, groups),
        jax.ShapeDtypeStruct((positions, width), f32),
        [
            pltpu.VMEM((positions + HALO, features), bf16),
            pltpu.VMEM((positions + HALO, width), f32),
            dma((18,)),
        ],
        2 * positions * features * width,
        18,
        place, *gathered, query_weight, taps,
    )
    gated = on_device(
        scan_kernel,
        jax.ShapeDtypeStruct((positions, width), bf16),
        [pltpu.VMEM((modes, blocks, width), f32), pltpu.VMEM(lanes, f32)],
        4 * modes * positions * width,
        0,
        signal, query, block_ends, start_state, rates, amplitude,
    )
    gated = by_core(gated, swap_cores(gated), 1)
    return reduced(gated, out_weight, core, z, groups)


def reduced(gated, out_weight, core, z, groups):
    rows = gated.shape[0] // 2
    width = out_weight.shape[1] // groups
    ahead = 1 - 2 * core

    def product(values, distance, first=0, columns=width):
        start = (z + ahead * distance) % groups * width + first
        weight = lax.dynamic_slice_in_dim(out_weight, start, columns, axis=1)
        return jnp.dot(values, weight, preferred_element_type=jnp.float32).astype(jnp.bfloat16)

    half = width // 2
    part = product(gated, 4, core * half, half)
    streams = [part[:rows], part[rows:]]
    for distance in (3, 2, 1):
        part = product(gated, distance)
        for number in range(2):
            arrived = group_ring(streams[number])
            if distance == 3:
                nothing = jnp.zeros_like(arrived)
                arrived = jnp.where(
                    core == 0,
                    jnp.concatenate([arrived, nothing], axis=1),
                    jnp.concatenate([nothing, arrived], axis=1),
                )
            streams[number] = part[number * rows : (number + 1) * rows] + arrived
    low, high = [group_ring(stream) for stream in streams]
    kept = jnp.where(core == 0, low, high)
    got = swap_cores(jnp.where(core == 0, high, low))
    own = product(lax.dynamic_slice_in_dim(gated, core * rows, rows, axis=0), 0)
    total = own.astype(jnp.float32) + kept.astype(jnp.float32) + got.astype(jnp.float32)
    return total.astype(jnp.bfloat16)


def solution(mesh):
    devices = mesh.devices.reshape(4, 4, 2, 8)
    chips = Mesh(devices, ("y", "x", "core", "chan"))
    seq = ("y", "x", "core")
    placed = (
        P(seq, "chan"),
        P(None, seq, "chan"),
        P(None, None, "chan"),
        P(None, "chan"),
        P(None, "chan"),
        P("chan", None),
    )
    return jax.shard_map(
        shards, mesh=chips, in_specs=placed, out_specs=P(seq, "chan"), check_vma=False
    )
```

time: 184 us -> 181 us (0.984); the launches traced: 184 us -> 178 us
  waiting for transfers between devices: 104 us -> 63.8 us
  starting transfers between devices: 34.2 us -> 52.8 us
  local copies, waits for them, and re-layouts: 14.9 us -> 26.8 us
  matrix products: 2.63 us -> 7.75 us
  other arithmetic: 3.83 us -> 1.56 us
    ppermute x1 -> x25, waiting for transfers between devices: 3.28 us -> 55.6 us  [the longest x16 45.7 us: group_ring(): return lax.ppermute(block, ('core', 'chan'), pairs)]
    reduce_scatter x1 -> x0, waiting for transfers between devices: 41.8 us -> none  [shards(): lax.psum_scatter(partial_sum.astype(bf16), 'chan', scatter_dimension=1, t...]
    all_gather x2 -> x1, waiting for transfers between devices: 35.2 us -> 0.02 us  [shards(): query_weight = lax.all_gather(both[0], ('y', 'x'), axis=0, tiled=True)]
    ppermute x1 -> x25, starting transfers between devices: 2.03 us -> 24.2 us  [the longest x8 13.9 us: chip_ring(): return lax.ppermute(block, ('y', 'x', 'core'), pairs)]
    ppermute x11 -> x3, waiting for transfers between devices: 20.7 us -> 2.12 us  [shift(): lax.ppermute(block, axis, [(i, (i + distance) % n) for i in range(n)])]
    ppermute x11 -> x3, starting transfers between devices: 20.2 us -> 5.16 us  [shift(): lax.ppermute(block, axis, [(i, (i + distance) % n) for i in range(n)])]
    unnamed x29 -> x73, local copies, waits for them, and re-layouts: 10.2 us -> 23.2 us
    ppermute x11 -> x12, starting transfers between devices: 1.78 us -> 14.2 us  [swap_cores(): return lax.ppermute(block, 'core', [(0, 1), (1, 0)])]
  transfers between devices with their start and end apart: 29 -> 44, of which waited for: 11 -> 24; matrix products, arithmetic and copies ran while one was open for 3% -> 4% of each run, Pallas kernels for 5% -> 3%
where the time goes in v1:
time: 181 us; the launch traced here: 178 us
  waiting for transfers between devices  63.8 us (35%)
  starting transfers between devices  52.8 us (29%)
  local copies, waits for them, and re-layouts  26.8 us (15%)
  between operations  14 us (8%)
  Pallas kernels  11.6 us (6%)
  matrix products  7.75 us (4%)
    ppermute x16, waiting for transfers between devices, group_ring(): return lax.ppermute(block, ('core', 'chan'), pairs)  45.7 us
    unnamed x73, local copies, waits for them, and re-layouts  23.2 us
    ppermute x12, starting transfers between devices, swap_cores(): return lax.ppermute(block, 'core', [(0, 1), (1, 0)])  14.2 us
    ppermute x8, starting transfers between devices, chip_ring(): return lax.ppermute(block, ('y', 'x', 'core'), pairs)  13.9 us
    pallas_call x3, Pallas kernels, on_device(): pl.pallas_call(kernel, out_shape=outs, in_specs=specs, out_specs=jax.tree...  11.6 us
    ppermute x3, starting transfers between devices, shift_open(): lax.ppermute(block, axis, [(i, i + distance) for i in range(n - distance)])  9.12 us
    dot_general x5, matrix products, product(): jnp.dot(values, weight, preferred_element_type=jnp.float32)  7.75 us
    ppermute x16, starting transfers between devices, group_ring(): return lax.ppermute(block, ('core', 'chan'), pairs)  7.23 us
  transfers between devices with their start and end apart: 44, of which 24 were waited for; matrix products, arithmetic and copies ran while one was open for 4% of the time, Pallas kernels for 3%

profile of v1, /device:TPU:2, one launch (start us, length us, event | category | flops | bytes accessed | tf_op | source)
XLA Modules:
  0.0 178.2 jit_solution(5582122665927388945)
XLA Ops:
  7.7 1.4 collective-permute-done.18
  10.1 1.6 collective-permute-start.19
  12.5 4.3 %collective-permute-done.19 = bf16[256,512]{1,0:T(8,128)(2,1)S(1)} collective-permute-done((bf16[256,512]{1,0:T(8,128)(2,1)S(1)}, bf16[256,512]{1,0:T(8,128)(2,1)S(1)}, u32[]{:S(2)}, u32[]{:S(2)}) %collective-permute-start.19) | collective-permute-done | bytes 262176 | tf_op jit(solution)/shard_map/ppermute | solution.py:36
  16.8 1.3 collective-permute-start.20
  18.1 2.2 %collective-permute-start.22 = (bf16[128,512]{1,0:T(8,128)(2,1)S(1)}, bf16[128,512]{1,0:T(8,128)(2,1)S(1)}, u32[]{:S(2)}, u32[]{:S(2)}) collective-permute-start(bf16[128,512]{1,0:T(8,128)(2,1)S(1)} %slice.68), channel_id=1, source_target_pairs={{0,48},{8,200},{16,0},{24,216},{32,16},{40,232},{48,32},{56,248},{... | collective-permute-start | bytes 393224 | tf_op jit(solution)/shard_map/ppermute | solution.py:36
  20.3 2.7 %collective-permute-done.20 = bf16[128,512]{1,0:T(8,128)(2,1)S(1)} collective-permute-done((bf16[128,512]{1,0:T(8,128)(2,1)S(1)}, bf16[128,512]{1,0:T(8,128)(2,1)S(1)}, u32[]{:S(2)}, u32[]{:S(2)}) %collective-permute-start.20) | collective-permute-done | bytes 131104 | tf_op jit(solution)/shard_map/ppermute | solution.py:36
  23.2 1.7 collective-permute-start.23
  24.9 1.7 collective-permute-start.24
  26.6 2.0 %collective-permute-start.1 = (bf16[256,512]{1,0:T(8,128)(2,1)S(1)}, bf16[256,512]{1,0:T(8,128)(2,1)S(1)}, u32[]{:S(2)}, u32[]{:S(2)}) collective-permute-start(bf16[256,512]{1,0:T(8,128)(2,1)S(1)} %get-tuple-element.18.refs_0_), channel_id=1, source_target_pairs={{0,1},{1,2},{2,3},{3,4},{4,5},{5,6},{6,7},{7,0},{8,15},{9,8},{10,9... | collective-permute-start | bytes 786440 | tf_op jit(solution)/shard_map/ppermute | solution.py:45
  28.6 3.1 %collective-permute-start.9 = (bf16[16,512]{1,0:T(8,128)(2,1)S(1)}, bf16[16,512]{1,0:T(8,128)(2,1)S(1)}, u32[]{:S(2)}, u32[]{:S(2)}) collective-permute-start(bf16[16,512]{1,0:T(8,128)(2,1)S(1)} %slice.64), channel_id=1, source_target_pairs={{0,16},{8,24},{16,32},{24,40},{32,48},{40,56},{48,64},{56,72},{64,... | collective-permute-start | bytes 49160 | tf_op jit(solution)/shard_map/ppermute | solution.py:295
  31.7 2.8 %collective-permute-done.9 = bf16[16,512]{1,0:T(8,128)(2,1)S(1)} collective-permute-done((bf16[16,512]{1,0:T(8,128)(2,1)S(1)}, bf16[16,512]{1,0:T(8,128)(2,1)S(1)}, u32[]{:S(2)}, u32[]{:S(2)}) %collective-permute-start.9) | collective-permute-done | bytes 16416 | tf_op jit(solution)/shard_map/ppermute | solution.py:295
  34.5 2.0 %collective-permute-start.10 = (bf16[272,512]{1,0:T(8,128)(2,1)S(1)}, bf16[272,512]{1,0:T(8,128)(2,1)S(1)}, u32[]{:S(2)}, u32[]{:S(2)}) collective-permute-start(bf16[272,512]{1,0:T(8,128)(2,1)S(1)} %pad_maximum_fusion.refs_9_), channel_id=1, source_target_pairs={{0,1},{1,2},{2,3},{3,4},{4,5},{5,6},{6,7},{7,0},{8,15},{9,8},{10,9... | collective-permute-start | bytes 835592 | tf_op jit(solution)/shard_map/ppermute | solution.py:45
  36.9 1.5 collective-permute-start.2
  38.4 4.7 %collective-permute-done.10.refs_10_ = bf16[272,512]{1,0:T(8,128)(2,1)S(1)} collective-permute-done((bf16[272,512]{1,0:T(8,128)(2,1)S(1)}, bf16[272,512]{1,0:T(8,128)(2,1)S(1)}, u32[]{:S(2)}, u32[]{:S(2)}) %collective-permute-start.10) | collective-permute-done | bytes 278560 | tf_op jit(solution)/shard_map/ppermute | solution.py:45
  43.0 2.8 %collective-permute-done.2.refs_2_ = bf16[256,512]{1,0:T(8,128)(2,1)S(1)} collective-permute-done((bf16[256,512]{1,0:T(8,128)(2,1)S(1)}, bf16[256,512]{1,0:T(8,128)(2,1)S(1)}, u32[]{:S(2)}, u32[]{:S(2)}) %collective-permute-start.2) | collective-permute-done | bytes 262176 | tf_op jit(solution)/shard_map/ppermute | solution.py:45
  45.9 8.5 %collective-permute-start.14 = (bf16[272,512]{1,0:T(8,128)(2,1)S(1)}, bf16[272,512]{1,0:T(8,128)(2,1)S(1)}, u32[]{:S(2)}, u32[]{:S(2)}) collective-permute-start(bf16[272,512]{1,0:T(8,128)(2,1)S(1)} %collective-permute-done.10.refs_10_), channel_id=1, source_target_pairs={{0,8},{8,0},{1,9},{9,1},{2,10},{10,2},{3,11},{11,3},{4,12},{12,4},... | collective-permute-start | bytes 835592 | tf_op jit(solution)/shard_map/ppermute | solution.py:25
  54.3 3.9 %collective-permute-start.5 = (bf16[256,512]{1,0:T(8,128)(2,1)S(1)}, bf16[256,512]{1,0:T(8,128)(2,1)S(1)}, u32[]{:S(2)}, u32[]{:S(2)}) collective-permute-start(bf16[256,512]{1,0:T(8,128)(2,1)S(1)} %collective-permute-done.1.refs_1_), channel_id=1, source_target_pairs={{0,8},{8,0},{1,9},{9,1},{2,10},{10,2},{3,11},{11,3},{4,12},{12,4},... | collective-permute-start | bytes 786440 | tf_op jit(solution)/shard_map/ppermute | solution.py:25
  62.2 3.7 %collective-permute-start.26 = (bf16[512,512]{1,0:T(8,128)(2,1)}, bf16[512,512]{1,0:T(8,128)(2,1)}, u32[]{:S(2)}, u32[]{:S(2)}) collective-permute-start(bf16[512,512]{1,0:T(8,128)(2,1)} %slice.70), channel_id=1, source_target_pairs={{0,192},{8,56},{16,208},{24,8},{32,224},{40,24},{48,240},{56,40},{... | collective-permute-start | bytes 1572872 | tf_op jit(solution)/shard_map/ppermute | solution.py:36
  68.8 4.0 %collective-permute-done.13.refs_13_ = bf16[272,256]{1,0:T(8,128)(2,1)S(1)} collective-permute-done((bf16[272,256]{1,0:T(8,128)(2,1)S(1)}, bf16[272,256]{1,0:T(8,128)(2,1)S(1)}, u32[]{:S(2)}, u32[]{:S(2)}) %collective-permute-start.13) | collective-permute-done | bytes 139296 | tf_op jit(solution)/shard_map/ppermute | solution.py:45
  75.5 1.3 copy-done.3
  84.4 6.2 %shard_map.64 = (f32[2,512,128]{2,1,0:T(8,128)S(1)}, f32[16,8,256]{2,1,0:T(8,128)S(1)}, f32[16,256]{1,0:T(8,128)S(1)}) custom-call(s32[4]{0:T(128)S(1)} %pad_add_fusion.place, bf16[256,512]{1,0:T(8,128)(2,1)S(1)} %get-tuple-element.18.refs_0_, bf16[256,512]{1,0:T(8,128)(2,1)S(1)} %copy-done.14, bf16[256,512]{1,0:T(8,128)(2,1)S(1)} %copy-done.17, ...), custom_call_target="tpu_custom_call" | custom-call | flops 2147483648 | bytes 5368709 | tf_op jit(solution)/shard_map/pallas_call | solution.py:234
  92.1 1.2 collective-permute-start.27
  93.3 2.3 %collective-permute-start.28 = (f32[16,256]{1,0:T(8,128)S(1)}, f32[16,256]{1,0:T(8,128)S(1)}, u32[]{:S(2)}, u32[]{:S(2)}) collective-permute-start(f32[16,256]{1,0:T(8,128)S(1)} %get-tuple-element.10), channel_id=1, source_target_pairs={{0,32},{16,48},{32,0},{48,16},{1,33},{17,49},{33,1},{49,17},{2,34}... | collective-permute-start | bytes 49160 | tf_op jit(solution)/shard_map/ppermute | solution.py:16
  95.6 1.6 collective-permute-start.29
  97.2 1.3 collective-permute-done.28
  99.4 2.6 %collective-permute-start.30 = (f32[16,256]{1,0:T(8,128)S(1)}, f32[16,256]{1,0:T(8,128)S(1)}, u32[]{:S(2)}, u32[]{:S(2)}) collective-permute-start(f32[16,256]{1,0:T(8,128)S(1)} %multiply_add_fusion.1), channel_id=1, source_target_pairs={{0,64},{64,128},{128,192},{1,65},{65,129},{129,193},{2,66},{66,130... | collective-permute-start | bytes 49160 | tf_op jit(solution)/shard_map/ppermute | solution.py:21
  102.0 5.0 %collective-permute-start.31 = (f32[16,256]{1,0:T(8,128)S(1)}, f32[16,256]{1,0:T(8,128)S(1)}, u32[]{:S(2)}, u32[]{:S(2)}) collective-permute-start(f32[16,256]{1,0:T(8,128)S(1)} %multiply_add_fusion.1), channel_id=1, source_target_pairs={{0,128},{64,192},{1,129},{65,193},{2,130},{66,194},{3,131},{67,195... | collective-permute-start | bytes 49160 | tf_op jit(solution)/shard_map/ppermute | solution.py:21
  107.0 1.5 collective-permute-start.32
  108.6 1.2 collective-permute-done.32
  109.8 1.6 copy-done.1
  119.9 3.5 %shard_map.65.query = f32[512,256]{1,0:T(8,128)S(1)} custom-call(s32[4]{0:T(128)S(1)} %pad_add_fusion.place, bf16[256,512]{1,0:T(8,128)(2,1)S(1)} %get-tuple-element.18.refs_0_, bf16[256,512]{1,0:T(8,128)(2,1)S(1)} %copy-done.15, bf16[256,512]{1,0:T(8,128)(2,1)S(1)} %copy-done.18, bf16[256,512]{1,0:T(8,128)(2,1)S(1)} %collective-permute-done.3.refs_3_, ...), custom_call_target="tpu_custom_call" | custom-call | flops 1073741824 | bytes 2684354 | tf_op jit(solution)/shard_map/pallas_call | solution.py:234
  123.4 1.9 %shard_map.66 = bf16[512,256]{1,0:T(8,128)(2,1)S(1)} custom-call(f32[2,512,128]{2,1,0:T(8,128)S(1)} %copy-done.31, f32[512,256]{1,0:T(8,128)S(1)} %shard_map.65.query, f32[16,8,256]{2,1,0:T(8,128)S(1)} %copy-done.33, f32[16,256]{1,0:T(8,128)S(1)} %multiply_add_fusion.start_state, f32[16,256]{1,0:T(8,128)S(1)} %get-tuple-element.29.refs_24_.rates, ...), custom_call_target="tpu_custom_call" | custom-call | flops 8388608 | bytes 20971 | tf_op jit(solution)/shard_map/pallas_call | solution.py:234
  125.4 1.5 collective-permute-done.33
  127.0 1.2 convolution_convert_fusion.3
  128.4 1.1 collective-permute-start.38
  129.5 1.5 convolution_convert_fusion
  131.0 3.6 %collective-permute-done.34 = bf16[256,256]{1,0:T(8,128)(2,1)S(1)} collective-permute-done((bf16[256,256]{1,0:T(8,128)(2,1)S(1)}, bf16[256,256]{1,0:T(8,128)(2,1)S(1)}, u32[]{:S(2)}, u32[]{:S(2)}) %collective-permute-start.34) | collective-permute-done | bytes 131104 | tf_op jit(solution)/shard_map/ppermute | solution.py:45
  134.6 1.4 collective-permute-done.38
  136.4 1.5 convolution_convert_fusion.1
  137.8 6.0 %collective-permute-done.35 = bf16[256,512]{1,0:T(8,128)(2,1)S(1)} collective-permute-done((bf16[256,512]{1,0:T(8,128)(2,1)S(1)}, bf16[256,512]{1,0:T(8,128)(2,1)S(1)}, u32[]{:S(2)}, u32[]{:S(2)}) %collective-permute-start.35) | collective-permute-done | bytes 262176 | tf_op jit(solution)/shard_map/ppermute | solution.py:45
  143.8 2.8 %collective-permute-done.39 = bf16[256,512]{1,0:T(8,128)(2,1)S(1)} collective-permute-done((bf16[256,512]{1,0:T(8,128)(2,1)S(1)}, bf16[256,512]{1,0:T(8,128)(2,1)S(1)}, u32[]{:S(2)}, u32[]{:S(2)}) %collective-permute-start.39) | collective-permute-done | bytes 262176 | tf_op jit(solution)/shard_map/ppermute | solution.py:45
  146.9 1.5 convolution_convert_fusion.2
  148.4 6.0 %collective-permute-done.36 = bf16[256,512]{1,0:T(8,128)(2,1)S(1)} collective-permute-done((bf16[256,512]{1,0:T(8,128)(2,1)S(1)}, bf16[256,512]{1,0:T(8,128)(2,1)S(1)}, u32[]{:S(2)}, u32[]{:S(2)}) %collective-permute-start.36) | collective-permute-done | bytes 262176 | tf_op jit(solution)/shard_map/ppermute | solution.py:45
  154.3 2.8 %collective-permute-done.40 = bf16[256,512]{1,0:T(8,128)(2,1)S(1)} collective-permute-done((bf16[256,512]{1,0:T(8,128)(2,1)S(1)}, bf16[256,512]{1,0:T(8,128)(2,1)S(1)}, u32[]{:S(2)}, u32[]{:S(2)}) %collective-permute-start.40) | collective-permute-done | bytes 262176 | tf_op jit(solution)/shard_map/ppermute | solution.py:45
  157.4 7.5 %collective-permute-done.37 = bf16[256,512]{1,0:T(8,128)(2,1)S(1)} collective-permute-done((bf16[256,512]{1,0:T(8,128)(2,1)S(1)}, bf16[256,512]{1,0:T(8,128)(2,1)S(1)}, u32[]{:S(2)}, u32[]{:S(2)}) %collective-permute-start.37) | collective-permute-done | bytes 262176 | tf_op jit(solution)/shard_map/ppermute | solution.py:45
  164.9 2.8 %collective-permute-done.41 = bf16[256,512]{1,0:T(8,128)(2,1)S(1)} collective-permute-done((bf16[256,512]{1,0:T(8,128)(2,1)S(1)}, bf16[256,512]{1,0:T(8,128)(2,1)S(1)}, u32[]{:S(2)}, u32[]{:S(2)}) %collective-permute-start.41) | collective-permute-done | bytes 262176 | tf_op jit(solution)/shard_map/ppermute | solution.py:45
  167.8 1.5 collective-permute-done.42
  169.3 2.1 %fusion.3 = bf16[256,512]{1,0:T(8,128)(2,1)} fusion(bf16[256,512]{1,0:T(8,128)(2,1)S(1)} %collective-permute-done.42, bf16[512,4096]{1,0:T(8,128)(2,1)} %param.11, s32[]{:T(128)S(6)} %select_n.150, bf16[256,512]{1,0:T(8,128)(2,1)S(1)} %collective-permute-done.37, bf16[256,512]{1,0:T(8,128)(2,1)S(1)} %collective-permute-done.41, ...), kind=kOutput, calls=%fused_computation.8 | convolution fusion | flops 135266304 | bytes 1835017 | tf_op jit(solution)/shard_map/dot_general | solution.py:364
  (147 shorter events, 32.7 us)
Async XLA Ops:
  6.5 67.0 %copy-start = (f32[3,3,512]{2,1,0:T(4,128)S(1)}, f32[3,3,512]{2,1,0:T(4,128)}, u32[]{:S(2)}) copy-start(f32[3,3,512]{2,1,0:T(4,128)} %param.8) | copy-start | bytes 55300
  6.5 103.2 %all-gather.3.cloned.1.call-start = ((), (), s32[]{:S(2)}) async-start(), calls=%async_computation | async-start | bytes 2228224 | tf_op jit(solution)/shard_map/all_gather | solution.py:289
  7.6 1.5 collective-permute-start.18
  10.1 6.7 %collective-permute-start.19 = (bf16[256,512]{1,0:T(8,128)(2,1)S(1)}, bf16[256,512]{1,0:T(8,128)(2,1)S(1)}, u32[]{:S(2)}, u32[]{:S(2)}) collective-permute-start(bf16[256,512]{1,0:T(8,128)(2,1)S(1)} %get-tuple-element.26), channel_id=1, source_target_pairs={{0,16},{8,72},{16,32},{24,88},{32,48},{40,104},{48,0},{56,120},{64... | collective-permute-start | bytes 786440 | tf_op jit(solution)/shard_map/ppermute | solution.py:36
  11.6 6.5 %collective-permute-start.21 = (bf16[256,512]{1,0:T(8,128)(2,1)S(1)}, bf16[256,512]{1,0:T(8,128)(2,1)S(1)}, u32[]{:S(2)}, u32[]{:S(2)}) collective-permute-start(bf16[256,512]{1,0:T(8,128)(2,1)S(1)} %get-tuple-element.26), channel_id=1, source_target_pairs={{0,48},{8,200},{16,0},{24,216},{32,16},{40,232},{48,32},{56,248},{... | collective-permute-start | bytes 786440 | tf_op jit(solution)/shard_map/ppermute | solution.py:36
  16.8 6.3 %collective-permute-start.20 = (bf16[128,512]{1,0:T(8,128)(2,1)S(1)}, bf16[128,512]{1,0:T(8,128)(2,1)S(1)}, u32[]{:S(2)}, u32[]{:S(2)}) collective-permute-start(bf16[128,512]{1,0:T(8,128)(2,1)S(1)} %slice.67), channel_id=1, source_target_pairs={{0,16},{8,72},{16,32},{24,88},{32,48},{40,104},{48,0},{56,120},{64... | collective-permute-start | bytes 393224 | tf_op jit(solution)/shard_map/ppermute | solution.py:36
  18.1 8.4 %collective-permute-start = (bf16[256,512]{1,0:T(8,128)(2,1)}, bf16[256,512]{1,0:T(8,128)(2,1)S(1)}, u32[]{:S(2)}, u32[]{:S(2)}) collective-permute-start(bf16[256,512]{1,0:T(8,128)(2,1)} %param.6), channel_id=1, source_target_pairs={{0,8},{8,0},{1,9},{9,1},{2,10},{10,2},{3,11},{11,3},{4,12},{12,4},... | collective-permute-start | bytes 786440 | tf_op jit(solution)/shard_map/ppermute | solution.py:25
  18.1 5.0 %collective-permute-start.22 = (bf16[128,512]{1,0:T(8,128)(2,1)S(1)}, bf16[128,512]{1,0:T(8,128)(2,1)S(1)}, u32[]{:S(2)}, u32[]{:S(2)}) collective-permute-start(bf16[128,512]{1,0:T(8,128)(2,1)S(1)} %slice.68), channel_id=1, source_target_pairs={{0,48},{8,200},{16,0},{24,216},{32,16},{40,232},{48,32},{56,248},{... | collective-permute-start | bytes 393224 | tf_op jit(solution)/shard_map/ppermute | solution.py:36
  23.2 45.6 %copy-start.2 = (bf16[1024,512]{1,0:T(8,128)(2,1)}, bf16[1024,512]{1,0:T(8,128)(2,1)S(1)}, u32[]{:S(2)}) copy-start(bf16[1024,512]{1,0:T(8,128)(2,1)S(1)} %constant_dynamic-update-slice_fusion.refs_18_) | copy-start | bytes 3145732
  23.2 35.0 %collective-permute-start.23 = (bf16[1024,512]{1,0:T(8,128)(2,1)S(1)}, bf16[1024,512]{1,0:T(8,128)(2,1)S(1)}, u32[]{:S(2)}, u32[]{:S(2)}) collective-permute-start(bf16[1024,512]{1,0:T(8,128)(2,1)S(1)} %constant_dynamic-update-slice_fusion.refs_18_), channel_id=1, source_target_pairs={{0,64},{8,24},{16,80},{24,40},{32,96},{40,56},{48,112},{56,8},{64,... | collective-permute-start | bytes 3145736 | tf_op jit(solution)/shard_map/ppermute | solution.py:36
  24.9 33.6 %collective-permute-start.24 = (bf16[1024,512]{1,0:T(8,128)(2,1)S(1)}, bf16[1024,512]{1,0:T(8,128)(2,1)S(1)}, u32[]{:S(2)}, u32[]{:S(2)}) collective-permute-start(bf16[1024,512]{1,0:T(8,128)(2,1)S(1)} %constant_dynamic-update-slice_fusion.refs_18_), channel_id=1, source_target_pairs={{0,192},{8,56},{16,208},{24,8},{32,224},{40,24},{48,240},{56,40},{... | collective-permute-start | bytes 3145736 | tf_op jit(solution)/shard_map/ppermute | solution.py:36
  26.6 10.3 %collective-permute-start.1 = (bf16[256,512]{1,0:T(8,128)(2,1)S(1)}, bf16[256,512]{1,0:T(8,128)(2,1)S(1)}, u32[]{:S(2)}, u32[]{:S(2)}) collective-permute-start(bf16[256,512]{1,0:T(8,128)(2,1)S(1)} %get-tuple-element.18.refs_0_), channel_id=1, source_target_pairs={{0,1},{1,2},{2,3},{3,4},{4,5},{5,6},{6,7},{7,0},{8,15},{9,8},{10,9... | collective-permute-start | bytes 786440 | tf_op jit(solution)/shard_map/ppermute | solution.py:45
  28.6 5.9 %collective-permute-start.9 = (bf16[16,512]{1,0:T(8,128)(2,1)S(1)}, bf16[16,512]{1,0:T(8,128)(2,1)S(1)}, u32[]{:S(2)}, u32[]{:S(2)}) collective-permute-start(bf16[16,512]{1,0:T(8,128)(2,1)S(1)} %slice.64), channel_id=1, source_target_pairs={{0,16},{8,24},{16,32},{24,40},{32,48},{40,56},{48,64},{56,72},{64,... | collective-permute-start | bytes 49160 | tf_op jit(solution)/shard_map/ppermute | solution.py:295
  34.5 8.6 %collective-permute-start.10 = (bf16[272,512]{1,0:T(8,128)(2,1)S(1)}, bf16[272,512]{1,0:T(8,128)(2,1)S(1)}, u32[]{:S(2)}, u32[]{:S(2)}) collective-permute-start(bf16[272,512]{1,0:T(8,128)(2,1)S(1)} %pad_maximum_fusion.refs_9_), channel_id=1, source_target_pairs={{0,1},{1,2},{2,3},{3,4},{4,5},{5,6},{6,7},{7,0},{8,15},{9,8},{10,9... | collective-permute-start | bytes 835592 | tf_op jit(solution)/shard_map/ppermute | solution.py:45
  36.9 36.7 %copy-start.13 = (bf16[256,512]{1,0:T(8,128)(2,1)}, bf16[256,512]{1,0:T(8,128)(2,1)S(1)}, u32[]{:S(2)}) copy-start(bf16[256,512]{1,0:T(8,128)(2,1)S(1)} %collective-permute-done.1.refs_1_) | copy-start | bytes 786436
  36.9 9.0 %collective-permute-start.2 = (bf16[256,512]{1,0:T(8,128)(2,1)S(1)}, bf16[256,512]{1,0:T(8,128)(2,1)S(1)}, u32[]{:S(2)}, u32[]{:S(2)}) collective-permute-start(bf16[256,512]{1,0:T(8,128)(2,1)S(1)} %collective-permute-done.1.refs_1_), channel_id=1, source_target_pairs={{0,1},{1,2},{2,3},{3,4},{4,5},{5,6},{6,7},{7,0},{8,15},{9,8},{10,9... | collective-permute-start | bytes 786440 | tf_op jit(solution)/shard_map/ppermute | solution.py:45
  43.0 11.3 %collective-permute-start.11 = (bf16[272,512]{1,0:T(8,128)(2,1)S(1)}, bf16[272,512]{1,0:T(8,128)(2,1)S(1)}, u32[]{:S(2)}, u32[]{:S(2)}) collective-permute-start(bf16[272,512]{1,0:T(8,128)(2,1)S(1)} %collective-permute-done.10.refs_10_), channel_id=1, source_target_pairs={{0,1},{1,2},{2,3},{3,4},{4,5},{5,6},{6,7},{7,0},{8,15},{9,8},{10,9... | collective-permute-start | bytes 835592 | tf_op jit(solution)/shard_map/ppermute | solution.py:45
  45.9 8.5 %collective-permute-start.3 = (bf16[256,512]{1,0:T(8,128)(2,1)S(1)}, bf16[256,512]{1,0:T(8,128)(2,1)S(1)}, u32[]{:S(2)}, u32[]{:S(2)}) collective-permute-start(bf16[256,512]{1,0:T(8,128)(2,1)S(1)} %collective-permute-done.2.refs_2_), channel_id=1, source_target_pairs={{0,1},{1,2},{2,3},{3,4},{4,5},{5,6},{6,7},{7,0},{8,15},{9,8},{10,9... | collective-permute-start | bytes 786440 | tf_op jit(solution)/shard_map/ppermute | solution.py:45
  45.9 15.3 %collective-permute-start.14 = (bf16[272,512]{1,0:T(8,128)(2,1)S(1)}, bf16[272,512]{1,0:T(8,128)(2,1)S(1)}, u32[]{:S(2)}, u32[]{:S(2)}) collective-permute-start(bf16[272,512]{1,0:T(8,128)(2,1)S(1)} %collective-permute-done.10.refs_10_), channel_id=1, source_target_pairs={{0,8},{8,0},{1,9},{9,1},{2,10},{10,2},{3,11},{11,3},{4,12},{12,4},... | collective-permute-start | bytes 835592 | tf_op jit(solution)/shard_map/ppermute | solution.py:25
  54.3 7.8 %collective-permute-start.12 = (bf16[272,512]{1,0:T(8,128)(2,1)S(1)}, bf16[272,512]{1,0:T(8,128)(2,1)S(1)}, u32[]{:S(2)}, u32[]{:S(2)}) collective-permute-start(bf16[272,512]{1,0:T(8,128)(2,1)S(1)} %collective-permute-done.11.refs_11_), channel_id=1, source_target_pairs={{0,1},{1,2},{2,3},{3,4},{4,5},{5,6},{6,7},{7,0},{8,15},{9,8},{10,9... | collective-permute-start | bytes 835592 | tf_op jit(solution)/shard_map/ppermute | solution.py:45
  54.3 6.1 %collective-permute-start.5 = (bf16[256,512]{1,0:T(8,128)(2,1)S(1)}, bf16[256,512]{1,0:T(8,128)(2,1)S(1)}, u32[]{:S(2)}, u32[]{:S(2)}) collective-permute-start(bf16[256,512]{1,0:T(8,128)(2,1)S(1)} %collective-permute-done.1.refs_1_), channel_id=1, source_target_pairs={{0,8},{8,0},{1,9},{9,1},{2,10},{10,2},{3,11},{11,3},{4,12},{12,4},... | collective-permute-start | bytes 786440 | tf_op jit(solution)/shard_map/ppermute | solution.py:25
  58.2 7.6 %collective-permute-start.6 = (bf16[256,512]{1,0:T(8,128)(2,1)S(1)}, bf16[256,512]{1,0:T(8,128)(2,1)S(1)}, u32[]{:S(2)}, u32[]{:S(2)}) collective-permute-start(bf16[256,512]{1,0:T(8,128)(2,1)S(1)} %collective-permute-done.2.refs_2_), channel_id=1, source_target_pairs={{0,8},{8,0},{1,9},{9,1},{2,10},{10,2},{3,11},{11,3},{4,12},{12,4},... | collective-permute-start | bytes 786440 | tf_op jit(solution)/shard_map/ppermute | solution.py:25
  58.5 9.1 %collective-permute-start.15 = (bf16[272,512]{1,0:T(8,128)(2,1)S(1)}, bf16[272,512]{1,0:T(8,128)(2,1)S(1)}, u32[]{:S(2)}, u32[]{:S(2)}) collective-permute-start(bf16[272,512]{1,0:T(8,128)(2,1)S(1)} %collective-permute-done.11.refs_11_), channel_id=1, source_target_pairs={{0,8},{8,0},{1,9},{9,1},{2,10},{10,2},{3,11},{11,3},{4,12},{12,4},... | collective-permute-start | bytes 835592 | tf_op jit(solution)/shard_map/ppermute | solution.py:25
  61.2 6.4 %collective-permute-start.4 = (bf16[256,256]{1,0:T(8,128)(2,1)S(1)}, bf16[256,256]{1,0:T(8,128)(2,1)}, u32[]{:S(2)}, u32[]{:S(2)}) collective-permute-start(bf16[256,256]{1,0:T(8,128)(2,1)S(1)} %constant_dynamic-slice_fusion.4), channel_id=1, source_target_pairs={{0,1},{1,2},{2,3},{3,4},{4,5},{5,6},{6,7},{7,0},{8,15},{9,8},{10,9... | collective-permute-start | bytes 393224 | tf_op jit(solution)/shard_map/ppermute | solution.py:45
  61.2 14.3 %collective-permute-start.25 = (bf16[512,512]{1,0:T(8,128)(2,1)}, bf16[512,512]{1,0:T(8,128)(2,1)}, u32[]{:S(2)}, u32[]{:S(2)}) collective-permute-start(bf16[512,512]{1,0:T(8,128)(2,1)} %slice.69), channel_id=1, source_target_pairs={{0,64},{8,24},{16,80},{24,40},{32,96},{40,56},{48,112},{56,8},{64,... | collective-permute-start | bytes 1572872 | tf_op jit(solution)/shard_map/ppermute | solution.py:36
  62.2 13.4 %collective-permute-start.26 = (bf16[512,512]{1,0:T(8,128)(2,1)}, bf16[512,512]{1,0:T(8,128)(2,1)}, u32[]{:S(2)}, u32[]{:S(2)}) collective-permute-start(bf16[512,512]{1,0:T(8,128)(2,1)} %slice.70), channel_id=1, source_target_pairs={{0,192},{8,56},{16,208},{24,8},{32,224},{40,24},{48,240},{56,40},{... | collective-permute-start | bytes 1572872 | tf_op jit(solution)/shard_map/ppermute | solution.py:36
  66.6 6.3 %collective-permute-start.13 = (bf16[272,256]{1,0:T(8,128)(2,1)S(1)}, bf16[272,256]{1,0:T(8,128)(2,1)S(1)}, u32[]{:S(2)}, u32[]{:S(2)}) collective-permute-start(bf16[272,256]{1,0:T(8,128)(2,1)S(1)} %constant_dynamic-slice_fusion.3), channel_id=1, source_target_pairs={{0,1},{1,2},{2,3},{3,4},{4,5},{5,6},{6,7},{7,0},{8,15},{9,8},{10,9... | collective-permute-start | bytes 417800 | tf_op jit(solution)/shard_map/ppermute | solution.py:45
  67.6 6.0 %collective-permute-start.8 = (bf16[256,256]{1,0:T(8,128)(2,1)}, bf16[256,256]{1,0:T(8,128)(2,1)}, u32[]{:S(2)}, u32[]{:S(2)}) collective-permute-start(bf16[256,256]{1,0:T(8,128)(2,1)} %collective-permute-done.4.refs_4_), channel_id=1, source_target_pairs={{0,8},{8,0},{1,9},{9,1},{2,10},{10,2},{3,11},{11,3},{4,12},{12,4},... | collective-permute-start | bytes 393224 | tf_op jit(solution)/shard_map/ppermute | solution.py:25
  68.3 6.7 %collective-permute-start.7 = (bf16[256,512]{1,0:T(8,128)(2,1)S(1)}, bf16[256,512]{1,0:T(8,128)(2,1)}, u32[]{:S(2)}, u32[]{:S(2)}) collective-permute-start(bf16[256,512]{1,0:T(8,128)(2,1)S(1)} %collective-permute-done.3.refs_3_), channel_id=1, source_target_pairs={{0,8},{8,0},{1,9},{9,1},{2,10},{10,2},{3,11},{11,3},{4,12},{12,4},... | collective-permute-start | bytes 786440 | tf_op jit(solution)/shard_map/ppermute | solution.py:25
  73.5 2.0 %collective-permute-start.16 = (bf16[272,512]{1,0:T(8,128)(2,1)S(1)}, bf16[272,512]{1,0:T(8,128)(2,1)}, u32[]{:S(2)}, u32[]{:S(2)}) collective-permute-start(bf16[272,512]{1,0:T(8,128)(2,1)S(1)} %collective-permute-done.12.refs_12_), channel_id=1, source_target_pairs={{0,8},{8,0},{1,9},{9,1},{2,10},{10,2},{3,11},{11,3},{4,12},{12,4},... | collective-permute-start | bytes 835592 | tf_op jit(solution)/shard_map/ppermute | solution.py:25
  73.6 1.9 %collective-permute-start.17 = (bf16[272,256]{1,0:T(8,128)(2,1)}, bf16[272,256]{1,0:T(8,128)(2,1)S(1)}, u32[]{:S(2)}, u32[]{:S(2)}) collective-permute-start(bf16[272,256]{1,0:T(8,128)(2,1)} %copy-done.25), channel_id=1, source_target_pairs={{0,8},{8,0},{1,9},{9,1},{2,10},{10,2},{3,11},{11,3},{4,12},{12,4},... | collective-permute-start | bytes 417800 | tf_op jit(solution)/shard_map/ppermute | solution.py:25
  92.1 31.3 %copy-start.33 = (f32[16,8,256]{2,1,0:T(8,128)S(1)}, f32[16,8,256]{2,1,0:T(8,128)}, u32[]{:S(2)}) copy-start(f32[16,8,256]{2,1,0:T(8,128)} %copy-done.32) | copy-start | bytes 393220
  92.1 5.2 %collective-permute-start.27 = (f32[16,256]{1,0:T(8,128)S(1)}, f32[16,256]{1,0:T(8,128)S(1)}, u32[]{:S(2)}, u32[]{:S(2)}) collective-permute-start(f32[16,256]{1,0:T(8,128)S(1)} %get-tuple-element.10), channel_id=1, source_target_pairs={{0,16},{16,32},{32,48},{48,0},{1,17},{17,33},{33,49},{49,1},{2,18}... | collective-permute-start | bytes 49160 | tf_op jit(solution)/shard_map/ppermute | solution.py:16
  93.3 5.2 %collective-permute-start.28 = (f32[16,256]{1,0:T(8,128)S(1)}, f32[16,256]{1,0:T(8,128)S(1)}, u32[]{:S(2)}, u32[]{:S(2)}) collective-permute-start(f32[16,256]{1,0:T(8,128)S(1)} %get-tuple-element.10), channel_id=1, source_target_pairs={{0,32},{16,48},{32,0},{48,16},{1,33},{17,49},{33,1},{49,17},{2,34}... | collective-permute-start | bytes 49160 | tf_op jit(solution)/shard_map/ppermute | solution.py:16
  95.6 3.7 %collective-permute-start.29 = (f32[16,256]{1,0:T(8,128)S(1)}, f32[16,256]{1,0:T(8,128)S(1)}, u32[]{:S(2)}, u32[]{:S(2)}) collective-permute-start(f32[16,256]{1,0:T(8,128)S(1)} %get-tuple-element.10), channel_id=1, source_target_pairs={{0,48},{16,0},{32,16},{48,32},{1,49},{17,1},{33,17},{49,33},{2,50}... | collective-permute-start | bytes 49160 | tf_op jit(solution)/shard_map/ppermute | solution.py:16
  99.4 9.2 %collective-permute-start.30 = (f32[16,256]{1,0:T(8,128)S(1)}, f32[16,256]{1,0:T(8,128)S(1)}, u32[]{:S(2)}, u32[]{:S(2)}) collective-permute-start(f32[16,256]{1,0:T(8,128)S(1)} %multiply_add_fusion.1), channel_id=1, source_target_pairs={{0,64},{64,128},{128,192},{1,65},{65,129},{129,193},{2,66},{66,130... | collective-permute-start | bytes 49160 | tf_op jit(solution)/shard_map/ppermute | solution.py:21
  102.0 6.6 %collective-permute-start.31 = (f32[16,256]{1,0:T(8,128)S(1)}, f32[16,256]{1,0:T(8,128)S(1)}, u32[]{:S(2)}, u32[]{:S(2)}) collective-permute-start(f32[16,256]{1,0:T(8,128)S(1)} %multiply_add_fusion.1), channel_id=1, source_target_pairs={{0,128},{64,192},{1,129},{65,193},{2,130},{66,194},{3,131},{67,195... | collective-permute-start | bytes 49160 | tf_op jit(solution)/shard_map/ppermute | solution.py:21
  107.0 2.7 %collective-permute-start.32 = (f32[16,256]{1,0:T(8,128)S(1)}, f32[16,256]{1,0:T(8,128)S(1)}, u32[]{:S(2)}, u32[]{:S(2)}) collective-permute-start(f32[16,256]{1,0:T(8,128)S(1)} %multiply_add_fusion.1), channel_id=1, source_target_pairs={{0,192},{1,193},{2,194},{3,195},{4,196},{5,197},{6,198},{7,199},{8... | collective-permute-start | bytes 49160 | tf_op jit(solution)/shard_map/ppermute | solution.py:21
  125.3 1.6 collective-permute-start.33
  128.3 6.3 %collective-permute-start.34 = (bf16[256,256]{1,0:T(8,128)(2,1)S(1)}, bf16[256,256]{1,0:T(8,128)(2,1)S(1)}, u32[]{:S(2)}, u32[]{:S(2)}) collective-permute-start(bf16[256,256]{1,0:T(8,128)(2,1)S(1)} %get-tuple-element.24), channel_id=1, source_target_pairs={{0,1},{1,2},{2,3},{3,4},{4,5},{5,6},{6,7},{7,0},{8,15},{9,8},{10,9... | collective-permute-start | bytes 393224 | tf_op jit(solution)/shard_map/ppermute | solution.py:45
  128.4 7.6 %collective-permute-start.38 = (bf16[256,256]{1,0:T(8,128)(2,1)S(1)}, bf16[256,256]{1,0:T(8,128)(2,1)S(1)}, u32[]{:S(2)}, u32[]{:S(2)}) collective-permute-start(bf16[256,256]{1,0:T(8,128)(2,1)S(1)} %get-tuple-element.25), channel_id=1, source_target_pairs={{0,1},{1,2},{2,3},{3,4},{4,5},{5,6},{6,7},{7,0},{8,15},{9,8},{10,9... | collective-permute-start | bytes 393224 | tf_op jit(solution)/shard_map/ppermute | solution.py:45
  136.1 7.7 %collective-permute-start.35 = (bf16[256,512]{1,0:T(8,128)(2,1)S(1)}, bf16[256,512]{1,0:T(8,128)(2,1)S(1)}, u32[]{:S(2)}, u32[]{:S(2)}) collective-permute-start(bf16[256,512]{1,0:T(8,128)(2,1)S(1)} %get-tuple-element.15), channel_id=1, source_target_pairs={{0,1},{1,2},{2,3},{3,4},{4,5},{5,6},{6,7},{7,0},{8,15},{9,8},{10,9... | collective-permute-start | bytes 786440 | tf_op jit(solution)/shard_map/ppermute | solution.py:45
  136.2 10.4 %collective-permute-start.39 = (bf16[256,512]{1,0:T(8,128)(2,1)S(1)}, bf16[256,512]{1,0:T(8,128)(2,1)S(1)}, u32[]{:S(2)}, u32[]{:S(2)}) collective-permute-start(bf16[256,512]{1,0:T(8,128)(2,1)S(1)} %get-tuple-element.16), channel_id=1, source_target_pairs={{0,1},{1,2},{2,3},{3,4},{4,5},{5,6},{6,7},{7,0},{8,15},{9,8},{10,9... | collective-permute-start | bytes 786440 | tf_op jit(solution)/shard_map/ppermute | solution.py:45
  146.7 7.7 %collective-permute-start.36 = (bf16[256,512]{1,0:T(8,128)(2,1)S(1)}, bf16[256,512]{1,0:T(8,128)(2,1)S(1)}, u32[]{:S(2)}, u32[]{:S(2)}) collective-permute-start(bf16[256,512]{1,0:T(8,128)(2,1)S(1)} %get-tuple-element.13), channel_id=1, source_target_pairs={{0,1},{1,2},{2,3},{3,4},{4,5},{5,6},{6,7},{7,0},{8,15},{9,8},{10,9... | collective-permute-start | bytes 786440 | tf_op jit(solution)/shard_map/ppermute | solution.py:45
  146.8 10.4 %collective-permute-start.40 = (bf16[256,512]{1,0:T(8,128)(2,1)S(1)}, bf16[256,512]{1,0:T(8,128)(2,1)S(1)}, u32[]{:S(2)}, u32[]{:S(2)}) collective-permute-start(bf16[256,512]{1,0:T(8,128)(2,1)S(1)} %get-tuple-element.14), channel_id=1, source_target_pairs={{0,1},{1,2},{2,3},{3,4},{4,5},{5,6},{6,7},{7,0},{8,15},{9,8},{10,9... | collective-permute-start | bytes 786440 | tf_op jit(solution)/shard_map/ppermute | solution.py:45
  157.2 7.7 %collective-permute-start.37 = (bf16[256,512]{1,0:T(8,128)(2,1)S(1)}, bf16[256,512]{1,0:T(8,128)(2,1)S(1)}, u32[]{:S(2)}, u32[]{:S(2)}) collective-permute-start(bf16[256,512]{1,0:T(8,128)(2,1)S(1)} %get-tuple-element.11), channel_id=1, source_target_pairs={{0,1},{1,2},{2,3},{3,4},{4,5},{5,6},{6,7},{7,0},{8,15},{9,8},{10,9... | collective-permute-start | bytes 786440 | tf_op jit(solution)/shard_map/ppermute | solution.py:45
  157.3 10.4 %collective-permute-start.41 = (bf16[256,512]{1,0:T(8,128)(2,1)S(1)}, bf16[256,512]{1,0:T(8,128)(2,1)S(1)}, u32[]{:S(2)}, u32[]{:S(2)}) collective-permute-start(bf16[256,512]{1,0:T(8,128)(2,1)S(1)} %get-tuple-element.12), channel_id=1, source_target_pairs={{0,1},{1,2},{2,3},{3,4},{4,5},{5,6},{6,7},{7,0},{8,15},{9,8},{10,9... | collective-permute-start | bytes 786440 | tf_op jit(solution)/shard_map/ppermute | solution.py:45
  167.7 1.6 collective-permute-start.42
  (31 other events, 120.4 us)
Sparse Core Ops, SparseCore 0:
  10.2 52.9 all-gather.2

commit v2 on v1

v2 whole, which is shorter than its diff:
```python
import functools

import jax
import jax.numpy as jnp
from jax import lax
from jax.experimental import pallas as pl
from jax.experimental.pallas import tpu as pltpu
from jax.sharding import Mesh, PartitionSpec as P

HALO = 16


def swap_cores(block):
    return lax.ppermute(block, "core", [(0, 1), (1, 0)])


def chip_ring(block, sides, stage, sign):
    ny, nx = sides
    pairs = []
    for y in range(ny):
        for x in range(nx):
            for c in range(2):
                to = (y, (x + sign) % nx) if c == stage else ((y + sign) % ny, x)
                pairs.append(((y * nx + x) * 2 + c, (to[0] * nx + to[1]) * 2 + c))
    return lax.ppermute(block, ("y", "x", "core"), pairs)


def group_ring(block):
    n = lax.axis_size("chan")
    pairs = []
    for c in range(2):
        for z in range(n):
            pairs.append((c * n + z, c * n + (z + 1 - 2 * c) % n))
    return lax.ppermute(block, ("core", "chan"), pairs)


def weights_around(block, sides):
    def ring(own, stage):
        half = own.shape[0] // 2
        before = chip_ring(own, sides, stage, 1)
        behind = chip_ring(own, sides, stage, -1)
        far = chip_ring(before[:half], sides, stage, 1), chip_ring(behind[half:], sides, stage, -1)
        return before, behind, far

    before, behind, far = ring(block, 0)
    near = jnp.concatenate([block, before, *far, behind], axis=0)
    before, behind, far = ring(near, 1)
    return near, before, behind, *far


def tokens_around(block, core):
    blocks = [block]
    for _ in range(3):
        blocks.append(group_ring(blocks[-1]))
    half = block.shape[1] // 2
    blocks.append(group_ring(lax.dynamic_slice_in_dim(blocks[-1], core * half, half, axis=1)))
    return blocks[1:]


def tokens_in_order(place, groups, blocks, gathered, semaphores):
    copies = []
    core = place[1]
    ahead = 1 - 2 * core
    own, mine, partner = blocks
    depth = own.shape[1]
    pieces = [(own, 0, 0, 0)]
    for distance, block in enumerate(mine, 1):
        pieces.append((block, -distance, distance == len(mine), core))
    for distance, block in enumerate(partner, 1):
        pieces.append((block, distance, distance == len(partner), 1 - core))
    for block, offset, halved, side in pieces:
        group = lax.rem(place[0] + offset * ahead + groups, groups)
        column = group * depth
        if halved:
            column = column + side * (depth // 2)
        column = pl.multiple_of(column, 128)
        copies.append(
            pltpu.make_async_copy(
                block,
                gathered.at[:, pl.ds(column, block.shape[1])],
                semaphores.at[len(copies)],
            )
        )
    for copy in copies:
        copy.start()
    return copies


def weights_in_order(place, sides, blocks, gathered, semaphores):
    ny, nx = sides
    core, y, x = place[1], place[2], place[3]
    near, before, behind, far_top, far_bottom = blocks
    rows = near.shape[0] // 4
    order = (0, -1, -2, 1)
    pieces = [(near, i, first, 0) for i, first in enumerate(order)]
    pieces += [(before, i, first, -1) for i, first in enumerate(order)]
    pieces += [(behind, i, first, 1) for i, first in enumerate(order)]
    pieces += [(far_top, i, order[i], -2) for i in range(2)]
    pieces += [(far_bottom, i, order[i + 2], -2) for i in range(2)]
    copies = []
    for block, i, first, second in pieces:
        dx = jnp.where(core == 0, first, second)
        dy = jnp.where(core == 0, second, first)
        chip = lax.rem(y + dy + ny, ny) * nx + lax.rem(x + dx + nx, nx)
        to = pl.multiple_of(chip * rows, 128)
        copies.append(
            pltpu.make_async_copy(
                block.at[pl.ds(i * rows, rows)],
                gathered.at[pl.ds(to, rows)],
                semaphores.at[len(copies)],
            )
        )
    for copy in copies:
        copy.start()
    return copies


def take_tokens(refs):
    return refs[0], refs[1:5], refs[5:9]


def project(tokens, weight, columns, projected):
    rows = tokens.shape[0] - HALO
    total = jnp.dot(tokens[...], weight[:, columns], preferred_element_type=jnp.float32)
    total = total.astype(jnp.bfloat16).astype(jnp.float32)
    projected[pl.ds(0, HALO), columns] = total[rows:]
    projected[pl.ds(HALO, rows), columns] = total[:rows]


def filtered(projected, taps, group, channels, columns):
    rows = projected.shape[0] - HALO
    return sum(
        taps[group, lag : lag + 1, channels] * projected[pl.ds(HALO - lag, rows), columns]
        for lag in range(taps.shape[1])
    )


def project_kernel(groups, sides, place, *refs):
    blocks, weights, query_weight = take_tokens(refs[:9]), refs[9:14], refs[14]
    taps, rates, query, signal, block_ends, end_state, tokens, weight, projected, *semaphores = refs[15:]
    width = query.shape[1]
    early = tokens_in_order(place, groups, blocks, tokens, semaphores[0])
    copy = pltpu.make_async_copy(
        query_weight, weight.at[:, pl.ds(2 * width, width)], semaphores[1].at[0]
    )
    copy.start()
    late = weights_in_order(place, sides, weights, weight.at[:, pl.ds(0, 2 * width)], semaphores[2])
    for each in early + [copy]:
        each.wait()
    project(tokens, weight, pl.ds(2 * width, width), projected)
    query[...] = filtered(projected, taps, 0, slice(None), pl.ds(2 * width, width))
    for each in late:
        each.wait()
    project(tokens, weight, pl.ds(0, 2 * width), projected)
    modes, blocks, width = block_ends.shape
    steps = signal.shape[1] // blocks
    for part in range(width // 128):
        lanes = pl.ds(part * 128, 128)
        key = filtered(projected, taps, 1, lanes, lanes)
        value = filtered(projected, taps, 2, lanes, pl.ds(width + part * 128, 128))
        signal[part] = key * value
        decay = [
            jnp.broadcast_to(jnp.exp(-rates[m : m + 1, lanes]), (blocks, 128)) for m in range(modes)
        ]

        def step(s, states):
            u = signal[part, pl.ds(s, blocks, steps), :]
            return tuple(decay[m] * states[m] + u for m in range(modes))

        zero = jnp.zeros((blocks, 128), jnp.float32)
        states = lax.fori_loop(0, steps, step, (zero,) * modes, unroll=8)
        for m in range(modes):
            block_ends[m, :, lanes] = states[m]
    block_decay = jnp.exp(-rates[...] * float(steps))
    state = block_ends[:, 0, :]
    for b in range(1, blocks):
        state = block_decay * state + block_ends[:, b, :]
    end_state[...] = state


def scan_kernel(place, signal, query, block_ends, states, rates, amplitude, gated, block_starts, result):
    modes, blocks, width = block_ends.shape
    steps = signal.shape[1] // blocks
    chip_decay = jnp.exp(-rates[...] * float(steps * blocks))
    state = jnp.zeros((modes, width), jnp.float32)
    for chip in range(states.shape[0] - 1):
        state = jnp.where(chip < place[4], chip_decay * state + states[chip], state)
    block_decay = jnp.exp(-rates[...] * float(steps))
    for b in range(blocks):
        block_starts[:, b, :] = state
        state = block_decay * state + block_ends[:, b, :]
    for part in range(width // 128):
        lanes = pl.ds(part * 128, 128)
        decay = [
            jnp.broadcast_to(jnp.exp(-rates[m : m + 1, lanes]), (blocks, 128)) for m in range(modes)
        ]
        scale = [jnp.broadcast_to(amplitude[m : m + 1, lanes], (blocks, 128)) for m in range(modes)]

        def step(s, states):
            u = signal[part, pl.ds(s, blocks, steps), :]
            states = tuple(decay[m] * states[m] + u for m in range(modes))
            terms = [scale[m] * states[m] for m in range(modes)]
            while len(terms) > 1:
                terms = [a + b for a, b in zip(terms[::2], terms[1::2])]
            result[part, pl.ds(s, blocks, steps), :] = terms[0]
            return states

        states_now = tuple(block_starts[m, :, lanes] for m in range(modes))
        lax.fori_loop(0, steps, step, states_now, unroll=4)
        gated[:, lanes] = (query[:, lanes] * result[part]).astype(jnp.bfloat16)


def on_device(kernel, outs, scratch, cost, limit, copied, place, *arrays):
    smem = pl.BlockSpec(memory_space=pltpu.SMEM)
    vmem = pl.BlockSpec(memory_space=pltpu.VMEM)
    hbm = pl.BlockSpec(memory_space=pltpu.HBM)
    kept = [pltpu.with_memory_space_constraint(a, pltpu.HBM) for a in arrays[:copied]]
    return pl.pallas_call(
        kernel,
        out_shape=outs,
        in_specs=[smem] + [hbm] * copied + [vmem] * (len(arrays) - copied),
        out_specs=jax.tree.map(lambda _: vmem, outs),
        scratch_shapes=scratch,
        compiler_params=pltpu.CompilerParams(vmem_limit_bytes=limit * 1024 * 1024),
        cost_estimate=pl.CostEstimate(flops=cost, bytes_accessed=cost // 400, transcendentals=0),
    )(place, *kept, *arrays[copied:])


def shards(tokens, input_weight, short_taps, residue, decay_rate, out_weight):
    f32, bf16 = jnp.float32, jnp.bfloat16
    rows, depth = tokens.shape
    width = input_weight.shape[2] // 2
    groups = lax.axis_size("chan")
    sides = lax.axis_size("y"), lax.axis_size("x")
    chips = sides[0] * sides[1]
    core, z = lax.axis_index("core"), lax.axis_index("chan")
    positions = 2 * rows
    sequence = positions * chips
    y, x = lax.axis_index("y"), lax.axis_index("x")
    place = jnp.stack([z, core, y, x, y * sides[1] + x]).astype(jnp.int32)

    def own_columns(array, owner):
        return lax.dynamic_slice_in_dim(array, owner * width, width, axis=array.ndim - 1)

    def by_core(own, other, axis):
        return jnp.where(
            core == 0,
            jnp.concatenate([own, other], axis=axis),
            jnp.concatenate([other, own], axis=axis),
        )

    other = swap_cores(tokens)
    block = by_core(tokens, other, 0)
    earlier = lax.ppermute(
        block[-HALO:], ("y", "x", "core"), [(i, i + 2) for i in range(2 * chips - 2)]
    )
    block = jnp.concatenate([block, earlier], axis=0)
    mine = tokens_around(block, core)
    gathered = [block, *mine, *[swap_cores(each) for each in mine]]

    kept = own_columns(input_weight, core)
    got = swap_cores(own_columns(input_weight, 1 - core))
    both = by_core(kept, got, 1)
    query_weight = lax.all_gather(both[0].reshape(-1, width), ("y", "x"), axis=0, tiled=True)
    key_value, _ = lax.optimization_barrier((jnp.concatenate([both[1], both[2]], axis=1), other))
    weights = weights_around(key_value, sides)

    rates_all = decay_rate / float(sequence)
    rates = own_columns(rates_all, core)
    amplitude = own_columns(residue * jnp.sqrt(-jnp.expm1(-2.0 * rates_all)), core)
    taps = own_columns(short_taps, core)
    modes = rates.shape[0]
    blocks = 8
    lanes = (width // 128, positions, 128)
    features = depth * groups
    dma = pltpu.SemaphoreType.DMA

    query, signal, block_ends, end_state = on_device(
        functools.partial(project_kernel, groups, sides),
        (
            jax.ShapeDtypeStruct((positions, width), f32),
            jax.ShapeDtypeStruct(lanes, f32),
            jax.ShapeDtypeStruct((modes, blocks, width), f32),
            jax.ShapeDtypeStruct((modes, width), f32),
        ),
        [
            pltpu.VMEM((positions + HALO, features), bf16),
            pltpu.VMEM((features, 3 * width), bf16),
            pltpu.VMEM((positions + HALO, 3 * width), f32),
            dma((9,)),
            dma((1,)),
            dma((16,)),
        ],
        6 * positions * features * width,
        24,
        15,
        place, *gathered, *weights, query_weight, taps, rates,
    )
    states = lax.all_to_all(
        jnp.broadcast_to(end_state[None], (chips, modes, width)), ("y", "x"), 0, 0, tiled=True
    )
    gated = on_device(
        scan_kernel,
        jax.ShapeDtypeStruct((positions, width), bf16),
        [pltpu.VMEM((modes, blocks, width), f32), pltpu.VMEM(lanes, f32)],
        4 * modes * positions * width,
        12,
        0,
        place, signal, query, block_ends, states, rates, amplitude,
    )
    gated = by_core(gated, swap_cores(gated), 1)
    return reduced(gated, out_weight, core, z, groups)


def reduced(gated, out_weight, core, z, groups):
    rows = gated.shape[0] // 2
    width = out_weight.shape[1] // groups
    ahead = 1 - 2 * core

    def product(values, distance, first=0, columns=width):
        start = (z + ahead * distance) % groups * width + first
        weight = lax.dynamic_slice_in_dim(out_weight, start, columns, axis=1)
        return jnp.dot(values, weight, preferred_element_type=jnp.float32).astype(jnp.bfloat16)

    half = width // 2
    part = product(gated, 4, core * half, half)
    cut = rows - 16
    spans = slice(0, cut), slice(cut, 2 * rows)
    streams = [part[span] for span in spans]
    own = product(lax.dynamic_slice_in_dim(gated, core * rows, rows, axis=0), 0)
    for distance in (3, 2, 1):
        part = product(gated, distance)
        for number, span in enumerate(spans):
            arrived = group_ring(streams[number])
            if distance == 3:
                nothing = jnp.zeros_like(arrived)
                arrived = jnp.where(
                    core == 0,
                    jnp.concatenate([arrived, nothing], axis=1),
                    jnp.concatenate([nothing, arrived], axis=1),
                )
            before = own if number == 0 else streams[0]
            arrived, _ = lax.optimization_barrier((arrived, before))
            streams[number] = part[span] + arrived
    total = jnp.concatenate([group_ring(stream) for stream in streams], axis=0)
    kept = lax.dynamic_slice_in_dim(total, core * rows, rows, axis=0)
    got = swap_cores(lax.dynamic_slice_in_dim(total, (1 - core) * rows, rows, axis=0))
    total = own.astype(jnp.float32) + kept.astype(jnp.float32) + got.astype(jnp.float32)
    return total.astype(jnp.bfloat16)


def solution(mesh):
    devices = mesh.devices.reshape(4, 4, 2, 8)
    chips = Mesh(devices, ("y", "x", "core", "chan"))
    seq = ("y", "x", "core")
    placed = (
        P(seq, "chan"),
        P(None, seq, "chan"),
        P(None, None, "chan"),
        P(None, "chan"),
        P(None, "chan"),
        P("chan", None),
    )
    return jax.shard_map(
        shards, mesh=chips, in_specs=placed, out_specs=P(seq, "chan"), check_vma=False
    )
```

time: 181 us -> 147 us (0.81)
  local copies, waits for them, and re-layouts: 26.8 us -> 2.16 us
  starting transfers between devices: 52.8 us -> 38.2 us
  blocking collectives: 0 us -> 14.5 us
  waiting for transfers between devices: 63.8 us -> 54.4 us
    unnamed x73 -> x25, local copies, waits for them, and re-layouts: 23.2 us -> 0.11 us
    all_to_all x0 -> x1, blocking collectives: none -> 14.5 us  [shards(): lax.all_to_all(jnp.broadcast_to(end_state[None], (chips, modes, width)),...]
    ppermute x7 -> x1, starting transfers between devices: 17.4 us -> 3.4 us  [shards(): lax.ppermute(block[-HALO:], ('y', 'x', 'core'), [(i, i + 2) for i in rang...]
    ppermute x16 -> x12, starting transfers between devices: 7.23 us -> 17.9 us  [group_ring(): return lax.ppermute(block, ('core', 'chan'), pairs)]
    ppermute x12 -> x8, starting transfers between devices: 14.2 us -> 4.82 us  [swap_cores(): return lax.ppermute(block, 'core', [(0, 1), (1, 0)])]
    ppermute x16 -> x12, waiting for transfers between devices: 45.7 us -> 36.8 us  [group_ring(): return lax.ppermute(block, ('core', 'chan'), pairs)]
    ppermute x7 -> x1, waiting for transfers between devices: 6.05 us -> 0.92 us  [shards(): lax.ppermute(block[-HALO:], ('y', 'x', 'core'), [(i, i + 2) for i in rang...]
    ppermute x8, waiting for transfers between devices: 7.09 us -> 10.9 us  [chip_ring(): return lax.ppermute(block, ('y', 'x', 'core'), pairs)]
  transfers between devices with their start and end apart: 44 -> 30, of which waited for: 24 -> 19; matrix products, arithmetic and copies ran while one was open for 4% -> 5% of each run, Pallas kernels for 3% -> 0%
where the time goes in v2:
time: 147 us; the launch traced here: 145 us
  waiting for transfers between devices  54.4 us (37%)
  starting transfers between devices  38.2 us (26%)
  blocking collectives  14.5 us (10%)
  between operations  13.8 us (9%)
  Pallas kernels  12.1 us (8%)
  matrix products  7.02 us (5%)
  other arithmetic  2.63 us (2%)
  local copies, waits for them, and re-layouts  2.16 us (1%)
    ppermute x12, waiting for transfers between devices, group_ring(): return lax.ppermute(block, ('core', 'chan'), pairs)  36.8 us
    ppermute x12, starting transfers between devices, group_ring(): return lax.ppermute(block, ('core', 'chan'), pairs)  17.9 us
    all_to_all x1, blocking collectives, shards(): lax.all_to_all(jnp.broadcast_to(end_state[None], (chips, modes, width)),...  14.5 us
    pallas_call x2, Pallas kernels, on_device(): pl.pallas_call(kernel, out_shape=outs, in_specs=[smem] + [hbm] * copied +...  12.1 us
    ppermute x8, starting transfers between devices, chip_ring(): return lax.ppermute(block, ('y', 'x', 'core'), pairs)  12.1 us
    ppermute x8, waiting for transfers between devices, chip_ring(): return lax.ppermute(block, ('y', 'x', 'core'), pairs)  10.9 us
    dot_general x5, matrix products, product(): jnp.dot(values, weight, preferred_element_type=jnp.float32)  7.02 us
    ppermute x8, waiting for transfers between devices, swap_cores(): return lax.ppermute(block, 'core', [(0, 1), (1, 0)])  5.73 us
  transfers between devices with their start and end apart: 30, of which 19 were waited for; matrix products, arithmetic and copies ran while one was open for 5% of the time, Pallas kernels for 0%

profile of v2, /device:TPU:2, one launch (start us, length us, event | category | flops | bytes accessed | tf_op | source)
XLA Modules:
  0.0 144.8 jit_solution(8436591418774969089)
XLA Ops:
  6.5 1.1 constant_dynamic-slice_fusion.3
  7.7 1.4 collective-permute-done.10
  9.3 0.7 fusion.11
  10.2 1.6 %collective-permute-done = bf16[256,512]{1,0:T(8,128)(2,1)S(1)} collective-permute-done((bf16[256,512]{1,0:T(8,128)(2,1)}, bf16[256,512]{1,0:T(8,128)(2,1)S(1)}, u32[]{:S(2)}, u32[]{:S(2)}) %collective-permute-start) | collective-permute-done | bytes 262176 | tf_op jit(solution)/shard_map/ppermute | solution.py:14
  11.8 1.2 maximum_select_fusion
  13.0 3.4 %collective-permute-start.1 = (bf16[16,512]{1,0:T(8,128)(2,1)S(1)}, bf16[16,512]{1,0:T(8,128)(2,1)S(1)}, u32[]{:S(2)}, u32[]{:S(2)}) collective-permute-start(bf16[16,512]{1,0:T(8,128)(2,1)S(1)} %slice.64), channel_id=1, source_target_pairs={{0,16},{8,24},{16,32},{24,40},{32,48},{40,56},{48,64},{56,72},{64,... | collective-permute-start | bytes 49160 | tf_op jit(solution)/shard_map/ppermute | solution.py:254
  16.5 1.3 collective-permute-start.11
  17.7 0.9 collective-permute-done.1
  18.7 2.0 %collective-permute-start.2 = (bf16[528,512]{1,0:T(8,128)(2,1)S(1)}, bf16[528,512]{1,0:T(8,128)(2,1)S(1)}, u32[]{:S(2)}, u32[]{:S(2)}) collective-permute-start(bf16[528,512]{1,0:T(8,128)(2,1)S(1)} %pad_maximum_fusion.refs_0_), channel_id=1, source_target_pairs={{0,1},{1,2},{2,3},{3,4},{4,5},{5,6},{6,7},{7,0},{8,15},{9,8},{10,9... | collective-permute-start | bytes 1622024 | tf_op jit(solution)/shard_map/ppermute | solution.py:34
  20.7 2.2 %collective-permute-done.11 = bf16[256,512]{1,0:T(8,128)(2,1)S(1)} collective-permute-done((bf16[256,512]{1,0:T(8,128)(2,1)S(1)}, bf16[256,512]{1,0:T(8,128)(2,1)S(1)}, u32[]{:S(2)}, u32[]{:S(2)}) %collective-permute-start.11) | collective-permute-done | bytes 262176 | tf_op jit(solution)/shard_map/ppermute | solution.py:25
  22.9 1.3 collective-permute-start.12
  24.2 2.9 %collective-permute-done.13 = bf16[256,512]{1,0:T(8,128)(2,1)S(1)} collective-permute-done((bf16[256,512]{1,0:T(8,128)(2,1)S(1)}, bf16[256,512]{1,0:T(8,128)(2,1)S(1)}, u32[]{:S(2)}, u32[]{:S(2)}) %collective-permute-start.13) | collective-permute-done | bytes 262176 | tf_op jit(solution)/shard_map/ppermute | solution.py:25
  27.1 1.6 %collective-permute-start.14 = (bf16[128,512]{1,0:T(8,128)(2,1)S(1)}, bf16[128,512]{1,0:T(8,128)(2,1)S(1)}, u32[]{:S(2)}, u32[]{:S(2)}) collective-permute-start(bf16[128,512]{1,0:T(8,128)(2,1)S(1)} %slice.68), channel_id=1, source_target_pairs={{0,48},{8,200},{16,0},{24,216},{32,16},{40,232},{48,32},{56,248},{... | collective-permute-start | bytes 393224 | tf_op jit(solution)/shard_map/ppermute | solution.py:25
  28.7 3.2 %collective-permute-done.2.refs_1_ = bf16[528,512]{1,0:T(8,128)(2,1)S(1)} collective-permute-done((bf16[528,512]{1,0:T(8,128)(2,1)S(1)}, bf16[528,512]{1,0:T(8,128)(2,1)S(1)}, u32[]{:S(2)}, u32[]{:S(2)}) %collective-permute-start.2) | collective-permute-done | bytes 540704 | tf_op jit(solution)/shard_map/ppermute | solution.py:34
  32.4 3.0 %collective-permute-start.15 = (bf16[1024,512]{1,0:T(8,128)(2,1)S(1)}, bf16[1024,512]{1,0:T(8,128)(2,1)S(1)}, u32[]{:S(2)}, u32[]{:S(2)}) collective-permute-start(bf16[1024,512]{1,0:T(8,128)(2,1)S(1)} %constant_dynamic-update-slice_fusion.refs_9_), channel_id=1, source_target_pairs={{0,64},{8,24},{16,80},{24,40},{32,96},{40,56},{48,112},{56,8},{64,... | collective-permute-start | bytes 3145736 | tf_op jit(solution)/shard_map/ppermute | solution.py:25
  35.3 1.4 collective-permute-start.16
  36.7 6.0 %collective-permute-done.3.refs_2_ = bf16[528,512]{1,0:T(8,128)(2,1)} collective-permute-done((bf16[528,512]{1,0:T(8,128)(2,1)S(1)}, bf16[528,512]{1,0:T(8,128)(2,1)}, u32[]{:S(2)}, u32[]{:S(2)}) %collective-permute-start.3) | collective-permute-done | bytes 540704 | tf_op jit(solution)/shard_map/ppermute | solution.py:34
  42.6 1.5 %collective-permute-start.6 = (bf16[528,512]{1,0:T(8,128)(2,1)S(1)}, bf16[528,512]{1,0:T(8,128)(2,1)S(1)}, u32[]{:S(2)}, u32[]{:S(2)}) collective-permute-start(bf16[528,512]{1,0:T(8,128)(2,1)S(1)} %collective-permute-done.2.refs_1_), channel_id=1, source_target_pairs={{0,8},{8,0},{1,9},{9,1},{2,10},{10,2},{3,11},{11,3},{4,12},{12,4},... | collective-permute-start | bytes 1622024 | tf_op jit(solution)/shard_map/ppermute | solution.py:14
  44.2 9.2 %collective-permute-done.4.refs_3_ = bf16[528,512]{1,0:T(8,128)(2,1)S(1)} collective-permute-done((bf16[528,512]{1,0:T(8,128)(2,1)}, bf16[528,512]{1,0:T(8,128)(2,1)S(1)}, u32[]{:S(2)}, u32[]{:S(2)}) %collective-permute-start.4) | collective-permute-done | bytes 540704 | tf_op jit(solution)/shard_map/ppermute | solution.py:34
  53.6 0.4 collective-permute-start.8
  54.0 1.4 collective-permute-start.17
  55.4 2.2 %collective-permute-start.18 = (bf16[512,512]{1,0:T(8,128)(2,1)S(1)}, bf16[512,512]{1,0:T(8,128)(2,1)}, u32[]{:S(2)}, u32[]{:S(2)}) collective-permute-start(bf16[512,512]{1,0:T(8,128)(2,1)S(1)} %slice.70), channel_id=1, source_target_pairs={{0,192},{8,56},{16,208},{24,8},{32,224},{40,24},{48,240},{56,40},{... | collective-permute-start | bytes 1572872 | tf_op jit(solution)/shard_map/ppermute | solution.py:25
  57.7 3.6 %collective-permute-done.5.refs_4_ = bf16[528,256]{1,0:T(8,128)(2,1)} collective-permute-done((bf16[528,256]{1,0:T(8,128)(2,1)S(1)}, bf16[528,256]{1,0:T(8,128)(2,1)}, u32[]{:S(2)}, u32[]{:S(2)}) %collective-permute-start.5) | collective-permute-done | bytes 270368 | tf_op jit(solution)/shard_map/ppermute | solution.py:34
  61.6 5.5 %collective-permute-done.17.refs_12_ = bf16[512,512]{1,0:T(8,128)(2,1)} collective-permute-done((bf16[512,512]{1,0:T(8,128)(2,1)S(1)}, bf16[512,512]{1,0:T(8,128)(2,1)}, u32[]{:S(2)}, u32[]{:S(2)}) %collective-permute-start.17) | collective-permute-done | bytes 524320 | tf_op jit(solution)/shard_map/ppermute | solution.py:25
  67.2 9.6 %shard_map.64 = (f32[512,256]{1,0:T(8,128)S(1)}, f32[2,512,128]{2,1,0:T(8,128)S(1)}, f32[16,8,256]{2,1,0:T(8,128)S(1)}, f32[16,256]{1,0:T(8,128)S(1)}) custom-call(s32[5]{0:T(128)S(1)} %stack.23.place, bf16[528,512]{1,0:T(8,128)(2,1)} %copy-done.1, bf16[528,512]{1,0:T(8,128)(2,1)} %copy-done.8, bf16[528,512]{1,0:T(8,128)(2,1)} %collective-permute-done.3.refs_2_, ...), custom_call_target="tpu_custom_call" | custom-call | flops 3221225472 | bytes 8053063 | tf_op jit(solution)/shard_map/pallas_call | solution.py:218
  76.8 14.5 %all_to_all.5.states = f32[16,16,256]{2,1,0:T(8,128)S(1)} all-to-all(f32[16,16,256]{2,1,0:T(8,128)S(1)} %broadcast_in_dim.2), channel_id=1, replica_groups=mesh['y'=4,'x'=4,'core'=2,'chan'=8] {'y','x'}, dimensions={0} | all-to-all | bytes 524288 | tf_op jit(solution)/shard_map/all_to_all | solution.py:299
  91.4 2.5 %shard_map.65 = bf16[512,256]{1,0:T(8,128)(2,1)S(1)} custom-call(s32[5]{0:T(128)S(1)} %stack.23.place, f32[2,512,128]{2,1,0:T(8,128)S(1)} %get-tuple-element.17.signal, f32[512,256]{1,0:T(8,128)S(1)} %get-tuple-element.18.query, f32[16,8,256]{2,1,0:T(8,128)S(1)} %get-tuple-element.19.block_ends, f32[16,16,256]{2,1,0:T(8,128)S(1)} %all_to_all.5.states, ...), custom_call_target="tpu_custom_call" | custom-call | flops 8388608 | bytes 20971 | tf_op jit(solution)/shard_map/pallas_call | solution.py:218
  93.9 2.4 %collective-permute-start.19 = (bf16[512,256]{1,0:T(8,128)(2,1)S(1)}, bf16[512,256]{1,0:T(8,128)(2,1)S(1)}, u32[]{:S(2)}, u32[]{:S(2)}) collective-permute-start(bf16[512,256]{1,0:T(8,128)(2,1)S(1)} %shard_map.65), channel_id=1, source_target_pairs={{0,8},{8,0},{1,9},{9,1},{2,10},{10,2},{3,11},{11,3},{4,12},{12,4},... | collective-permute-start | bytes 786440 | tf_op jit(solution)/shard_map/ppermute | solution.py:14
  96.3 1.2 collective-permute-done.19
  97.6 1.3 convolution_convert_fusion.3
  98.9 1.5 %convolution_convert_fusion = bf16[512,512]{1,0:T(8,128)(2,1)S(1)} fusion(bf16[512,512]{1,0:T(8,128)(2,1)S(1)} %maximum_select_fusion.1, bf16[512,4096]{1,0:T(8,128)(2,1)} %param.11, s32[]{:T(128)S(6)} %select_n.101), kind=kOutput, calls=%fused_computation | convolution fusion | flops 268697600 | bytes 1572868 | tf_op jit(solution)/shard_map/dot_general | solution.py:323
  100.4 6.5 %collective-permute-start.24 = (bf16[272,256]{1,0:T(8,128)(2,1)S(1)}, bf16[272,256]{1,0:T(8,128)(2,1)S(1)}, u32[]{:S(2)}, u32[]{:S(2)}) collective-permute-start(bf16[272,256]{1,0:T(8,128)(2,1)S(1)} %slice.79), channel_id=1, source_target_pairs={{0,1},{1,2},{2,3},{3,4},{4,5},{5,6},{6,7},{7,0},{8,15},{9,8},{10,9... | collective-permute-start | bytes 417800 | tf_op jit(solution)/shard_map/ppermute | solution.py:34
  107.0 1.3 convolution_convert_fusion.4
  108.4 3.4 %collective-permute-start.21 = (bf16[240,512]{1,0:T(8,128)(2,1)S(1)}, bf16[240,512]{1,0:T(8,128)(2,1)S(1)}, u32[]{:S(2)}, u32[]{:S(2)}) collective-permute-start(bf16[240,512]{1,0:T(8,128)(2,1)S(1)} %slice_add_fusion.3), channel_id=1, source_target_pairs={{0,1},{1,2},{2,3},{3,4},{4,5},{5,6},{6,7},{7,0},{8,15},{9,8},{10,9... | collective-permute-start | bytes 737288 | tf_op jit(solution)/shard_map/ppermute | solution.py:34
  111.9 1.1 collective-permute-start.25
  113.1 1.5 %convolution_convert_fusion.1 = bf16[512,512]{1,0:T(8,128)(2,1)S(1)} fusion(bf16[512,512]{1,0:T(8,128)(2,1)S(1)} %maximum_select_fusion.1, bf16[512,4096]{1,0:T(8,128)(2,1)} %param.11, s32[]{:T(128)S(6)} %select_n.99), kind=kOutput, calls=%fused_computation.1 | convolution fusion | flops 268697600 | bytes 1572868 | tf_op jit(solution)/shard_map/dot_general | solution.py:323
  114.6 1.3 collective-permute-done.21
  115.9 2.2 %collective-permute-start.22 = (bf16[240,512]{1,0:T(8,128)(2,1)S(1)}, bf16[240,512]{1,0:T(8,128)(2,1)S(1)}, u32[]{:S(2)}, u32[]{:S(2)}) collective-permute-start(bf16[240,512]{1,0:T(8,128)(2,1)S(1)} %slice_add_fusion.4), channel_id=1, source_target_pairs={{0,1},{1,2},{2,3},{3,4},{4,5},{5,6},{6,7},{7,0},{8,15},{9,8},{10,9... | collective-permute-start | bytes 737288 | tf_op jit(solution)/shard_map/ppermute | solution.py:34
  118.1 1.6 %collective-permute-done.25 = bf16[272,512]{1,0:T(8,128)(2,1)S(1)} collective-permute-done((bf16[272,512]{1,0:T(8,128)(2,1)S(1)}, bf16[272,512]{1,0:T(8,128)(2,1)S(1)}, u32[]{:S(2)}, u32[]{:S(2)}) %collective-permute-start.25) | collective-permute-done | bytes 278560 | tf_op jit(solution)/shard_map/ppermute | solution.py:34
  119.8 1.3 collective-permute-start.26
  121.1 1.5 %convolution_convert_fusion.2 = bf16[512,512]{1,0:T(8,128)(2,1)S(1)} fusion(bf16[512,512]{1,0:T(8,128)(2,1)S(1)} %maximum_select_fusion.1, bf16[512,4096]{1,0:T(8,128)(2,1)} %param.11, s32[]{:T(128)S(6)} %select_n.97), kind=kOutput, calls=%fused_computation.2 | convolution fusion | flops 268697600 | bytes 1572868 | tf_op jit(solution)/shard_map/dot_general | solution.py:323
  122.6 0.8 collective-permute-done.22
  123.4 1.0 collective-permute-start.23
  124.4 3.2 %collective-permute-done.26 = bf16[272,512]{1,0:T(8,128)(2,1)S(1)} collective-permute-done((bf16[272,512]{1,0:T(8,128)(2,1)S(1)}, bf16[272,512]{1,0:T(8,128)(2,1)S(1)}, u32[]{:S(2)}, u32[]{:S(2)}) %collective-permute-start.26) | collective-permute-done | bytes 278560 | tf_op jit(solution)/shard_map/ppermute | solution.py:34
  127.8 3.1 %collective-permute-done.23 = bf16[240,512]{1,0:T(8,128)(2,1)S(1)} collective-permute-done((bf16[240,512]{1,0:T(8,128)(2,1)S(1)}, bf16[240,512]{1,0:T(8,128)(2,1)S(1)}, u32[]{:S(2)}, u32[]{:S(2)}) %collective-permute-start.23) | collective-permute-done | bytes 245792 | tf_op jit(solution)/shard_map/ppermute | solution.py:34
  130.9 4.6 %collective-permute-done.27 = bf16[272,512]{1,0:T(8,128)(2,1)S(1)} collective-permute-done((bf16[272,512]{1,0:T(8,128)(2,1)S(1)}, bf16[272,512]{1,0:T(8,128)(2,1)S(1)}, u32[]{:S(2)}, u32[]{:S(2)}) %collective-permute-start.27) | collective-permute-done | bytes 278560 | tf_op jit(solution)/shard_map/ppermute | solution.py:34
  135.7 1.5 %collective-permute-done.28 = bf16[256,512]{1,0:T(8,128)(2,1)S(1)} collective-permute-done((bf16[256,512]{1,0:T(8,128)(2,1)S(1)}, bf16[256,512]{1,0:T(8,128)(2,1)S(1)}, u32[]{:S(2)}, u32[]{:S(2)}) %collective-permute-start.28) | collective-permute-done | bytes 262176 | tf_op jit(solution)/shard_map/ppermute | solution.py:14
  137.2 0.8 add_convert_fusion
  (77 shorter events, 2.3 us)
Async XLA Ops:
  6.5 55.0 %copy-start = (f32[3,3,512]{2,1,0:T(4,128)S(1)}, f32[3,3,512]{2,1,0:T(4,128)}, u32[]{:S(2)}) copy-start(f32[3,3,512]{2,1,0:T(4,128)} %param.8) | copy-start | bytes 55300
  6.5 60.6 %all-gather.3.cloned.1.call-start = ((), (), s32[]{:S(2)}) async-start(), calls=%async_computation.1 | async-start | bytes 2228224 | tf_op jit(solution)/shard_map/all_gather | solution.py:264
  7.6 1.5 %collective-permute-start.10 = (bf16[3,128,256]{2,1,0:T(8,128)(2,1)S(1)}, bf16[3,128,256]{2,1,0:T(8,128)(2,1)S(1)}, u32[]{:S(2)}, u32[]{:S(2)}) collective-permute-start(bf16[3,128,256]{2,1,0:T(8,128)(2,1)S(1)} %get-tuple-element.31), channel_id=1, source_target_pairs={{0,8},{8,0},{1,9},{9,1},{2,10},{10,2},{3,11},{11,3},{4,12},{12,4},... | collective-permute-start | bytes 589832 | tf_op jit(solution)/shard_map/ppermute | solution.py:14
  10.0 51.6 %copy-start.6 = (f32[16,512]{1,0:T(8,128)S(1)}, f32[16,512]{1,0:T(8,128)}, u32[]{:S(2)}) copy-start(f32[16,512]{1,0:T(8,128)} %param.9) | copy-start | bytes 98308
  10.0 51.6 %copy-start.7 = (f32[16,512]{1,0:T(8,128)S(1)}, f32[16,512]{1,0:T(8,128)}, u32[]{:S(2)}) copy-start(f32[16,512]{1,0:T(8,128)} %param.10) | copy-start | bytes 98308
  10.0 1.8 %collective-permute-start = (bf16[256,512]{1,0:T(8,128)(2,1)}, bf16[256,512]{1,0:T(8,128)(2,1)S(1)}, u32[]{:S(2)}, u32[]{:S(2)}) collective-permute-start(bf16[256,512]{1,0:T(8,128)(2,1)} %param.6), channel_id=1, source_target_pairs={{0,8},{8,0},{1,9},{9,1},{2,10},{10,2},{3,11},{11,3},{4,12},{12,4},... | collective-permute-start | bytes 786440 | tf_op jit(solution)/shard_map/ppermute | solution.py:14
  13.0 5.6 %collective-permute-start.1 = (bf16[16,512]{1,0:T(8,128)(2,1)S(1)}, bf16[16,512]{1,0:T(8,128)(2,1)S(1)}, u32[]{:S(2)}, u32[]{:S(2)}) collective-permute-start(bf16[16,512]{1,0:T(8,128)(2,1)S(1)} %slice.64), channel_id=1, source_target_pairs={{0,16},{8,24},{16,32},{24,40},{32,48},{40,56},{48,64},{56,72},{64,... | collective-permute-start | bytes 49160 | tf_op jit(solution)/shard_map/ppermute | solution.py:254
  16.5 6.4 %collective-permute-start.11 = (bf16[256,512]{1,0:T(8,128)(2,1)S(1)}, bf16[256,512]{1,0:T(8,128)(2,1)S(1)}, u32[]{:S(2)}, u32[]{:S(2)}) collective-permute-start(bf16[256,512]{1,0:T(8,128)(2,1)S(1)} %pad_maximum_fusion.1), channel_id=1, source_target_pairs={{0,16},{8,72},{16,32},{24,88},{32,48},{40,104},{48,0},{56,120},{64... | collective-permute-start | bytes 786440 | tf_op jit(solution)/shard_map/ppermute | solution.py:25
  18.7 48.4 %copy-start.1 = (bf16[528,512]{1,0:T(8,128)(2,1)}, bf16[528,512]{1,0:T(8,128)(2,1)S(1)}, u32[]{:S(2)}) copy-start(bf16[528,512]{1,0:T(8,128)(2,1)S(1)} %pad_maximum_fusion.refs_0_) | copy-start | bytes 1622020
  18.7 13.3 %collective-permute-start.2 = (bf16[528,512]{1,0:T(8,128)(2,1)S(1)}, bf16[528,512]{1,0:T(8,128)(2,1)S(1)}, u32[]{:S(2)}, u32[]{:S(2)}) collective-permute-start(bf16[528,512]{1,0:T(8,128)(2,1)S(1)} %pad_maximum_fusion.refs_0_), channel_id=1, source_target_pairs={{0,1},{1,2},{2,3},{3,4},{4,5},{5,6},{6,7},{7,0},{8,15},{9,8},{10,9... | collective-permute-start | bytes 1622024 | tf_op jit(solution)/shard_map/ppermute | solution.py:34
  20.7 6.4 %collective-permute-start.13 = (bf16[256,512]{1,0:T(8,128)(2,1)S(1)}, bf16[256,512]{1,0:T(8,128)(2,1)S(1)}, u32[]{:S(2)}, u32[]{:S(2)}) collective-permute-start(bf16[256,512]{1,0:T(8,128)(2,1)S(1)} %pad_maximum_fusion.1), channel_id=1, source_target_pairs={{0,48},{8,200},{16,0},{24,216},{32,16},{40,232},{48,32},{56,248},{... | collective-permute-start | bytes 786440 | tf_op jit(solution)/shard_map/ppermute | solution.py:25
  22.9 5.8 %collective-permute-start.12 = (bf16[128,512]{1,0:T(8,128)(2,1)S(1)}, bf16[128,512]{1,0:T(8,128)(2,1)S(1)}, u32[]{:S(2)}, u32[]{:S(2)}) collective-permute-start(bf16[128,512]{1,0:T(8,128)(2,1)S(1)} %slice.67), channel_id=1, source_target_pairs={{0,16},{8,72},{16,32},{24,88},{32,48},{40,104},{48,0},{56,120},{64... | collective-permute-start | bytes 393224 | tf_op jit(solution)/shard_map/ppermute | solution.py:25
  27.1 5.2 %collective-permute-start.14 = (bf16[128,512]{1,0:T(8,128)(2,1)S(1)}, bf16[128,512]{1,0:T(8,128)(2,1)S(1)}, u32[]{:S(2)}, u32[]{:S(2)}) collective-permute-start(bf16[128,512]{1,0:T(8,128)(2,1)S(1)} %slice.68), channel_id=1, source_target_pairs={{0,48},{8,200},{16,0},{24,216},{32,16},{40,232},{48,32},{56,248},{... | collective-permute-start | bytes 393224 | tf_op jit(solution)/shard_map/ppermute | solution.py:25
  32.0 29.3 %copy-start.8 = (bf16[528,512]{1,0:T(8,128)(2,1)}, bf16[528,512]{1,0:T(8,128)(2,1)S(1)}, u32[]{:S(2)}) copy-start(bf16[528,512]{1,0:T(8,128)(2,1)S(1)} %collective-permute-done.2.refs_1_) | copy-start | bytes 1622020
  32.0 10.7 %collective-permute-start.3 = (bf16[528,512]{1,0:T(8,128)(2,1)S(1)}, bf16[528,512]{1,0:T(8,128)(2,1)}, u32[]{:S(2)}, u32[]{:S(2)}) collective-permute-start(bf16[528,512]{1,0:T(8,128)(2,1)S(1)} %collective-permute-done.2.refs_1_), channel_id=1, source_target_pairs={{0,1},{1,2},{2,3},{3,4},{4,5},{5,6},{6,7},{7,0},{8,15},{9,8},{10,9... | collective-permute-start | bytes 1622024 | tf_op jit(solution)/shard_map/ppermute | solution.py:34
  32.3 29.0 %copy-start.5 = (bf16[1024,512]{1,0:T(8,128)(2,1)}, bf16[1024,512]{1,0:T(8,128)(2,1)S(1)}, u32[]{:S(2)}) copy-start(bf16[1024,512]{1,0:T(8,128)(2,1)S(1)} %constant_dynamic-update-slice_fusion.refs_9_) | copy-start | bytes 3145732
  32.4 21.2 %collective-permute-start.15 = (bf16[1024,512]{1,0:T(8,128)(2,1)S(1)}, bf16[1024,512]{1,0:T(8,128)(2,1)S(1)}, u32[]{:S(2)}, u32[]{:S(2)}) collective-permute-start(bf16[1024,512]{1,0:T(8,128)(2,1)S(1)} %constant_dynamic-update-slice_fusion.refs_9_), channel_id=1, source_target_pairs={{0,64},{8,24},{16,80},{24,40},{32,96},{40,56},{48,112},{56,8},{64,... | collective-permute-start | bytes 3145736 | tf_op jit(solution)/shard_map/ppermute | solution.py:25
  35.3 18.6 %collective-permute-start.16 = (bf16[1024,512]{1,0:T(8,128)(2,1)S(1)}, bf16[1024,512]{1,0:T(8,128)(2,1)S(1)}, u32[]{:S(2)}, u32[]{:S(2)}) collective-permute-start(bf16[1024,512]{1,0:T(8,128)(2,1)S(1)} %constant_dynamic-update-slice_fusion.refs_9_), channel_id=1, source_target_pairs={{0,192},{8,56},{16,208},{24,8},{32,224},{40,24},{48,240},{56,40},{... | collective-permute-start | bytes 3145736 | tf_op jit(solution)/shard_map/ppermute | solution.py:25
  42.6 10.8 %collective-permute-start.4 = (bf16[528,512]{1,0:T(8,128)(2,1)}, bf16[528,512]{1,0:T(8,128)(2,1)S(1)}, u32[]{:S(2)}, u32[]{:S(2)}) collective-permute-start(bf16[528,512]{1,0:T(8,128)(2,1)} %collective-permute-done.3.refs_2_), channel_id=1, source_target_pairs={{0,1},{1,2},{2,3},{3,4},{4,5},{5,6},{6,7},{7,0},{8,15},{9,8},{10,9... | collective-permute-start | bytes 1622024 | tf_op jit(solution)/shard_map/ppermute | solution.py:34
  42.6 12.8 %collective-permute-start.6 = (bf16[528,512]{1,0:T(8,128)(2,1)S(1)}, bf16[528,512]{1,0:T(8,128)(2,1)S(1)}, u32[]{:S(2)}, u32[]{:S(2)}) collective-permute-start(bf16[528,512]{1,0:T(8,128)(2,1)S(1)} %collective-permute-done.2.refs_1_), channel_id=1, source_target_pairs={{0,8},{8,0},{1,9},{9,1},{2,10},{10,2},{3,11},{11,3},{4,12},{12,4},... | collective-permute-start | bytes 1622024 | tf_op jit(solution)/shard_map/ppermute | solution.py:14
  44.2 17.4 %collective-permute-start.7 = (bf16[528,512]{1,0:T(8,128)(2,1)}, bf16[528,512]{1,0:T(8,128)(2,1)}, u32[]{:S(2)}, u32[]{:S(2)}) collective-permute-start(bf16[528,512]{1,0:T(8,128)(2,1)} %collective-permute-done.3.refs_2_), channel_id=1, source_target_pairs={{0,8},{8,0},{1,9},{9,1},{2,10},{10,2},{3,11},{11,3},{4,12},{12,4},... | collective-permute-start | bytes 1622024 | tf_op jit(solution)/shard_map/ppermute | solution.py:14
  53.4 13.7 %copy-start.4 = (bf16[528,512]{1,0:T(8,128)(2,1)}, bf16[528,512]{1,0:T(8,128)(2,1)S(1)}, u32[]{:S(2)}) copy-start(bf16[528,512]{1,0:T(8,128)(2,1)S(1)} %collective-permute-done.4.refs_3_) | copy-start | bytes 1622020
  53.4 7.9 %collective-permute-start.5 = (bf16[528,256]{1,0:T(8,128)(2,1)S(1)}, bf16[528,256]{1,0:T(8,128)(2,1)}, u32[]{:S(2)}, u32[]{:S(2)}) collective-permute-start(bf16[528,256]{1,0:T(8,128)(2,1)S(1)} %constant_dynamic-slice_fusion.4), channel_id=1, source_target_pairs={{0,1},{1,2},{2,3},{3,4},{4,5},{5,6},{6,7},{7,0},{8,15},{9,8},{10,9... | collective-permute-start | bytes 811016 | tf_op jit(solution)/shard_map/ppermute | solution.py:34
  53.6 13.6 %copy-start.2 = (bf16[1024,512]{1,0:T(8,128)(2,1)}, bf16[1024,512]{1,0:T(8,128)(2,1)S(1)}, u32[]{:S(2)}) copy-start(bf16[1024,512]{1,0:T(8,128)(2,1)S(1)} %collective-permute-done.15.refs_10_) | copy-start | bytes 3145732
  53.6 13.5 %collective-permute-start.8 = (bf16[528,512]{1,0:T(8,128)(2,1)S(1)}, bf16[528,512]{1,0:T(8,128)(2,1)}, u32[]{:S(2)}, u32[]{:S(2)}) collective-permute-start(bf16[528,512]{1,0:T(8,128)(2,1)S(1)} %collective-permute-done.4.refs_3_), channel_id=1, source_target_pairs={{0,8},{8,0},{1,9},{9,1},{2,10},{10,2},{3,11},{11,3},{4,12},{12,4},... | collective-permute-start | bytes 1622024 | tf_op jit(solution)/shard_map/ppermute | solution.py:14
  54.0 7.3 %copy-start.3 = (bf16[1024,512]{1,0:T(8,128)(2,1)}, bf16[1024,512]{1,0:T(8,128)(2,1)S(1)}, u32[]{:S(2)}) copy-start(bf16[1024,512]{1,0:T(8,128)(2,1)S(1)} %collective-permute-done.16.refs_11_) | copy-start | bytes 3145732
  54.0 13.1 %collective-permute-start.17 = (bf16[512,512]{1,0:T(8,128)(2,1)S(1)}, bf16[512,512]{1,0:T(8,128)(2,1)}, u32[]{:S(2)}, u32[]{:S(2)}) collective-permute-start(bf16[512,512]{1,0:T(8,128)(2,1)S(1)} %slice.69), channel_id=1, source_target_pairs={{0,64},{8,24},{16,80},{24,40},{32,96},{40,56},{48,112},{56,8},{64,... | collective-permute-start | bytes 1572872 | tf_op jit(solution)/shard_map/ppermute | solution.py:25
  55.4 5.9 %copy-start.9 = (bf16[528,512]{1,0:T(8,128)(2,1)}, bf16[528,512]{1,0:T(8,128)(2,1)S(1)}, u32[]{:S(2)}) copy-start(bf16[528,512]{1,0:T(8,128)(2,1)S(1)} %collective-permute-done.6.refs_5_) | copy-start | bytes 1622020
  55.4 11.7 %collective-permute-start.18 = (bf16[512,512]{1,0:T(8,128)(2,1)S(1)}, bf16[512,512]{1,0:T(8,128)(2,1)}, u32[]{:S(2)}, u32[]{:S(2)}) collective-permute-start(bf16[512,512]{1,0:T(8,128)(2,1)S(1)} %slice.70), channel_id=1, source_target_pairs={{0,192},{8,56},{16,208},{24,8},{32,224},{40,24},{48,240},{56,40},{... | collective-permute-start | bytes 1572872 | tf_op jit(solution)/shard_map/ppermute | solution.py:25
  61.3 5.8 %collective-permute-start.9 = (bf16[528,256]{1,0:T(8,128)(2,1)}, bf16[528,256]{1,0:T(8,128)(2,1)}, u32[]{:S(2)}, u32[]{:S(2)}) collective-permute-start(bf16[528,256]{1,0:T(8,128)(2,1)} %collective-permute-done.5.refs_4_), channel_id=1, source_target_pairs={{0,8},{8,0},{1,9},{9,1},{2,10},{10,2},{3,11},{11,3},{4,12},{12,4},... | collective-permute-start | bytes 811016 | tf_op jit(solution)/shard_map/ppermute | solution.py:14
  93.9 3.6 %collective-permute-start.19 = (bf16[512,256]{1,0:T(8,128)(2,1)S(1)}, bf16[512,256]{1,0:T(8,128)(2,1)S(1)}, u32[]{:S(2)}, u32[]{:S(2)}) collective-permute-start(bf16[512,256]{1,0:T(8,128)(2,1)S(1)} %shard_map.65), channel_id=1, source_target_pairs={{0,8},{8,0},{1,9},{9,1},{2,10},{10,2},{3,11},{11,3},{4,12},{12,4},... | collective-permute-start | bytes 786440 | tf_op jit(solution)/shard_map/ppermute | solution.py:14
  98.9 9.5 %collective-permute-start.20 = (bf16[240,256]{1,0:T(8,128)(2,1)S(1)}, bf16[240,256]{1,0:T(8,128)(2,1)S(1)}, u32[]{:S(2)}, u32[]{:S(2)}) collective-permute-start(bf16[240,256]{1,0:T(8,128)(2,1)S(1)} %slice.75), channel_id=1, source_target_pairs={{0,1},{1,2},{2,3},{3,4},{4,5},{5,6},{6,7},{7,0},{8,15},{9,8},{10,9... | collective-permute-start | bytes 368648 | tf_op jit(solution)/shard_map/ppermute | solution.py:34
  100.4 11.4 %collective-permute-start.24 = (bf16[272,256]{1,0:T(8,128)(2,1)S(1)}, bf16[272,256]{1,0:T(8,128)(2,1)S(1)}, u32[]{:S(2)}, u32[]{:S(2)}) collective-permute-start(bf16[272,256]{1,0:T(8,128)(2,1)S(1)} %slice.79), channel_id=1, source_target_pairs={{0,1},{1,2},{2,3},{3,4},{4,5},{5,6},{6,7},{7,0},{8,15},{9,8},{10,9... | collective-permute-start | bytes 417800 | tf_op jit(solution)/shard_map/ppermute | solution.py:34
  108.4 7.5 %collective-permute-start.21 = (bf16[240,512]{1,0:T(8,128)(2,1)S(1)}, bf16[240,512]{1,0:T(8,128)(2,1)S(1)}, u32[]{:S(2)}, u32[]{:S(2)}) collective-permute-start(bf16[240,512]{1,0:T(8,128)(2,1)S(1)} %slice_add_fusion.3), channel_id=1, source_target_pairs={{0,1},{1,2},{2,3},{3,4},{4,5},{5,6},{6,7},{7,0},{8,15},{9,8},{10,9... | collective-permute-start | bytes 737288 | tf_op jit(solution)/shard_map/ppermute | solution.py:34
  111.9 7.8 %collective-permute-start.25 = (bf16[272,512]{1,0:T(8,128)(2,1)S(1)}, bf16[272,512]{1,0:T(8,128)(2,1)S(1)}, u32[]{:S(2)}, u32[]{:S(2)}) collective-permute-start(bf16[272,512]{1,0:T(8,128)(2,1)S(1)} %slice_add_fusion), channel_id=1, source_target_pairs={{0,1},{1,2},{2,3},{3,4},{4,5},{5,6},{6,7},{7,0},{8,15},{9,8},{10,9... | collective-permute-start | bytes 835592 | tf_op jit(solution)/shard_map/ppermute | solution.py:34
  115.9 7.5 %collective-permute-start.22 = (bf16[240,512]{1,0:T(8,128)(2,1)S(1)}, bf16[240,512]{1,0:T(8,128)(2,1)S(1)}, u32[]{:S(2)}, u32[]{:S(2)}) collective-permute-start(bf16[240,512]{1,0:T(8,128)(2,1)S(1)} %slice_add_fusion.4), channel_id=1, source_target_pairs={{0,1},{1,2},{2,3},{3,4},{4,5},{5,6},{6,7},{7,0},{8,15},{9,8},{10,9... | collective-permute-start | bytes 737288 | tf_op jit(solution)/shard_map/ppermute | solution.py:34
  119.8 7.8 %collective-permute-start.26 = (bf16[272,512]{1,0:T(8,128)(2,1)S(1)}, bf16[272,512]{1,0:T(8,128)(2,1)S(1)}, u32[]{:S(2)}, u32[]{:S(2)}) collective-permute-start(bf16[272,512]{1,0:T(8,128)(2,1)S(1)} %slice_add_fusion.1), channel_id=1, source_target_pairs={{0,1},{1,2},{2,3},{3,4},{4,5},{5,6},{6,7},{7,0},{8,15},{9,8},{10,9... | collective-permute-start | bytes 835592 | tf_op jit(solution)/shard_map/ppermute | solution.py:34
  123.4 7.5 %collective-permute-start.23 = (bf16[240,512]{1,0:T(8,128)(2,1)S(1)}, bf16[240,512]{1,0:T(8,128)(2,1)S(1)}, u32[]{:S(2)}, u32[]{:S(2)}) collective-permute-start(bf16[240,512]{1,0:T(8,128)(2,1)S(1)} %slice_add_fusion.5), channel_id=1, source_target_pairs={{0,1},{1,2},{2,3},{3,4},{4,5},{5,6},{6,7},{7,0},{8,15},{9,8},{10,9... | collective-permute-start | bytes 737288 | tf_op jit(solution)/shard_map/ppermute | solution.py:34
  127.7 7.8 %collective-permute-start.27 = (bf16[272,512]{1,0:T(8,128)(2,1)S(1)}, bf16[272,512]{1,0:T(8,128)(2,1)S(1)}, u32[]{:S(2)}, u32[]{:S(2)}) collective-permute-start(bf16[272,512]{1,0:T(8,128)(2,1)S(1)} %slice_add_fusion.2), channel_id=1, source_target_pairs={{0,1},{1,2},{2,3},{3,4},{4,5},{5,6},{6,7},{7,0},{8,15},{9,8},{10,9... | collective-permute-start | bytes 835592 | tf_op jit(solution)/shard_map/ppermute | solution.py:34
  135.6 1.6 %collective-permute-start.28 = (bf16[256,512]{1,0:T(8,128)(2,1)S(1)}, bf16[256,512]{1,0:T(8,128)(2,1)S(1)}, u32[]{:S(2)}, u32[]{:S(2)}) collective-permute-start(bf16[256,512]{1,0:T(8,128)(2,1)S(1)} %constant_dynamic-slice_fusion), channel_id=1, source_target_pairs={{0,8},{8,0},{1,9},{9,1},{2,10},{10,2},{3,11},{11,3},{4,12},{12,4},... | collective-permute-start | bytes 786440 | tf_op jit(solution)/shard_map/ppermute | solution.py:14
Sparse Core Ops, SparseCore 0:
  10.1 53.8 all-gather.2

commit v3 on v2

--- a/solution.py
+++ b/solution.py
@@ -34,27 +34,13 @@
     return lax.ppermute(block, ("core", "chan"), pairs)
 
 
-def weights_around(block, sides):
-    def ring(own, stage):
-        half = own.shape[0] // 2
-        before = chip_ring(own, sides, stage, 1)
-        behind = chip_ring(own, sides, stage, -1)
-        far = chip_ring(before[:half], sides, stage, 1), chip_ring(behind[half:], sides, stage, -1)
-        return before, behind, far
-
-    before, behind, far = ring(block, 0)
-    near = jnp.concatenate([block, before, *far, behind], axis=0)
-    before, behind, far = ring(near, 1)
-    return near, before, behind, *far
-
-
-def tokens_around(block, core):
-    blocks = [block]
-    for _ in range(3):
-        blocks.append(group_ring(blocks[-1]))
-    half = block.shape[1] // 2
-    blocks.append(group_ring(lax.dynamic_slice_in_dim(blocks[-1], core * half, half, axis=1)))
-    return blocks[1:]
+def ring(own, sides, stage):
+    return chip_ring(own, sides, stage, 1), chip_ring(own, sides, stage, -1)
+
+
+def far_side(before, behind, sides, stage):
+    half = before.shape[0] // 2
+    return chip_ring(before[:half], sides, stage, 1), chip_ring(behind[half:], sides, stage, -1)
 
 
 def tokens_in_order(place, groups, blocks, gathered, semaphores):
@@ -89,14 +75,16 @@
 def weights_in_order(place, sides, blocks, gathered, semaphores):
     ny, nx = sides
     core, y, x = place[1], place[2], place[3]
-    near, before, behind, far_top, far_bottom = blocks
+    near, before, behind, *far = blocks
     rows = near.shape[0] // 4
     order = (0, -1, -2, 1)
-    pieces = [(near, i, first, 0) for i, first in enumerate(order)]
-    pieces += [(before, i, first, -1) for i, first in enumerate(order)]
-    pieces += [(behind, i, first, 1) for i, first in enumerate(order)]
-    pieces += [(far_top, i, order[i], -2) for i in range(2)]
-    pieces += [(far_bottom, i, order[i + 2], -2) for i in range(2)]
+    pieces = []
+    for block, second in ((near, 0), (before, -1), (behind, 1)):
+        pieces += [(block, i, first, second) for i, first in enumerate(order)]
+    if len(far) == 1:
+        pieces += [(far[0], i, first, -2) for i, first in enumerate(order)]
+    else:
+        pieces += [(far[i // 2], i % 2, first, -2) for i, first in enumerate(order)]
     copies = []
     for block, i, first, second in pieces:
         dx = jnp.where(core == 0, first, second)
@@ -115,16 +103,26 @@
     return copies
 
 
+def near_kernel(own, before, far_top, far_bottom, behind, key_value, query):
+    split = key_value.shape[1]
+    row = 0
+    for block in (own, before, far_top, far_bottom, behind):
+        rows = block.shape[0]
+        key_value[pl.ds(row, rows), :] = block[:, pl.ds(0, split)]
+        query[pl.ds(row, rows), :] = block[:, pl.ds(split, query.shape[1])]
+        row += rows
+
+
 def take_tokens(refs):
     return refs[0], refs[1:5], refs[5:9]
 
 
-def project(tokens, weight, columns, projected):
+def project(tokens, weight, projected):
     rows = tokens.shape[0] - HALO
-    total = jnp.dot(tokens[...], weight[:, columns], preferred_element_type=jnp.float32)
+    total = jnp.dot(tokens[...], weight[...], preferred_element_type=jnp.float32)
     total = total.astype(jnp.bfloat16).astype(jnp.float32)
-    projected[pl.ds(0, HALO), columns] = total[rows:]
-    projected[pl.ds(HALO, rows), columns] = total[:rows]
+    projected[pl.ds(0, HALO), :] = total[rows:]
+    projected[pl.ds(HALO, rows), :] = total[:rows]
 
 
 def filtered(projected, taps, group, channels, columns):
@@ -135,23 +133,25 @@
     )
 
 
-def project_kernel(groups, sides, place, *refs):
-    blocks, weights, query_weight = take_tokens(refs[:9]), refs[9:14], refs[14]
-    taps, rates, query, signal, block_ends, end_state, tokens, weight, projected, *semaphores = refs[15:]
-    width = query.shape[1]
-    early = tokens_in_order(place, groups, blocks, tokens, semaphores[0])
-    copy = pltpu.make_async_copy(
-        query_weight, weight.at[:, pl.ds(2 * width, width)], semaphores[1].at[0]
-    )
-    copy.start()
-    late = weights_in_order(place, sides, weights, weight.at[:, pl.ds(0, 2 * width)], semaphores[2])
-    for each in early + [copy]:
-        each.wait()
-    project(tokens, weight, pl.ds(2 * width, width), projected)
-    query[...] = filtered(projected, taps, 0, slice(None), pl.ds(2 * width, width))
-    for each in late:
-        each.wait()
-    project(tokens, weight, pl.ds(0, 2 * width), projected)
+def query_kernel(groups, sides, place, *refs):
+    blocks, weights = take_tokens(refs[:9]), refs[9:13]
+    taps, query, tokens, weight, projected, *semaphores = refs[13:]
+    copies = tokens_in_order(place, groups, blocks, tokens, semaphores[0])
+    copies += weights_in_order(place, sides, weights, weight, semaphores[1])
+    for copy in copies:
+        copy.wait()
+    project(tokens, weight, projected)
+    query[...] = filtered(projected, taps, 0, slice(None), slice(None))
+
+
+def key_value_kernel(groups, sides, place, *refs):
+    blocks, weights = take_tokens(refs[:9]), refs[9:14]
+    taps, rates, signal, block_ends, end_state, tokens, weight, projected, *semaphores = refs[14:]
+    copies = tokens_in_order(place, groups, blocks, tokens, semaphores[0])
+    copies += weights_in_order(place, sides, weights, weight, semaphores[1])
+    for copy in copies:
+        copy.wait()
+    project(tokens, weight, projected)
     modes, blocks, width = block_ends.shape
     steps = signal.shape[1] // blocks
     for part in range(width // 128):
@@ -175,7 +175,8 @@
     state = block_ends[:, 0, :]
     for b in range(1, blocks):
         state = block_decay * state + block_ends[:, b, :]
-    end_state[...] = state
+    for chip in range(end_state.shape[0]):
+        end_state[chip] = state
 
 
 def scan_kernel(place, signal, query, block_ends, states, rates, amplitude, gated, block_starts, result):
@@ -255,15 +256,41 @@
         block[-HALO:], ("y", "x", "core"), [(i, i + 2) for i in range(2 * chips - 2)]
     )
     block = jnp.concatenate([block, earlier], axis=0)
-    mine = tokens_around(block, core)
-    gathered = [block, *mine, *[swap_cores(each) for each in mine]]
-
     kept = own_columns(input_weight, core)
-    got = swap_cores(own_columns(input_weight, 1 - core))
-    both = by_core(kept, got, 1)
-    query_weight = lax.all_gather(both[0].reshape(-1, width), ("y", "x"), axis=0, tiled=True)
-    key_value, _ = lax.optimization_barrier((jnp.concatenate([both[1], both[2]], axis=1), other))
-    weights = weights_around(key_value, sides)
+    given, _ = lax.optimization_barrier((own_columns(input_weight, 1 - core), other))
+    both = by_core(kept, swap_cores(given), 1)
+    own = jnp.concatenate([both[1], both[2], both[0]], axis=1)
+    before, behind = first_ring = ring(own, sides, 0)
+    vmem = pl.BlockSpec(memory_space=pltpu.VMEM)
+    near, near_query = pl.pallas_call(
+        near_kernel,
+        out_shape=(
+            jax.ShapeDtypeStruct((4 * own.shape[0], 2 * width), bf16),
+            jax.ShapeDtypeStruct((4 * own.shape[0], width), bf16),
+        ),
+        in_specs=[vmem] * 5,
+        out_specs=(vmem, vmem),
+        compiler_params=pltpu.CompilerParams(vmem_limit_bytes=8 * 1024 * 1024),
+        cost_estimate=pl.CostEstimate(flops=0, bytes_accessed=8 * own.size * 2, transcendentals=0),
+    )(own, before, *far_side(before, behind, sides, 0), behind)
+    before, behind = ring(near, sides, 1)
+
+    mine = [group_ring(block)]
+    second, *_ = lax.optimization_barrier((mine[0], *first_ring))
+    mine.append(group_ring(second))
+    mine.append(group_ring(mine[1]))
+    last = lax.dynamic_slice_in_dim(mine[-1], core * (depth // 2), depth // 2, axis=1)
+    shared = [swap_cores(each) for each in mine[:2]]
+    last, *shared = lax.optimization_barrier((last, *shared))
+    mine.append(group_ring(last))
+    far = far_side(before, behind, sides, 1)
+    query_ring = ring(near_query, sides, 1)
+    *rest, top, bottom, before_query, behind_query = lax.optimization_barrier(
+        (*mine[2:], *far, *query_ring)
+    )
+    weights = near, before, behind, top, bottom
+    query_weights = near_query, before_query, behind_query, chip_ring(near_query, sides, 1, 2)
+    gathered = [block, *mine, *shared, *[swap_cores(each) for each in rest]]
 
     rates_all = decay_rate / float(sequence)
     rates = own_columns(rates_all, core)
@@ -275,29 +302,40 @@
     features = depth * groups
     dma = pltpu.SemaphoreType.DMA
 
-    query, signal, block_ends, end_state = on_device(
-        functools.partial(project_kernel, groups, sides),
+    signal, block_ends, end_state = on_device(
+        functools.partial(key_value_kernel, groups, sides),
         (
-            jax.ShapeDtypeStruct((positions, width), f32),
             jax.ShapeDtypeStruct(lanes, f32),
             jax.ShapeDtypeStruct((modes, blocks, width), f32),
-            jax.ShapeDtypeStruct((modes, width), f32),
+            jax.ShapeDtypeStruct((chips, modes, width), f32),
         ),
         [
             pltpu.VMEM((positions + HALO, features), bf16),
-            pltpu.VMEM((features, 3 * width), bf16),
-            pltpu.VMEM((positions + HALO, 3 * width), f32),
+            pltpu.VMEM((features, 2 * width), bf16),
+            pltpu.VMEM((positions + HALO, 2 * width), f32),
             dma((9,)),
-            dma((1,)),
             dma((16,)),
         ],
-        6 * positions * features * width,
-        24,
-        15,
-        place, *gathered, *weights, query_weight, taps, rates,
-    )
-    states = lax.all_to_all(
-        jnp.broadcast_to(end_state[None], (chips, modes, width)), ("y", "x"), 0, 0, tiled=True
+        4 * positions * features * width,
+        20,
+        14,
+        place, *gathered, *weights, taps, rates,
+    )
+    states = lax.all_to_all(end_state, ("y", "x"), 0, 0, tiled=True)
+    query = on_device(
+        functools.partial(query_kernel, groups, sides),
+        jax.ShapeDtypeStruct((positions, width), f32),
+        [
+            pltpu.VMEM((positions + HALO, features), bf16),
+            pltpu.VMEM((features, width), bf16),
+            pltpu.VMEM((positions + HALO, width), f32),
+            dma((9,)),
+            dma((16,)),
+        ],
+        2 * positions * features * width,
+        16,
+        13,
+        place, *gathered, *query_weights, taps,
     )
     gated = on_device(
         scan_kernel,
@@ -308,44 +346,38 @@
         0,
         place, signal, query, block_ends, states, rates, amplitude,
     )
-    gated = by_core(gated, swap_cores(gated), 1)
-    return reduced(gated, out_weight, core, z, groups)
-
-
-def reduced(gated, out_weight, core, z, groups):
-    rows = gated.shape[0] // 2
+    given = swap_cores(lax.dynamic_slice_in_dim(gated, (1 - core) * rows, rows, axis=0))
+    gated = by_core(lax.dynamic_slice_in_dim(gated, core * rows, rows, axis=0), given, 1)
+    return reduced(gated, out_weight, z, groups)
+
+
+def reduced(gated, out_weight, z, groups):
     width = out_weight.shape[1] // groups
-    ahead = 1 - 2 * core
-
-    def product(values, distance, first=0, columns=width):
-        start = (z + ahead * distance) % groups * width + first
-        weight = lax.dynamic_slice_in_dim(out_weight, start, columns, axis=1)
-        return jnp.dot(values, weight, preferred_element_type=jnp.float32).astype(jnp.bfloat16)
+
+    def send(block, direction):
+        return lax.ppermute(block, "chan", [(i, (i + direction) % groups) for i in range(groups)])
+
+    def product(distance):
+        start = (z + distance) % groups * width
+        weight = lax.dynamic_slice_in_dim(out_weight, start, width, axis=1)
+        total = jnp.dot(gated, weight, preferred_element_type=jnp.float32).astype(jnp.bfloat16)
+        return lax.optimization_barrier(total)
 
     half = width // 2
-    part = product(gated, 4, core * half, half)
-    cut = rows - 16
-    spans = slice(0, cut), slice(cut, 2 * rows)
-    streams = [part[span] for span in spans]
-    own = product(lax.dynamic_slice_in_dim(gated, core * rows, rows, axis=0), 0)
+    part = product(4)
+    ahead, behind = part[:, :half], part[:, half:]
+    own = product(0)
     for distance in (3, 2, 1):
-        part = product(gated, distance)
-        for number, span in enumerate(spans):
-            arrived = group_ring(streams[number])
-            if distance == 3:
-                nothing = jnp.zeros_like(arrived)
-                arrived = jnp.where(
-                    core == 0,
-                    jnp.concatenate([arrived, nothing], axis=1),
-                    jnp.concatenate([nothing, arrived], axis=1),
-                )
-            before = own if number == 0 else streams[0]
-            arrived, _ = lax.optimization_barrier((arrived, before))
-            streams[number] = part[span] + arrived
-    total = jnp.concatenate([group_ring(stream) for stream in streams], axis=0)
-    kept = lax.dynamic_slice_in_dim(total, core * rows, rows, axis=0)
-    got = swap_cores(lax.dynamic_slice_in_dim(total, (1 - core) * rows, rows, axis=0))
-    total = own.astype(jnp.float32) + kept.astype(jnp.float32) + got.astype(jnp.float32)
+        ahead_part, behind_part = product(distance), product(-distance)
+        ahead, behind = send(ahead, 1), send(behind, -1)
+        if distance == 3:
+            ahead = jnp.concatenate([ahead, jnp.zeros_like(ahead)], axis=1)
+            behind = jnp.concatenate([jnp.zeros_like(behind), behind], axis=1)
+        ahead = ahead_part + ahead
+        behind, _ = lax.optimization_barrier((behind, ahead))
+        behind = behind_part + behind
+    ahead, behind = send(ahead, 1), send(behind, -1)
+    total = own.astype(jnp.float32) + ahead.astype(jnp.float32) + behind.astype(jnp.float32)
     return total.astype(jnp.bfloat16)
 
 

time: 147 us -> 128 us (0.87)
  blocking collectives: 14.5 us -> 0 us
  between operations: 13.8 us -> 0.55 us
  starting transfers between devices: 38.2 us -> 49.6 us
  waiting for transfers between devices: 54.4 us -> 45.1 us
  Pallas kernels: 12.1 us -> 16.1 us
  matrix products: 7.02 us -> 10.8 us
    ppermute x0 -> x8, starting transfers between devices: none -> 17.7 us  [send(): lax.ppermute(block, 'chan', [(i, (i + direction) % groups) for i in range...]
    ppermute x12 -> x4, waiting for transfers between devices: 36.8 us -> 19.3 us  [group_ring(): return lax.ppermute(block, ('core', 'chan'), pairs)]
    ppermute x12 -> x4, starting transfers between devices: 17.9 us -> 2.47 us  [group_ring(): return lax.ppermute(block, ('core', 'chan'), pairs)]
    all_to_all x1 -> x0, blocking collectives: 14.5 us -> none  [shards(): lax.all_to_all(jnp.broadcast_to(end_state[None], (chips, modes, width)),...]
    ppermute x0 -> x8, waiting for transfers between devices: none -> 11.3 us  [send(): lax.ppermute(block, 'chan', [(i, (i + direction) % groups) for i in range...]
    all_to_all x0 -> x1, starting transfers between devices: none -> 7.57 us  [shards(): states = lax.all_to_all(end_state, ('y', 'x'), 0, 0, tiled=True)]
    pallas_call x2 -> x3, Pallas kernels: 12.1 us -> 16 us  [on_device(): pl.pallas_call(kernel, out_shape=outs, in_specs=[smem] + [hbm] * copied +...]
    dot_general x5 -> x8, matrix products: 7.02 us -> 10.8 us  [product(): jnp.dot(gated, weight, preferred_element_type=jnp.float32)]
  transfers between devices with their start and end apart: 30 -> 32, of which waited for: 19 -> 19; matrix products, arithmetic and copies ran while one was open for 5% -> 10% of each run, Pallas kernels for 0% -> 11%
where the time goes in v3:
time: 128 us; the launch traced here: 127 us
  starting transfers between devices  49.6 us (39%)
  waiting for transfers between devices  45.1 us (35%)
  Pallas kernels  16.1 us (13%)
  matrix products  10.8 us (8%)
  other arithmetic  2.6 us (2%)
  local copies, waits for them, and re-layouts  2.24 us (2%)
    ppermute x4, waiting for transfers between devices, group_ring(): return lax.ppermute(block, ('core', 'chan'), pairs)  19.3 us
    ppermute x8, starting transfers between devices, send(): lax.ppermute(block, 'chan', [(i, (i + direction) % groups) for i in range...  17.7 us
    pallas_call x3, Pallas kernels, on_device(): pl.pallas_call(kernel, out_shape=outs, in_specs=[smem] + [hbm] * copied +...  16 us
    ppermute x11, starting transfers between devices, chip_ring(): return lax.ppermute(block, ('y', 'x', 'core'), pairs)  15.4 us
    ppermute x8, waiting for transfers between devices, send(): lax.ppermute(block, 'chan', [(i, (i + direction) % groups) for i in range...  11.3 us
    dot_general x8, matrix products, product(): jnp.dot(gated, weight, preferred_element_type=jnp.float32)  10.8 us
    ppermute x11, waiting for transfers between devices, chip_ring(): return lax.ppermute(block, ('y', 'x', 'core'), pairs)  9.53 us
    all_to_all x1, starting transfers between devices, shards(): states = lax.all_to_all(end_state, ('y', 'x'), 0, 0, tiled=True)  7.57 us
  transfers between devices with their start and end apart: 32, of which 19 were waited for; matrix products, arithmetic and copies ran while one was open for 10% of the time, Pallas kernels for 11%

profile of v3, /device:TPU:2, one launch (start us, length us, event | category | flops | bytes accessed | tf_op | source)
XLA Modules:
  0.0 127.0 jit_solution(14169047135592989629)
XLA Ops:
  0.0 1.1 constant_dynamic-slice_fusion.5
  1.1 0.7 collective-permute-done
  1.9 1.2 maximum_select_fusion
  3.1 3.4 %collective-permute-start.1 = (bf16[16,512]{1,0:T(8,128)(2,1)S(1)}, bf16[16,512]{1,0:T(8,128)(2,1)S(1)}, u32[]{:S(2)}, u32[]{:S(2)}) collective-permute-start(bf16[16,512]{1,0:T(8,128)(2,1)S(1)} %slice.40), channel_id=1, source_target_pairs={{0,16},{8,24},{16,32},{24,40},{32,48},{40,56},{48,64},{56,72},{64,... | collective-permute-start | bytes 49160 | tf_op jit(solution)/shard_map/ppermute | solution.py:255
  6.8 1.3 %collective-permute-start.4 = (bf16[256,768]{1,0:T(8,128)(2,1)S(1)}, bf16[256,768]{1,0:T(8,128)(2,1)S(1)}, u32[]{:S(2)}, u32[]{:S(2)}) collective-permute-start(bf16[256,768]{1,0:T(8,128)(2,1)S(1)} %pad_maximum_fusion.1.own), channel_id=1, source_target_pairs={{0,16},{8,72},{16,32},{24,88},{32,48},{40,104},{48,0},{56,120},{64... | collective-permute-start | bytes 1179656 | tf_op jit(solution)/shard_map/ppermute | solution.py:25
  8.0 0.8 collective-permute-start.5
  8.9 2.0 %collective-permute-start.2 = (bf16[528,512]{1,0:T(8,128)(2,1)S(1)}, bf16[528,512]{1,0:T(8,128)(2,1)S(1)}, u32[]{:S(2)}, u32[]{:S(2)}) collective-permute-start(bf16[528,512]{1,0:T(8,128)(2,1)S(1)} %pad_maximum_fusion.refs_0_), channel_id=1, source_target_pairs={{0,1},{1,2},{2,3},{3,4},{4,5},{5,6},{6,7},{7,0},{8,15},{9,8},{10,9... | collective-permute-start | bytes 1622024 | tf_op jit(solution)/shard_map/ppermute | solution.py:34
  10.9 3.7 %collective-permute-done.4.before = bf16[256,768]{1,0:T(8,128)(2,1)S(1)} collective-permute-done((bf16[256,768]{1,0:T(8,128)(2,1)S(1)}, bf16[256,768]{1,0:T(8,128)(2,1)S(1)}, u32[]{:S(2)}, u32[]{:S(2)}) %collective-permute-start.4) | collective-permute-done | bytes 393248 | tf_op jit(solution)/shard_map/ppermute | solution.py:25
  14.6 1.3 %collective-permute-start.11 = (bf16[128,768]{1,0:T(8,128)(2,1)S(1)}, bf16[128,768]{1,0:T(8,128)(2,1)S(1)}, u32[]{:S(2)}, u32[]{:S(2)}) collective-permute-start(bf16[128,768]{1,0:T(8,128)(2,1)S(1)} %slice.44), channel_id=1, source_target_pairs={{0,16},{8,72},{16,32},{24,88},{32,48},{40,104},{48,0},{56,120},{64... | collective-permute-start | bytes 589832 | tf_op jit(solution)/shard_map/ppermute | solution.py:25
  15.9 0.9 collective-permute-start.12
  16.8 5.4 %collective-permute-done.2.refs_1_ = bf16[528,512]{1,0:T(8,128)(2,1)S(1)} collective-permute-done((bf16[528,512]{1,0:T(8,128)(2,1)S(1)}, bf16[528,512]{1,0:T(8,128)(2,1)S(1)}, u32[]{:S(2)}, u32[]{:S(2)}) %collective-permute-start.2) | collective-permute-done | bytes 540704 | tf_op jit(solution)/shard_map/ppermute | solution.py:34
  22.3 1.7 %collective-permute-start.13 = (bf16[1024,512]{1,0:T(8,128)(2,1)S(1)}, bf16[1024,512]{1,0:T(8,128)(2,1)S(1)}, u32[]{:S(2)}, u32[]{:S(2)}) collective-permute-start(bf16[1024,512]{1,0:T(8,128)(2,1)S(1)} %get-tuple-element.29.refs_9_), channel_id=1, source_target_pairs={{0,64},{8,24},{16,80},{24,40},{32,96},{40,56},{48,112},{56,8},{64,... | collective-permute-start | bytes 3145736 | tf_op jit(solution)/shard_map/ppermute | solution.py:25
  24.0 1.7 %collective-permute-start.15 = (bf16[1024,512]{1,0:T(8,128)(2,1)S(1)}, bf16[1024,512]{1,0:T(8,128)(2,1)S(1)}, u32[]{:S(2)}, u32[]{:S(2)}) collective-permute-start(bf16[1024,512]{1,0:T(8,128)(2,1)S(1)} %get-tuple-element.29.refs_9_), channel_id=1, source_target_pairs={{0,192},{8,56},{16,208},{24,8},{32,224},{40,24},{48,240},{56,40},{... | collective-permute-start | bytes 3145736 | tf_op jit(solution)/shard_map/ppermute | solution.py:25
  25.7 0.9 collective-permute-start.8
  26.5 6.2 %collective-permute-done.6.refs_2_ = bf16[528,512]{1,0:T(8,128)(2,1)S(1)} collective-permute-done((bf16[528,512]{1,0:T(8,128)(2,1)S(1)}, bf16[528,512]{1,0:T(8,128)(2,1)S(1)}, u32[]{:S(2)}, u32[]{:S(2)}) %collective-permute-start.6) | collective-permute-done | bytes 540704 | tf_op jit(solution)/shard_map/ppermute | solution.py:34
  32.8 1.8 %collective-permute-start.9 = (bf16[528,512]{1,0:T(8,128)(2,1)S(1)}, bf16[528,512]{1,0:T(8,128)(2,1)S(1)}, u32[]{:S(2)}, u32[]{:S(2)}) collective-permute-start(bf16[528,512]{1,0:T(8,128)(2,1)S(1)} %collective-permute-done.6.refs_2_), channel_id=1, source_target_pairs={{0,8},{8,0},{1,9},{9,1},{2,10},{10,2},{3,11},{11,3},{4,12},{12,4},... | collective-permute-start | bytes 1622024 | tf_op jit(solution)/shard_map/ppermute | solution.py:14
  34.6 3.8 %collective-permute-done.13.refs_10_ = bf16[1024,512]{1,0:T(8,128)(2,1)S(1)} collective-permute-done((bf16[1024,512]{1,0:T(8,128)(2,1)S(1)}, bf16[1024,512]{1,0:T(8,128)(2,1)S(1)}, u32[]{:S(2)}, u32[]{:S(2)}) %collective-permute-start.13) | collective-permute-done | bytes 1048608 | tf_op jit(solution)/shard_map/ppermute | solution.py:25
  38.9 2.9 %collective-permute-start.18 = (bf16[1024,256]{1,0:T(8,128)(2,1)S(1)}, bf16[1024,256]{1,0:T(8,128)(2,1)S(1)}, u32[]{:S(2)}, u32[]{:S(2)}) collective-permute-start(bf16[1024,256]{1,0:T(8,128)(2,1)S(1)} %get-tuple-element.30.refs_9_), channel_id=1, source_target_pairs={{0,192},{8,56},{16,208},{24,8},{32,224},{40,24},{48,240},{56,40},{... | collective-permute-start | bytes 1572872 | tf_op jit(solution)/shard_map/ppermute | solution.py:25
  42.1 1.2 collective-permute-done.7.refs_3_
  43.3 3.0 %collective-permute-start.16 = (bf16[512,512]{1,0:T(8,128)(2,1)S(1)}, bf16[512,512]{1,0:T(8,128)(2,1)S(1)}, u32[]{:S(2)}, u32[]{:S(2)}) collective-permute-start(bf16[512,512]{1,0:T(8,128)(2,1)S(1)} %slice.47), channel_id=1, source_target_pairs={{0,192},{8,56},{16,208},{24,8},{32,224},{40,24},{48,240},{56,40},{... | collective-permute-start | bytes 1572872 | tf_op jit(solution)/shard_map/ppermute | solution.py:25
  46.9 2.0 %collective-permute-done.17.refs_10_ = bf16[1024,256]{1,0:T(8,128)(2,1)S(1)} collective-permute-done((bf16[1024,256]{1,0:T(8,128)(2,1)S(1)}, bf16[1024,256]{1,0:T(8,128)(2,1)S(1)}, u32[]{:S(2)}, u32[]{:S(2)}) %collective-permute-start.17) | collective-permute-done | bytes 524320 | tf_op jit(solution)/shard_map/ppermute | solution.py:25
  48.8 6.5 %collective-permute-done.10.refs_4_ = bf16[528,256]{1,0:T(8,128)(2,1)} collective-permute-done((bf16[528,256]{1,0:T(8,128)(2,1)S(1)}, bf16[528,256]{1,0:T(8,128)(2,1)}, u32[]{:S(2)}, u32[]{:S(2)}) %collective-permute-start.10) | collective-permute-done | bytes 270368 | tf_op jit(solution)/shard_map/ppermute | solution.py:34
  56.4 1.2 collective-permute-start.21
  58.3 8.5 %shard_map.65 = (f32[2,512,128]{2,1,0:T(8,128)S(1)}, f32[16,8,256]{2,1,0:T(8,128)S(1)}, f32[16,16,256]{2,1,0:T(8,128)}) custom-call(s32[5]{0:T(128)S(1)} %stack.23.place, bf16[528,512]{1,0:T(8,128)(2,1)} %copy-done.3, bf16[528,512]{1,0:T(8,128)(2,1)} %copy-done.7, bf16[528,512]{1,0:T(8,128)(2,1)} %copy-done.8, bf16[528,512]{1,0:T(8,128)(2,1)} %copy-done.4, ...), custom_call_target="tpu_custom_call" | custom-call | flops 2147483648 | bytes 5368709 | tf_op jit(solution)/shard_map/pallas_call | solution.py:219
  66.8 7.6 %all-to-all-start = ((f32[16,16,256]{2,1,0:T(8,128)}), f32[16,16,256]{2,1,0:T(8,128)S(1)}, u32[]{:S(2)}, u32[]{:S(2)}) async-start(f32[16,16,256]{2,1,0:T(8,128)} %get-tuple-element.39), calls=%async_computation | async-start | bytes 524288 | tf_op jit(solution)/shard_map/all_to_all | solution.py:324
  74.3 5.1 %shard_map.66.query = f32[512,256]{1,0:T(8,128)S(1)} custom-call(s32[5]{0:T(128)S(1)} %stack.23.place, bf16[528,512]{1,0:T(8,128)(2,1)} %copy-done.3, bf16[528,512]{1,0:T(8,128)(2,1)} %copy-done.7, bf16[528,512]{1,0:T(8,128)(2,1)} %copy-done.8, bf16[528,512]{1,0:T(8,128)(2,1)} %copy-done.4, bf16[528,256]{1,0:T(8,128)(2,1)} %collective-permute-done.10.refs_4_, ...), custom_call_target="tpu_custom_call" | custom-call | flops 1073741824 | bytes 2684354 | tf_op jit(solution)/shard_map/pallas_call | solution.py:219
  79.4 2.5 %all-to-all-done.states = f32[16,16,256]{2,1,0:T(8,128)S(1)} async-done(((f32[16,16,256]{2,1,0:T(8,128)}), f32[16,16,256]{2,1,0:T(8,128)S(1)}, u32[]{:S(2)}, u32[]{:S(2)}) %all-to-all-start) | async-done | bytes 262176 | tf_op jit(solution)/shard_map/all_to_all | solution.py:324
  81.8 2.5 %shard_map.67 = bf16[512,256]{1,0:T(8,128)(2,1)S(1)} custom-call(s32[5]{0:T(128)S(1)} %stack.23.place, f32[2,512,128]{2,1,0:T(8,128)S(1)} %get-tuple-element.35.signal, f32[512,256]{1,0:T(8,128)S(1)} %shard_map.66.query, f32[16,8,256]{2,1,0:T(8,128)S(1)} %get-tuple-element.38.block_ends, f32[16,16,256]{2,1,0:T(8,128)S(1)} %all-to-all-done.states, ...), custom_call_target="tpu_custom_call" | custom-call | flops 8388608 | bytes 20971 | tf_op jit(solution)/shard_map/pallas_call | solution.py:219
  84.5 1.3 %collective-permute-done.22 = bf16[256,256]{1,0:T(8,128)(2,1)S(1)} collective-permute-done((bf16[256,256]{1,0:T(8,128)(2,1)S(1)}, bf16[256,256]{1,0:T(8,128)(2,1)S(1)}, u32[]{:S(2)}, u32[]{:S(2)}) %collective-permute-start.22) | collective-permute-done | bytes 131104 | tf_op jit(solution)/shard_map/ppermute | solution.py:14
  85.8 1.3 %convolution_convert_fusion.3 = bf16[256,512]{1,0:T(8,128)(2,1)S(1)} fusion(bf16[512,4096]{1,0:T(8,128)(2,1)} %param.11, s32[]{:T(128)S(6)} %select_n.112, bf16[256,256]{1,0:T(8,128)(2,1)S(1)} %collective-permute-done.22, bf16[256,256]{1,0:T(8,128)(2,1)S(1)} %get-tuple-element.50, pred[]{:T(512)S(6)} %eq.14), kind=kOutput, calls=%fused_computation.3 | convolution fusion | flops 135528448 | bytes 1048581 | tf_op jit(solution)/shard_map/dot_general | solution.py:363
  87.2 2.0 %collective-permute-start.23 = (bf16[256,256]{1,0:T(8,128)(2,1)S(1)}, bf16[256,256]{1,0:T(8,128)(2,1)S(1)}, u32[]{:S(2)}, u32[]{:S(2)}) collective-permute-start(bf16[256,256]{1,0:T(8,128)(2,1)S(1)} %get-tuple-element.48), channel_id=1, source_target_pairs={{0,1},{1,2},{2,3},{3,4},{4,5},{5,6},{6,7},{7,0},{8,9},{9,10},{10,1... | collective-permute-start | bytes 393224 | tf_op jit(solution)/shard_map/ppermute | solution.py:358
  89.2 1.3 %convolution_convert_fusion = bf16[256,512]{1,0:T(8,128)(2,1)S(1)} fusion(bf16[512,4096]{1,0:T(8,128)(2,1)} %param.11, s32[]{:T(128)S(6)} %select_n.118, bf16[256,256]{1,0:T(8,128)(2,1)S(1)} %collective-permute-done.22, bf16[256,256]{1,0:T(8,128)(2,1)S(1)} %get-tuple-element.50, pred[]{:T(512)S(6)} %eq.14), kind=kOutput, calls=%fused_computation | convolution fusion | flops 135528448 | bytes 1048581 | tf_op jit(solution)/shard_map/dot_general | solution.py:363
  90.5 4.0 %collective-permute-start.27 = (bf16[256,256]{1,0:T(8,128)(2,1)S(1)}, bf16[256,256]{1,0:T(8,128)(2,1)S(1)}, u32[]{:S(2)}, u32[]{:S(2)}) collective-permute-start(bf16[256,256]{1,0:T(8,128)(2,1)S(1)} %get-tuple-element.49), channel_id=1, source_target_pairs={{0,7},{1,0},{2,1},{3,2},{4,3},{5,4},{6,5},{7,6},{8,15},{9,8},{10,9... | collective-permute-start | bytes 393224 | tf_op jit(solution)/shard_map/ppermute | solution.py:358
  94.6 1.3 %convolution_convert_fusion.4 = bf16[256,512]{1,0:T(8,128)(2,1)S(1)} fusion(bf16[512,4096]{1,0:T(8,128)(2,1)} %param.11, s32[]{:T(128)S(6)} %select_n.110, bf16[256,256]{1,0:T(8,128)(2,1)S(1)} %collective-permute-done.22, bf16[256,256]{1,0:T(8,128)(2,1)S(1)} %get-tuple-element.50, pred[]{:T(512)S(6)} %eq.14), kind=kOutput, calls=%fused_computation.4 | convolution fusion | flops 135528448 | bytes 1048581 | tf_op jit(solution)/shard_map/dot_general | solution.py:363
  95.9 1.0 collective-permute-done.23
  97.7 4.0 %collective-permute-start.28 = (bf16[256,512]{1,0:T(8,128)(2,1)S(1)}, bf16[256,512]{1,0:T(8,128)(2,1)S(1)}, u32[]{:S(2)}, u32[]{:S(2)}) collective-permute-start(bf16[256,512]{1,0:T(8,128)(2,1)S(1)} %add.143), channel_id=1, source_target_pairs={{0,7},{1,0},{2,1},{3,2},{4,3},{5,4},{6,5},{7,6},{8,15},{9,8},{10,9... | collective-permute-start | bytes 786440 | tf_op jit(solution)/shard_map/ppermute | solution.py:358
  101.7 1.3 %convolution_convert_fusion.1 = bf16[256,512]{1,0:T(8,128)(2,1)S(1)} fusion(bf16[512,4096]{1,0:T(8,128)(2,1)} %param.11, s32[]{:T(128)S(6)} %select_n.116, bf16[256,256]{1,0:T(8,128)(2,1)S(1)} %collective-permute-done.22, bf16[256,256]{1,0:T(8,128)(2,1)S(1)} %get-tuple-element.50, pred[]{:T(512)S(6)} %eq.14), kind=kOutput, calls=%fused_computation.1 | convolution fusion | flops 135528448 | bytes 1048581 | tf_op jit(solution)/shard_map/dot_general | solution.py:363
  103.1 1.3 %convolution_convert_fusion.5 = bf16[256,512]{1,0:T(8,128)(2,1)S(1)} fusion(bf16[512,4096]{1,0:T(8,128)(2,1)} %param.11, s32[]{:T(128)S(6)} %select_n.108, bf16[256,256]{1,0:T(8,128)(2,1)S(1)} %collective-permute-done.22, bf16[256,256]{1,0:T(8,128)(2,1)S(1)} %get-tuple-element.50, pred[]{:T(512)S(6)} %eq.14), kind=kOutput, calls=%fused_computation.5 | convolution fusion | flops 135528448 | bytes 1048581 | tf_op jit(solution)/shard_map/dot_general | solution.py:363
  104.4 1.7 %collective-permute-done.24 = bf16[256,512]{1,0:T(8,128)(2,1)S(1)} collective-permute-done((bf16[256,512]{1,0:T(8,128)(2,1)S(1)}, bf16[256,512]{1,0:T(8,128)(2,1)S(1)}, u32[]{:S(2)}, u32[]{:S(2)}) %collective-permute-start.24) | collective-permute-done | bytes 262176 | tf_op jit(solution)/shard_map/ppermute | solution.py:358
  106.8 3.8 %collective-permute-start.29 = (bf16[256,512]{1,0:T(8,128)(2,1)S(1)}, bf16[256,512]{1,0:T(8,128)(2,1)S(1)}, u32[]{:S(2)}, u32[]{:S(2)}) collective-permute-start(bf16[256,512]{1,0:T(8,128)(2,1)S(1)} %add.144), channel_id=1, source_target_pairs={{0,7},{1,0},{2,1},{3,2},{4,3},{5,4},{6,5},{7,6},{8,15},{9,8},{10,9... | collective-permute-start | bytes 786440 | tf_op jit(solution)/shard_map/ppermute | solution.py:358
  110.6 1.3 %convolution_convert_fusion.2 = bf16[256,512]{1,0:T(8,128)(2,1)S(1)} fusion(bf16[512,4096]{1,0:T(8,128)(2,1)} %param.11, s32[]{:T(128)S(6)} %select_n.114, bf16[256,256]{1,0:T(8,128)(2,1)S(1)} %collective-permute-done.22, bf16[256,256]{1,0:T(8,128)(2,1)S(1)} %get-tuple-element.50, pred[]{:T(512)S(6)} %eq.14), kind=kOutput, calls=%fused_computation.2 | convolution fusion | flops 135528448 | bytes 1048581 | tf_op jit(solution)/shard_map/dot_general | solution.py:363
  112.0 1.4 %convolution_convert_fusion.6 = bf16[256,512]{1,0:T(8,128)(2,1)S(1)} fusion(bf16[512,4096]{1,0:T(8,128)(2,1)} %param.11, s32[]{:T(128)S(6)} %select_n.106, bf16[256,256]{1,0:T(8,128)(2,1)S(1)} %collective-permute-done.22, bf16[256,256]{1,0:T(8,128)(2,1)S(1)} %get-tuple-element.50, pred[]{:T(512)S(6)} %eq.14), kind=kOutput, calls=%fused_computation.6 | convolution fusion | flops 135528448 | bytes 1048581 | tf_op jit(solution)/shard_map/dot_general | solution.py:363
  113.3 1.1 collective-permute-done.25
  114.8 3.8 %collective-permute-start.30 = (bf16[256,512]{1,0:T(8,128)(2,1)S(1)}, bf16[256,512]{1,0:T(8,128)(2,1)S(1)}, u32[]{:S(2)}, u32[]{:S(2)}) collective-permute-start(bf16[256,512]{1,0:T(8,128)(2,1)S(1)} %add.145), channel_id=1, source_target_pairs={{0,7},{1,0},{2,1},{3,2},{4,3},{5,4},{6,5},{7,6},{8,15},{9,8},{10,9... | collective-permute-start | bytes 786440 | tf_op jit(solution)/shard_map/ppermute | solution.py:358
  118.6 1.3 %convolution_convert_fusion.7 = bf16[256,512]{1,0:T(8,128)(2,1)S(1)} fusion(bf16[512,4096]{1,0:T(8,128)(2,1)} %param.11, s32[]{:T(128)S(6)} %select_n.104, bf16[256,256]{1,0:T(8,128)(2,1)S(1)} %collective-permute-done.22, bf16[256,256]{1,0:T(8,128)(2,1)S(1)} %get-tuple-element.50, pred[]{:T(512)S(6)} %eq.14), kind=kOutput, calls=%fused_computation.7 | convolution fusion | flops 135528448 | bytes 1048581 | tf_op jit(solution)/shard_map/dot_general | solution.py:363
  119.9 2.5 %collective-permute-done.30 = bf16[256,512]{1,0:T(8,128)(2,1)S(1)} collective-permute-done((bf16[256,512]{1,0:T(8,128)(2,1)S(1)}, bf16[256,512]{1,0:T(8,128)(2,1)S(1)}, u32[]{:S(2)}, u32[]{:S(2)}) %collective-permute-start.30) | collective-permute-done | bytes 262176 | tf_op jit(solution)/shard_map/ppermute | solution.py:358
  122.5 3.7 %collective-permute-done.26 = bf16[256,512]{1,0:T(8,128)(2,1)S(1)} collective-permute-done((bf16[256,512]{1,0:T(8,128)(2,1)S(1)}, bf16[256,512]{1,0:T(8,128)(2,1)S(1)}, u32[]{:S(2)}, u32[]{:S(2)}) %collective-permute-start.26) | collective-permute-done | bytes 262176 | tf_op jit(solution)/shard_map/ppermute | solution.py:358
  126.2 0.8 add_convert_fusion
  (87 shorter events, 5.4 us)
Async XLA Ops:
  0.0 57.7 %copy-start = (f32[3,3,512]{2,1,0:T(4,128)S(1)}, f32[3,3,512]{2,1,0:T(4,128)}, u32[]{:S(2)}) copy-start(f32[3,3,512]{2,1,0:T(4,128)} %param.8) | copy-start | bytes 55300
  0.0 1.7 %collective-permute-start = (bf16[256,512]{1,0:T(8,128)(2,1)}, bf16[256,512]{1,0:T(8,128)(2,1)S(1)}, u32[]{:S(2)}, u32[]{:S(2)}) collective-permute-start(bf16[256,512]{1,0:T(8,128)(2,1)} %param.6), channel_id=1, source_target_pairs={{0,8},{8,0},{1,9},{9,1},{2,10},{10,2},{3,11},{11,3},{4,12},{12,4},... | collective-permute-start | bytes 786440 | tf_op jit(solution)/shard_map/ppermute | solution.py:14
  1.8 4.7 %collective-permute-start.3 = (bf16[3,128,256]{2,1,0:T(8,128)(2,1)S(1)}, bf16[3,128,256]{2,1,0:T(8,128)(2,1)S(1)}, u32[]{:S(2)}, u32[]{:S(2)}) collective-permute-start(bf16[3,128,256]{2,1,0:T(8,128)(2,1)S(1)} %get-tuple-element.24), channel_id=1, source_target_pairs={{0,8},{8,0},{1,9},{9,1},{2,10},{10,2},{3,11},{11,3},{4,12},{12,4},... | collective-permute-start | bytes 589832 | tf_op jit(solution)/shard_map/ppermute | solution.py:14
  3.1 5.8 %collective-permute-start.1 = (bf16[16,512]{1,0:T(8,128)(2,1)S(1)}, bf16[16,512]{1,0:T(8,128)(2,1)S(1)}, u32[]{:S(2)}, u32[]{:S(2)}) collective-permute-start(bf16[16,512]{1,0:T(8,128)(2,1)S(1)} %slice.40), channel_id=1, source_target_pairs={{0,16},{8,24},{16,32},{24,40},{32,48},{40,56},{48,64},{56,72},{64,... | collective-permute-start | bytes 49160 | tf_op jit(solution)/shard_map/ppermute | solution.py:255
  6.5 51.2 %copy-start.15 = (f32[16,512]{1,0:T(8,128)S(1)}, f32[16,512]{1,0:T(8,128)}, u32[]{:S(2)}) copy-start(f32[16,512]{1,0:T(8,128)} %param.9) | copy-start | bytes 98308
  6.5 51.2 %copy-start.16 = (f32[16,512]{1,0:T(8,128)S(1)}, f32[16,512]{1,0:T(8,128)}, u32[]{:S(2)}) copy-start(f32[16,512]{1,0:T(8,128)} %param.10) | copy-start | bytes 98308
  6.8 7.9 %collective-permute-start.4 = (bf16[256,768]{1,0:T(8,128)(2,1)S(1)}, bf16[256,768]{1,0:T(8,128)(2,1)S(1)}, u32[]{:S(2)}, u32[]{:S(2)}) collective-permute-start(bf16[256,768]{1,0:T(8,128)(2,1)S(1)} %pad_maximum_fusion.1.own), channel_id=1, source_target_pairs={{0,16},{8,72},{16,32},{24,88},{32,48},{40,104},{48,0},{56,120},{64... | collective-permute-start | bytes 1179656 | tf_op jit(solution)/shard_map/ppermute | solution.py:25
  8.0 7.9 %collective-permute-start.5 = (bf16[256,768]{1,0:T(8,128)(2,1)S(1)}, bf16[256,768]{1,0:T(8,128)(2,1)S(1)}, u32[]{:S(2)}, u32[]{:S(2)}) collective-permute-start(bf16[256,768]{1,0:T(8,128)(2,1)S(1)} %pad_maximum_fusion.1.own), channel_id=1, source_target_pairs={{0,48},{8,200},{16,0},{24,216},{32,16},{40,232},{48,32},{56,248},{... | collective-permute-start | bytes 1179656 | tf_op jit(solution)/shard_map/ppermute | solution.py:25
  8.9 49.3 %copy-start.3 = (bf16[528,512]{1,0:T(8,128)(2,1)}, bf16[528,512]{1,0:T(8,128)(2,1)S(1)}, u32[]{:S(2)}) copy-start(bf16[528,512]{1,0:T(8,128)(2,1)S(1)} %pad_maximum_fusion.refs_0_) | copy-start | bytes 1622020
  8.9 13.3 %collective-permute-start.2 = (bf16[528,512]{1,0:T(8,128)(2,1)S(1)}, bf16[528,512]{1,0:T(8,128)(2,1)S(1)}, u32[]{:S(2)}, u32[]{:S(2)}) collective-permute-start(bf16[528,512]{1,0:T(8,128)(2,1)S(1)} %pad_maximum_fusion.refs_0_), channel_id=1, source_target_pairs={{0,1},{1,2},{2,3},{3,4},{4,5},{5,6},{6,7},{7,0},{8,15},{9,8},{10,9... | collective-permute-start | bytes 1622024 | tf_op jit(solution)/shard_map/ppermute | solution.py:34
  14.6 7.6 %collective-permute-start.11 = (bf16[128,768]{1,0:T(8,128)(2,1)S(1)}, bf16[128,768]{1,0:T(8,128)(2,1)S(1)}, u32[]{:S(2)}, u32[]{:S(2)}) collective-permute-start(bf16[128,768]{1,0:T(8,128)(2,1)S(1)} %slice.44), channel_id=1, source_target_pairs={{0,16},{8,72},{16,32},{24,88},{32,48},{40,104},{48,0},{56,120},{64... | collective-permute-start | bytes 589832 | tf_op jit(solution)/shard_map/ppermute | solution.py:25
  15.9 6.3 %collective-permute-start.12 = (bf16[128,768]{1,0:T(8,128)(2,1)S(1)}, bf16[128,768]{1,0:T(8,128)(2,1)S(1)}, u32[]{:S(2)}, u32[]{:S(2)}) collective-permute-start(bf16[128,768]{1,0:T(8,128)(2,1)S(1)} %slice.45), channel_id=1, source_target_pairs={{0,48},{8,200},{16,0},{24,216},{32,16},{40,232},{48,32},{56,248},{... | collective-permute-start | bytes 589832 | tf_op jit(solution)/shard_map/ppermute | solution.py:25
  22.2 35.5 %copy-start.7 = (bf16[528,512]{1,0:T(8,128)(2,1)}, bf16[528,512]{1,0:T(8,128)(2,1)S(1)}, u32[]{:S(2)}) copy-start(bf16[528,512]{1,0:T(8,128)(2,1)S(1)} %collective-permute-done.2.refs_1_) | copy-start | bytes 1622020
  22.2 10.6 %collective-permute-start.6 = (bf16[528,512]{1,0:T(8,128)(2,1)S(1)}, bf16[528,512]{1,0:T(8,128)(2,1)S(1)}, u32[]{:S(2)}, u32[]{:S(2)}) collective-permute-start(bf16[528,512]{1,0:T(8,128)(2,1)S(1)} %collective-permute-done.2.refs_1_), channel_id=1, source_target_pairs={{0,1},{1,2},{2,3},{3,4},{4,5},{5,6},{6,7},{7,0},{8,15},{9,8},{10,9... | collective-permute-start | bytes 1622024 | tf_op jit(solution)/shard_map/ppermute | solution.py:34
  22.3 35.9 %copy-start.1 = (bf16[1024,512]{1,0:T(8,128)(2,1)}, bf16[1024,512]{1,0:T(8,128)(2,1)S(1)}, u32[]{:S(2)}) copy-start(bf16[1024,512]{1,0:T(8,128)(2,1)S(1)} %get-tuple-element.29.refs_9_) | copy-start | bytes 3145732
  22.3 44.4 %copy-start.2 = (bf16[1024,256]{1,0:T(8,128)(2,1)}, bf16[1024,256]{1,0:T(8,128)(2,1)S(1)}, u32[]{:S(2)}) copy-start(bf16[1024,256]{1,0:T(8,128)(2,1)S(1)} %get-tuple-element.30.refs_9_) | copy-start | bytes 1572868
  22.3 16.1 %collective-permute-start.13 = (bf16[1024,512]{1,0:T(8,128)(2,1)S(1)}, bf16[1024,512]{1,0:T(8,128)(2,1)S(1)}, u32[]{:S(2)}, u32[]{:S(2)}) collective-permute-start(bf16[1024,512]{1,0:T(8,128)(2,1)S(1)} %get-tuple-element.29.refs_9_), channel_id=1, source_target_pairs={{0,64},{8,24},{16,80},{24,40},{32,96},{40,56},{48,112},{56,8},{64,... | collective-permute-start | bytes 3145736 | tf_op jit(solution)/shard_map/ppermute | solution.py:25
  24.0 14.8 %collective-permute-start.15 = (bf16[1024,512]{1,0:T(8,128)(2,1)S(1)}, bf16[1024,512]{1,0:T(8,128)(2,1)S(1)}, u32[]{:S(2)}, u32[]{:S(2)}) collective-permute-start(bf16[1024,512]{1,0:T(8,128)(2,1)S(1)} %get-tuple-element.29.refs_9_), channel_id=1, source_target_pairs={{0,192},{8,56},{16,208},{24,8},{32,224},{40,24},{48,240},{56,40},{... | collective-permute-start | bytes 3145736 | tf_op jit(solution)/shard_map/ppermute | solution.py:25
  25.7 16.2 %collective-permute-start.8 = (bf16[528,512]{1,0:T(8,128)(2,1)S(1)}, bf16[528,512]{1,0:T(8,128)(2,1)S(1)}, u32[]{:S(2)}, u32[]{:S(2)}) collective-permute-start(bf16[528,512]{1,0:T(8,128)(2,1)S(1)} %collective-permute-done.2.refs_1_), channel_id=1, source_target_pairs={{0,8},{8,0},{1,9},{9,1},{2,10},{10,2},{3,11},{11,3},{4,12},{12,4},... | collective-permute-start | bytes 1622024 | tf_op jit(solution)/shard_map/ppermute | solution.py:14
  32.8 22.7 %copy-start.8 = (bf16[528,512]{1,0:T(8,128)(2,1)}, bf16[528,512]{1,0:T(8,128)(2,1)S(1)}, u32[]{:S(2)}) copy-start(bf16[528,512]{1,0:T(8,128)(2,1)S(1)} %collective-permute-done.6.refs_2_) | copy-start | bytes 1622020
  32.8 10.6 %collective-permute-start.7 = (bf16[528,512]{1,0:T(8,128)(2,1)S(1)}, bf16[528,512]{1,0:T(8,128)(2,1)S(1)}, u32[]{:S(2)}, u32[]{:S(2)}) collective-permute-start(bf16[528,512]{1,0:T(8,128)(2,1)S(1)} %collective-permute-done.6.refs_2_), channel_id=1, source_target_pairs={{0,1},{1,2},{2,3},{3,4},{4,5},{5,6},{6,7},{7,0},{8,15},{9,8},{10,9... | collective-permute-start | bytes 1622024 | tf_op jit(solution)/shard_map/ppermute | solution.py:34
  32.8 13.6 %collective-permute-start.9 = (bf16[528,512]{1,0:T(8,128)(2,1)S(1)}, bf16[528,512]{1,0:T(8,128)(2,1)S(1)}, u32[]{:S(2)}, u32[]{:S(2)}) collective-permute-start(bf16[528,512]{1,0:T(8,128)(2,1)S(1)} %collective-permute-done.6.refs_2_), channel_id=1, source_target_pairs={{0,8},{8,0},{1,9},{9,1},{2,10},{10,2},{3,11},{11,3},{4,12},{12,4},... | collective-permute-start | bytes 1622024 | tf_op jit(solution)/shard_map/ppermute | solution.py:14
  38.4 16.9 %copy-start.5 = (bf16[1024,512]{1,0:T(8,128)(2,1)}, bf16[1024,512]{1,0:T(8,128)(2,1)S(1)}, u32[]{:S(2)}) copy-start(bf16[1024,512]{1,0:T(8,128)(2,1)S(1)} %collective-permute-done.13.refs_10_) | copy-start | bytes 3145732
  38.4 10.4 %collective-permute-start.17 = (bf16[1024,256]{1,0:T(8,128)(2,1)S(1)}, bf16[1024,256]{1,0:T(8,128)(2,1)S(1)}, u32[]{:S(2)}, u32[]{:S(2)}) collective-permute-start(bf16[1024,256]{1,0:T(8,128)(2,1)S(1)} %get-tuple-element.30.refs_9_), channel_id=1, source_target_pairs={{0,64},{8,24},{16,80},{24,40},{32,96},{40,56},{48,112},{56,8},{64,... | collective-permute-start | bytes 1572872 | tf_op jit(solution)/shard_map/ppermute | solution.py:25
  38.8 16.5 %copy-start.6 = (bf16[1024,512]{1,0:T(8,128)(2,1)}, bf16[1024,512]{1,0:T(8,128)(2,1)S(1)}, u32[]{:S(2)}) copy-start(bf16[1024,512]{1,0:T(8,128)(2,1)S(1)} %collective-permute-done.15.refs_11_) | copy-start | bytes 3145732
  38.9 10.0 %collective-permute-start.18 = (bf16[1024,256]{1,0:T(8,128)(2,1)S(1)}, bf16[1024,256]{1,0:T(8,128)(2,1)S(1)}, u32[]{:S(2)}, u32[]{:S(2)}) collective-permute-start(bf16[1024,256]{1,0:T(8,128)(2,1)S(1)} %get-tuple-element.30.refs_9_), channel_id=1, source_target_pairs={{0,192},{8,56},{16,208},{24,8},{32,224},{40,24},{48,240},{56,40},{... | collective-permute-start | bytes 1572872 | tf_op jit(solution)/shard_map/ppermute | solution.py:25
  41.9 13.6 %copy-start.9 = (bf16[528,512]{1,0:T(8,128)(2,1)}, bf16[528,512]{1,0:T(8,128)(2,1)S(1)}, u32[]{:S(2)}) copy-start(bf16[528,512]{1,0:T(8,128)(2,1)S(1)} %collective-permute-done.8.refs_5_) | copy-start | bytes 1622020
  41.9 13.5 %collective-permute-start.14 = (bf16[512,512]{1,0:T(8,128)(2,1)S(1)}, bf16[512,512]{1,0:T(8,128)(2,1)S(1)}, u32[]{:S(2)}, u32[]{:S(2)}) collective-permute-start(bf16[512,512]{1,0:T(8,128)(2,1)S(1)} %slice.46), channel_id=1, source_target_pairs={{0,64},{8,24},{16,80},{24,40},{32,96},{40,56},{48,112},{56,8},{64,... | collective-permute-start | bytes 1572872 | tf_op jit(solution)/shard_map/ppermute | solution.py:25
  43.3 14.9 %copy-start.4 = (bf16[528,512]{1,0:T(8,128)(2,1)}, bf16[528,512]{1,0:T(8,128)(2,1)S(1)}, u32[]{:S(2)}) copy-start(bf16[528,512]{1,0:T(8,128)(2,1)S(1)} %collective-permute-done.7.refs_3_) | copy-start | bytes 1622020
  43.3 12.0 %collective-permute-start.16 = (bf16[512,512]{1,0:T(8,128)(2,1)S(1)}, bf16[512,512]{1,0:T(8,128)(2,1)S(1)}, u32[]{:S(2)}, u32[]{:S(2)}) collective-permute-start(bf16[512,512]{1,0:T(8,128)(2,1)S(1)} %slice.47), channel_id=1, source_target_pairs={{0,192},{8,56},{16,208},{24,8},{32,224},{40,24},{48,240},{56,40},{... | collective-permute-start | bytes 1572872 | tf_op jit(solution)/shard_map/ppermute | solution.py:25
  46.4 9.1 %copy-start.10 = (bf16[528,512]{1,0:T(8,128)(2,1)}, bf16[528,512]{1,0:T(8,128)(2,1)S(1)}, u32[]{:S(2)}) copy-start(bf16[528,512]{1,0:T(8,128)(2,1)S(1)} %collective-permute-done.9.refs_6_) | copy-start | bytes 1622020
  46.4 9.0 %collective-permute-start.10 = (bf16[528,256]{1,0:T(8,128)(2,1)S(1)}, bf16[528,256]{1,0:T(8,128)(2,1)}, u32[]{:S(2)}, u32[]{:S(2)}) collective-permute-start(bf16[528,256]{1,0:T(8,128)(2,1)S(1)} %constant_dynamic-slice_fusion.3), channel_id=1, source_target_pairs={{0,1},{1,2},{2,3},{3,4},{4,5},{5,6},{6,7},{7,0},{8,15},{9,8},{10,9... | collective-permute-start | bytes 811016 | tf_op jit(solution)/shard_map/ppermute | solution.py:34
  48.8 6.7 %copy-start.11 = (bf16[1024,256]{1,0:T(8,128)(2,1)}, bf16[1024,256]{1,0:T(8,128)(2,1)S(1)}, u32[]{:S(2)}) copy-start(bf16[1024,256]{1,0:T(8,128)(2,1)S(1)} %collective-permute-done.17.refs_10_) | copy-start | bytes 1572868
  48.8 6.7 %copy-start.12 = (bf16[1024,256]{1,0:T(8,128)(2,1)}, bf16[1024,256]{1,0:T(8,128)(2,1)S(1)}, u32[]{:S(2)}) copy-start(bf16[1024,256]{1,0:T(8,128)(2,1)S(1)} %collective-permute-done.18.refs_11_) | copy-start | bytes 1572868
  55.4 1.0 copy-start.14
  55.4 2.9 %collective-permute-start.19 = (bf16[528,512]{1,0:T(8,128)(2,1)S(1)}, bf16[528,512]{1,0:T(8,128)(2,1)}, u32[]{:S(2)}, u32[]{:S(2)}) collective-permute-start(bf16[528,512]{1,0:T(8,128)(2,1)S(1)} %collective-permute-done.7.refs_3_), channel_id=1, source_target_pairs={{0,8},{8,0},{1,9},{9,1},{2,10},{10,2},{3,11},{11,3},{4,12},{12,4},... | collective-permute-start | bytes 1622024 | tf_op jit(solution)/shard_map/ppermute | solution.py:14
  56.4 1.9 %collective-permute-start.20 = (bf16[528,256]{1,0:T(8,128)(2,1)}, bf16[528,256]{1,0:T(8,128)(2,1)}, u32[]{:S(2)}, u32[]{:S(2)}) collective-permute-start(bf16[528,256]{1,0:T(8,128)(2,1)} %collective-permute-done.10.refs_4_), channel_id=1, source_target_pairs={{0,8},{8,0},{1,9},{9,1},{2,10},{10,2},{3,11},{11,3},{4,12},{12,4},... | collective-permute-start | bytes 811016 | tf_op jit(solution)/shard_map/ppermute | solution.py:14
  56.4 17.9 %collective-permute-start.21 = (bf16[1024,256]{1,0:T(8,128)(2,1)S(1)}, bf16[1024,256]{1,0:T(8,128)(2,1)}, u32[]{:S(2)}, u32[]{:S(2)}) collective-permute-start(bf16[1024,256]{1,0:T(8,128)(2,1)S(1)} %get-tuple-element.30.refs_9_), channel_id=1, source_target_pairs={{0,128},{8,40},{16,144},{24,56},{32,160},{40,8},{48,176},{56,24},{... | collective-permute-start | bytes 1572872 | tf_op jit(solution)/shard_map/ppermute | solution.py:25
  66.8 15.1 %all-to-all-start = ((f32[16,16,256]{2,1,0:T(8,128)}), f32[16,16,256]{2,1,0:T(8,128)S(1)}, u32[]{:S(2)}, u32[]{:S(2)}) async-start(f32[16,16,256]{2,1,0:T(8,128)} %get-tuple-element.39), calls=%async_computation | async-start | bytes 524288 | tf_op jit(solution)/shard_map/all_to_all | solution.py:324
  84.4 1.4 %collective-permute-start.22 = (bf16[256,256]{1,0:T(8,128)(2,1)S(1)}, bf16[256,256]{1,0:T(8,128)(2,1)S(1)}, u32[]{:S(2)}, u32[]{:S(2)}) collective-permute-start(bf16[256,256]{1,0:T(8,128)(2,1)S(1)} %get-tuple-element.51), channel_id=1, source_target_pairs={{0,8},{8,0},{1,9},{9,1},{2,10},{10,2},{3,11},{11,3},{4,12},{12,4},... | collective-permute-start | bytes 393224 | tf_op jit(solution)/shard_map/ppermute | solution.py:14
  87.2 9.7 %collective-permute-start.23 = (bf16[256,256]{1,0:T(8,128)(2,1)S(1)}, bf16[256,256]{1,0:T(8,128)(2,1)S(1)}, u32[]{:S(2)}, u32[]{:S(2)}) collective-permute-start(bf16[256,256]{1,0:T(8,128)(2,1)S(1)} %get-tuple-element.48), channel_id=1, source_target_pairs={{0,1},{1,2},{2,3},{3,4},{4,5},{5,6},{6,7},{7,0},{8,9},{9,10},{10,1... | collective-permute-start | bytes 393224 | tf_op jit(solution)/shard_map/ppermute | solution.py:358
  90.5 7.1 %collective-permute-start.27 = (bf16[256,256]{1,0:T(8,128)(2,1)S(1)}, bf16[256,256]{1,0:T(8,128)(2,1)S(1)}, u32[]{:S(2)}, u32[]{:S(2)}) collective-permute-start(bf16[256,256]{1,0:T(8,128)(2,1)S(1)} %get-tuple-element.49), channel_id=1, source_target_pairs={{0,7},{1,0},{2,1},{3,2},{4,3},{5,4},{6,5},{7,6},{8,15},{9,8},{10,9... | collective-permute-start | bytes 393224 | tf_op jit(solution)/shard_map/ppermute | solution.py:358
  97.0 9.1 %collective-permute-start.24 = (bf16[256,512]{1,0:T(8,128)(2,1)S(1)}, bf16[256,512]{1,0:T(8,128)(2,1)S(1)}, u32[]{:S(2)}, u32[]{:S(2)}) collective-permute-start(bf16[256,512]{1,0:T(8,128)(2,1)S(1)} %pad_add_fusion), channel_id=1, source_target_pairs={{0,1},{1,2},{2,3},{3,4},{4,5},{5,6},{6,7},{7,0},{8,9},{9,10},{10,1... | collective-permute-start | bytes 786440 | tf_op jit(solution)/shard_map/ppermute | solution.py:358
  97.7 9.0 %collective-permute-start.28 = (bf16[256,512]{1,0:T(8,128)(2,1)S(1)}, bf16[256,512]{1,0:T(8,128)(2,1)S(1)}, u32[]{:S(2)}, u32[]{:S(2)}) collective-permute-start(bf16[256,512]{1,0:T(8,128)(2,1)S(1)} %add.143), channel_id=1, source_target_pairs={{0,7},{1,0},{2,1},{3,2},{4,3},{5,4},{6,5},{7,6},{8,15},{9,8},{10,9... | collective-permute-start | bytes 786440 | tf_op jit(solution)/shard_map/ppermute | solution.py:358
  106.2 8.2 %collective-permute-start.25 = (bf16[256,512]{1,0:T(8,128)(2,1)S(1)}, bf16[256,512]{1,0:T(8,128)(2,1)S(1)}, u32[]{:S(2)}, u32[]{:S(2)}) collective-permute-start(bf16[256,512]{1,0:T(8,128)(2,1)S(1)} %add.131), channel_id=1, source_target_pairs={{0,1},{1,2},{2,3},{3,4},{4,5},{5,6},{6,7},{7,0},{8,9},{9,10},{10,1... | collective-permute-start | bytes 786440 | tf_op jit(solution)/shard_map/ppermute | solution.py:358
  106.8 7.9 %collective-permute-start.29 = (bf16[256,512]{1,0:T(8,128)(2,1)S(1)}, bf16[256,512]{1,0:T(8,128)(2,1)S(1)}, u32[]{:S(2)}, u32[]{:S(2)}) collective-permute-start(bf16[256,512]{1,0:T(8,128)(2,1)S(1)} %add.144), channel_id=1, source_target_pairs={{0,7},{1,0},{2,1},{3,2},{4,3},{5,4},{6,5},{7,6},{8,15},{9,8},{10,9... | collective-permute-start | bytes 786440 | tf_op jit(solution)/shard_map/ppermute | solution.py:358
  114.8 7.7 %collective-permute-start.30 = (bf16[256,512]{1,0:T(8,128)(2,1)S(1)}, bf16[256,512]{1,0:T(8,128)(2,1)S(1)}, u32[]{:S(2)}, u32[]{:S(2)}) collective-permute-start(bf16[256,512]{1,0:T(8,128)(2,1)S(1)} %add.145), channel_id=1, source_target_pairs={{0,7},{1,0},{2,1},{3,2},{4,3},{5,4},{6,5},{7,6},{8,15},{9,8},{10,9... | collective-permute-start | bytes 786440 | tf_op jit(solution)/shard_map/ppermute | solution.py:358
  118.6 7.6 %collective-permute-start.26 = (bf16[256,512]{1,0:T(8,128)(2,1)S(1)}, bf16[256,512]{1,0:T(8,128)(2,1)S(1)}, u32[]{:S(2)}, u32[]{:S(2)}) collective-permute-start(bf16[256,512]{1,0:T(8,128)(2,1)S(1)} %add.132), channel_id=1, source_target_pairs={{0,1},{1,2},{2,3},{3,4},{4,5},{5,6},{6,7},{7,0},{8,9},{9,10},{10,1... | collective-permute-start | bytes 786440 | tf_op jit(solution)/shard_map/ppermute | solution.py:358
  (1 other events, 0.8 us)

commit v4 on v3

--- a/solution.py
+++ b/solution.py
@@ -25,12 +25,12 @@
     return lax.ppermute(block, ("y", "x", "core"), pairs)
 
 
-def group_ring(block):
+def group_ring(block, hops=1):
     n = lax.axis_size("chan")
     pairs = []
     for c in range(2):
         for z in range(n):
-            pairs.append((c * n + z, c * n + (z + 1 - 2 * c) % n))
+            pairs.append((c * n + z, c * n + (z + (1 - 2 * c) * hops) % n))
     return lax.ppermute(block, ("core", "chan"), pairs)
 
 
@@ -179,7 +179,10 @@
         end_state[chip] = state
 
 
-def scan_kernel(place, signal, query, block_ends, states, rates, amplitude, gated, block_starts, result):
+def scan_kernel(place, out_weight, signal, query, block_ends, states, rates, amplitude, *refs):
+    gated, out_weight_near, block_starts, result, semaphore = refs
+    copy = pltpu.make_async_copy(out_weight, out_weight_near, semaphore.at[0])
+    copy.start()
     modes, blocks, width = block_ends.shape
     steps = signal.shape[1] // blocks
     chip_decay = jnp.exp(-rates[...] * float(steps * blocks))
@@ -209,6 +212,7 @@
         states_now = tuple(block_starts[m, :, lanes] for m in range(modes))
         lax.fori_loop(0, steps, step, states_now, unroll=4)
         gated[:, lanes] = (query[:, lanes] * result[part]).astype(jnp.bfloat16)
+    copy.wait()
 
 
 def on_device(kernel, outs, scratch, cost, limit, copied, place, *arrays):
@@ -337,47 +341,89 @@
         13,
         place, *gathered, *query_weights, taps,
     )
-    gated = on_device(
+    gated, out_weight_near = on_device(
         scan_kernel,
-        jax.ShapeDtypeStruct((positions, width), bf16),
-        [pltpu.VMEM((modes, blocks, width), f32), pltpu.VMEM(lanes, f32)],
+        (
+            jax.ShapeDtypeStruct((positions, width), bf16),
+            jax.ShapeDtypeStruct(out_weight.shape, bf16),
+        ),
+        [
+            pltpu.VMEM((modes, blocks, width), f32),
+            pltpu.VMEM(lanes, f32),
+            dma((1,)),
+        ],
         4 * modes * positions * width,
-        12,
+        16,
+        1,
+        place, out_weight, signal, query, block_ends, states, rates, amplitude,
+    )
+    given = swap_cores(gated)
+    out_width = out_weight.shape[1] // groups
+    half = out_width // 2
+    parts = on_device(
+        functools.partial(product_kernel, groups),
+        (
+            jax.ShapeDtypeStruct((positions, half), bf16),
+            jax.ShapeDtypeStruct((positions, out_width), bf16),
+            jax.ShapeDtypeStruct((positions, out_width), bf16),
+            jax.ShapeDtypeStruct((positions, out_width), bf16),
+            jax.ShapeDtypeStruct((rows, out_width), bf16),
+        ),
+        [],
+        3 * rows * out_weight.size,
+        20,
         0,
-        place, signal, query, block_ends, states, rates, amplitude,
-    )
-    given = swap_cores(lax.dynamic_slice_in_dim(gated, (1 - core) * rows, rows, axis=0))
-    gated = by_core(lax.dynamic_slice_in_dim(gated, core * rows, rows, axis=0), given, 1)
-    return reduced(gated, out_weight, z, groups)
-
-
-def reduced(gated, out_weight, z, groups):
-    width = out_weight.shape[1] // groups
-
-    def send(block, direction):
-        return lax.ppermute(block, "chan", [(i, (i + direction) % groups) for i in range(groups)])
-
-    def product(distance):
-        start = (z + distance) % groups * width
-        weight = lax.dynamic_slice_in_dim(out_weight, start, width, axis=1)
-        total = jnp.dot(gated, weight, preferred_element_type=jnp.float32).astype(jnp.bfloat16)
-        return lax.optimization_barrier(total)
-
-    half = width // 2
-    part = product(4)
-    ahead, behind = part[:, :half], part[:, half:]
-    own = product(0)
-    for distance in (3, 2, 1):
-        ahead_part, behind_part = product(distance), product(-distance)
-        ahead, behind = send(ahead, 1), send(behind, -1)
-        if distance == 3:
-            ahead = jnp.concatenate([ahead, jnp.zeros_like(ahead)], axis=1)
-            behind = jnp.concatenate([jnp.zeros_like(behind), behind], axis=1)
-        ahead = ahead_part + ahead
-        behind, _ = lax.optimization_barrier((behind, ahead))
-        behind = behind_part + behind
-    ahead, behind = send(ahead, 1), send(behind, -1)
-    total = own.astype(jnp.float32) + ahead.astype(jnp.float32) + behind.astype(jnp.float32)
+        place, gated, given, out_weight_near,
+    )
+    return reduced(parts, core)
+
+
+def product_kernel(groups, place, mine, given, weight, far, third, second, first, own):
+    core = place[1]
+    ahead = 1 - 2 * core
+    depth = mine.shape[1]
+    count, columns = own.shape
+    own_channels = pl.ds(pl.multiple_of(core * depth, depth), depth)
+    other_channels = pl.ds(pl.multiple_of((1 - core) * depth, depth), depth)
+    own_rows = pl.ds(pl.multiple_of(core * count, count), count)
+    other_rows = pl.ds(pl.multiple_of((1 - core) * count, count), count)
+    for distance, part in ((4, far), (3, third), (2, second), (1, first), (0, own)):
+        group = lax.rem(place[0] + ahead * distance + groups, groups)
+        start = group * columns
+        if distance == 4:
+            start = start + core * part.shape[1]
+        to = pl.ds(pl.multiple_of(start, part.shape[1]), part.shape[1])
+        wanted = [own_rows] if distance == 0 else [other_rows, own_rows]
+        for number, rows in enumerate(wanted):
+            total = jnp.dot(mine[rows, :], weight[own_channels, to], preferred_element_type=jnp.float32)
+            total += jnp.dot(given[rows, :], weight[other_channels, to], preferred_element_type=jnp.float32)
+            part[pl.ds(number * count, count), :] = total.astype(jnp.bfloat16)
+
+
+def reduced(parts, core):
+    far, third, second, first, own = parts
+    rows = own.shape[0]
+    far = group_ring(far, 2)
+    nothing = jnp.zeros_like(far)
+    far = jnp.where(
+        core == 0,
+        jnp.concatenate([far, nothing], axis=1),
+        jnp.concatenate([nothing, far], axis=1),
+    )
+    spans = slice(0, rows), slice(rows, 2 * rows)
+    streams = [third[span] for span in spans]
+    for part, more in ((second, far), (first, None)):
+        for number, span in enumerate(spans):
+            arrived = group_ring(streams[number])
+            if number:
+                arrived, _ = lax.optimization_barrier((arrived, streams[0]))
+            streams[number] = part[span] + arrived
+            if more is not None:
+                streams[number] += more[span]
+    other, kept = [group_ring(stream) for stream in streams]
+    got = swap_cores(other)
+    kept, got = lax.optimization_barrier((kept, got))
+    total = own.astype(jnp.float32) + kept.astype(jnp.float32) + got.astype(jnp.float32)
     return total.astype(jnp.bfloat16)
 
 

time: 128 us -> 125 us (0.977)
  waiting for transfers between devices: 45.1 us -> 58.2 us
  matrix products: 10.8 us -> 0 us
  starting transfers between devices: 49.6 us -> 40.6 us
  Pallas kernels: 16.1 us -> 18.2 us
  local copies, waits for them, and re-layouts: 2.24 us -> 3.73 us
    ppermute x4 -> x11, waiting for transfers between devices: 19.3 us -> 44.1 us  [group_ring(): return lax.ppermute(block, ('core', 'chan'), pairs)]
    ppermute x8 -> x0, starting transfers between devices: 17.7 us -> none  [send(): lax.ppermute(block, 'chan', [(i, (i + direction) % groups) for i in range...]
    ppermute x8 -> x0, waiting for transfers between devices: 11.3 us -> none  [send(): lax.ppermute(block, 'chan', [(i, (i + direction) % groups) for i in range...]
    dot_general x8 -> x0, matrix products: 10.8 us -> none  [product(): jnp.dot(gated, weight, preferred_element_type=jnp.float32)]
    ppermute x4 -> x11, starting transfers between devices: 2.47 us -> 10.9 us  [group_ring(): return lax.ppermute(block, ('core', 'chan'), pairs)]
    pallas_call x3 -> x4, Pallas kernels: 16 us -> 18.1 us  [on_device(): pl.pallas_call(kernel, out_shape=outs, in_specs=[smem] + [hbm] * copied +...]
    unnamed x34 -> x40, local copies, waits for them, and re-layouts: 0.89 us -> 2.41 us
    ppermute x7 -> x8, starting transfers between devices: 3.04 us -> 3.03 us  [swap_cores(): return lax.ppermute(block, 'core', [(0, 1), (1, 0)])]
  transfers between devices with their start and end apart: 32 -> 32, of which waited for: 19 -> 18; matrix products, arithmetic and copies ran while one was open for 10% -> 2% of each run, Pallas kernels for 11% -> 11%
where the time goes in v4:
time: 125 us; the launch traced here: 124 us
  waiting for transfers between devices  58.2 us (47%)
  starting transfers between devices  40.6 us (32%)
  Pallas kernels  18.2 us (15%)
  local copies, waits for them, and re-layouts  3.73 us (3%)
  other arithmetic  2.48 us (2%)
    ppermute x11, waiting for transfers between devices, group_ring(): return lax.ppermute(block, ('core', 'chan'), pairs)  44.1 us
    pallas_call x4, Pallas kernels, on_device(): pl.pallas_call(kernel, out_shape=outs, in_specs=[smem] + [hbm] * copied +...  18.1 us
    ppermute x11, starting transfers between devices, chip_ring(): return lax.ppermute(block, ('y', 'x', 'core'), pairs)  15.5 us
    ppermute x11, starting transfers between devices, group_ring(): return lax.ppermute(block, ('core', 'chan'), pairs)  10.9 us
    ppermute x11, waiting for transfers between devices, chip_ring(): return lax.ppermute(block, ('y', 'x', 'core'), pairs)  9.49 us
    all_to_all x1, starting transfers between devices, shards(): states = lax.all_to_all(end_state, ('y', 'x'), 0, 0, tiled=True)  7.85 us
    ppermute x1, starting transfers between devices, shards(): lax.ppermute(block[-HALO:], ('y', 'x', 'core'), [(i, i + 2) for i in rang...  3.41 us
    ppermute x8, starting transfers between devices, swap_cores(): return lax.ppermute(block, 'core', [(0, 1), (1, 0)])  3.03 us
  transfers between devices with their start and end apart: 32, of which 18 were waited for; matrix products, arithmetic and copies ran while one was open for 2% of the time, Pallas kernels for 11%

profile of v4, /device:TPU:2, one launch (start us, length us, event | category | flops | bytes accessed | tf_op | source)
XLA Modules:
  0.0 123.7 jit_solution(5925687016296910248)
XLA Ops:
  0.0 1.1 constant_dynamic-slice_fusion.3
  1.1 0.7 collective-permute-done
  1.9 1.2 maximum_select_fusion
  3.1 3.4 %collective-permute-start.1 = (bf16[16,512]{1,0:T(8,128)(2,1)S(1)}, bf16[16,512]{1,0:T(8,128)(2,1)S(1)}, u32[]{:S(2)}, u32[]{:S(2)}) collective-permute-start(bf16[16,512]{1,0:T(8,128)(2,1)S(1)} %slice.64), channel_id=1, source_target_pairs={{0,16},{8,24},{16,32},{24,40},{32,48},{40,56},{48,64},{56,72},{64,... | collective-permute-start | bytes 49160 | tf_op jit(solution)/shard_map/ppermute | solution.py:259
  6.7 1.3 %collective-permute-start.4 = (bf16[256,768]{1,0:T(8,128)(2,1)S(1)}, bf16[256,768]{1,0:T(8,128)(2,1)S(1)}, u32[]{:S(2)}, u32[]{:S(2)}) collective-permute-start(bf16[256,768]{1,0:T(8,128)(2,1)S(1)} %pad_maximum_fusion.1.own), channel_id=1, source_target_pairs={{0,16},{8,72},{16,32},{24,88},{32,48},{40,104},{48,0},{56,120},{64... | collective-permute-start | bytes 1179656 | tf_op jit(solution)/shard_map/ppermute | solution.py:25
  8.0 0.8 collective-permute-start.5
  8.9 2.0 %collective-permute-start.2 = (bf16[528,512]{1,0:T(8,128)(2,1)S(1)}, bf16[528,512]{1,0:T(8,128)(2,1)S(1)}, u32[]{:S(2)}, u32[]{:S(2)}) collective-permute-start(bf16[528,512]{1,0:T(8,128)(2,1)S(1)} %pad_maximum_fusion.refs_0_), channel_id=1, source_target_pairs={{0,1},{1,2},{2,3},{3,4},{4,5},{5,6},{6,7},{7,0},{8,15},{9,8},{10,9... | collective-permute-start | bytes 1622024 | tf_op jit(solution)/shard_map/ppermute | solution.py:34
  10.9 3.7 %collective-permute-done.4.before = bf16[256,768]{1,0:T(8,128)(2,1)S(1)} collective-permute-done((bf16[256,768]{1,0:T(8,128)(2,1)S(1)}, bf16[256,768]{1,0:T(8,128)(2,1)S(1)}, u32[]{:S(2)}, u32[]{:S(2)}) %collective-permute-start.4) | collective-permute-done | bytes 393248 | tf_op jit(solution)/shard_map/ppermute | solution.py:25
  14.6 1.3 %collective-permute-start.11 = (bf16[128,768]{1,0:T(8,128)(2,1)S(1)}, bf16[128,768]{1,0:T(8,128)(2,1)S(1)}, u32[]{:S(2)}, u32[]{:S(2)}) collective-permute-start(bf16[128,768]{1,0:T(8,128)(2,1)S(1)} %slice.68), channel_id=1, source_target_pairs={{0,16},{8,72},{16,32},{24,88},{32,48},{40,104},{48,0},{56,120},{64... | collective-permute-start | bytes 589832 | tf_op jit(solution)/shard_map/ppermute | solution.py:25
  15.9 0.9 collective-permute-start.12
  16.8 5.4 %collective-permute-done.2.refs_1_ = bf16[528,512]{1,0:T(8,128)(2,1)S(1)} collective-permute-done((bf16[528,512]{1,0:T(8,128)(2,1)S(1)}, bf16[528,512]{1,0:T(8,128)(2,1)S(1)}, u32[]{:S(2)}, u32[]{:S(2)}) %collective-permute-start.2) | collective-permute-done | bytes 540704 | tf_op jit(solution)/shard_map/ppermute | solution.py:34
  22.3 1.7 %collective-permute-start.13 = (bf16[1024,512]{1,0:T(8,128)(2,1)S(1)}, bf16[1024,512]{1,0:T(8,128)(2,1)S(1)}, u32[]{:S(2)}, u32[]{:S(2)}) collective-permute-start(bf16[1024,512]{1,0:T(8,128)(2,1)S(1)} %get-tuple-element.37.refs_9_), channel_id=1, source_target_pairs={{0,64},{8,24},{16,80},{24,40},{32,96},{40,56},{48,112},{56,8},{64,... | collective-permute-start | bytes 3145736 | tf_op jit(solution)/shard_map/ppermute | solution.py:25
  24.0 1.7 %collective-permute-start.15 = (bf16[1024,512]{1,0:T(8,128)(2,1)S(1)}, bf16[1024,512]{1,0:T(8,128)(2,1)S(1)}, u32[]{:S(2)}, u32[]{:S(2)}) collective-permute-start(bf16[1024,512]{1,0:T(8,128)(2,1)S(1)} %get-tuple-element.37.refs_9_), channel_id=1, source_target_pairs={{0,192},{8,56},{16,208},{24,8},{32,224},{40,24},{48,240},{56,40},{... | collective-permute-start | bytes 3145736 | tf_op jit(solution)/shard_map/ppermute | solution.py:25
  25.6 0.9 collective-permute-start.8
  26.5 6.2 %collective-permute-done.6.refs_2_ = bf16[528,512]{1,0:T(8,128)(2,1)S(1)} collective-permute-done((bf16[528,512]{1,0:T(8,128)(2,1)S(1)}, bf16[528,512]{1,0:T(8,128)(2,1)S(1)}, u32[]{:S(2)}, u32[]{:S(2)}) %collective-permute-start.6) | collective-permute-done | bytes 540704 | tf_op jit(solution)/shard_map/ppermute | solution.py:34
  32.7 1.8 %collective-permute-start.9 = (bf16[528,512]{1,0:T(8,128)(2,1)S(1)}, bf16[528,512]{1,0:T(8,128)(2,1)S(1)}, u32[]{:S(2)}, u32[]{:S(2)}) collective-permute-start(bf16[528,512]{1,0:T(8,128)(2,1)S(1)} %collective-permute-done.6.refs_2_), channel_id=1, source_target_pairs={{0,8},{8,0},{1,9},{9,1},{2,10},{10,2},{3,11},{11,3},{4,12},{12,4},... | collective-permute-start | bytes 1622024 | tf_op jit(solution)/shard_map/ppermute | solution.py:14
  34.6 3.9 %collective-permute-done.13.refs_10_ = bf16[1024,512]{1,0:T(8,128)(2,1)S(1)} collective-permute-done((bf16[1024,512]{1,0:T(8,128)(2,1)S(1)}, bf16[1024,512]{1,0:T(8,128)(2,1)S(1)}, u32[]{:S(2)}, u32[]{:S(2)}) %collective-permute-start.13) | collective-permute-done | bytes 1048608 | tf_op jit(solution)/shard_map/ppermute | solution.py:25
  38.4 0.4 collective-permute-start.17
  38.9 2.9 %collective-permute-start.18 = (bf16[1024,256]{1,0:T(8,128)(2,1)S(1)}, bf16[1024,256]{1,0:T(8,128)(2,1)S(1)}, u32[]{:S(2)}, u32[]{:S(2)}) collective-permute-start(bf16[1024,256]{1,0:T(8,128)(2,1)S(1)} %get-tuple-element.38.refs_9_), channel_id=1, source_target_pairs={{0,192},{8,56},{16,208},{24,8},{32,224},{40,24},{48,240},{56,40},{... | collective-permute-start | bytes 1572872 | tf_op jit(solution)/shard_map/ppermute | solution.py:25
  41.9 0.3 collective-permute-start.14
  42.2 1.1 collective-permute-done.7.refs_3_
  43.3 3.0 %collective-permute-start.16 = (bf16[512,512]{1,0:T(8,128)(2,1)S(1)}, bf16[512,512]{1,0:T(8,128)(2,1)S(1)}, u32[]{:S(2)}, u32[]{:S(2)}) collective-permute-start(bf16[512,512]{1,0:T(8,128)(2,1)S(1)} %slice.71), channel_id=1, source_target_pairs={{0,192},{8,56},{16,208},{24,8},{32,224},{40,24},{48,240},{56,40},{... | collective-permute-start | bytes 1572872 | tf_op jit(solution)/shard_map/ppermute | solution.py:25
  46.4 0.5 collective-permute-start.10
  46.9 1.9 %collective-permute-done.17.refs_10_ = bf16[1024,256]{1,0:T(8,128)(2,1)S(1)} collective-permute-done((bf16[1024,256]{1,0:T(8,128)(2,1)S(1)}, bf16[1024,256]{1,0:T(8,128)(2,1)S(1)}, u32[]{:S(2)}, u32[]{:S(2)}) %collective-permute-start.17) | collective-permute-done | bytes 524320 | tf_op jit(solution)/shard_map/ppermute | solution.py:25
  48.8 6.5 %collective-permute-done.10.refs_4_ = bf16[528,256]{1,0:T(8,128)(2,1)S(1)} collective-permute-done((bf16[528,256]{1,0:T(8,128)(2,1)S(1)}, bf16[528,256]{1,0:T(8,128)(2,1)S(1)}, u32[]{:S(2)}, u32[]{:S(2)}) %collective-permute-start.10) | collective-permute-done | bytes 270368 | tf_op jit(solution)/shard_map/ppermute | solution.py:34
  55.3 0.8 copy-done.16
  56.2 0.7 copy-done.17
  57.0 1.3 %collective-permute-start.21 = (bf16[1024,256]{1,0:T(8,128)(2,1)S(1)}, bf16[1024,256]{1,0:T(8,128)(2,1)}, u32[]{:S(2)}, u32[]{:S(2)}) collective-permute-start(bf16[1024,256]{1,0:T(8,128)(2,1)S(1)} %get-tuple-element.38.refs_9_), channel_id=1, source_target_pairs={{0,128},{8,40},{16,144},{24,56},{32,160},{40,8},{48,176},{56,24},{... | collective-permute-start | bytes 1572872 | tf_op jit(solution)/shard_map/ppermute | solution.py:25
  58.6 0.7 copy-done.13
  59.4 8.5 %shard_map.65 = (f32[2,512,128]{2,1,0:T(8,128)S(1)}, f32[16,8,256]{2,1,0:T(8,128)S(1)}, f32[16,16,256]{2,1,0:T(8,128)}) custom-call(s32[5]{0:T(128)S(1)} %stack.23.place, bf16[528,512]{1,0:T(8,128)(2,1)} %copy-done.3, bf16[528,512]{1,0:T(8,128)(2,1)} %copy-done.7, bf16[528,512]{1,0:T(8,128)(2,1)} %copy-done.8, bf16[528,512]{1,0:T(8,128)(2,1)} %copy-done.4, ...), custom_call_target="tpu_custom_call" | custom-call | flops 2147483648 | bytes 5368709 | tf_op jit(solution)/shard_map/pallas_call | solution.py:223
  67.9 7.8 %all-to-all-start = ((f32[16,16,256]{2,1,0:T(8,128)}), f32[16,16,256]{2,1,0:T(8,128)S(1)}, u32[]{:S(2)}, u32[]{:S(2)}) async-start(f32[16,16,256]{2,1,0:T(8,128)} %get-tuple-element.47), calls=%async_computation | async-start | bytes 524288 | tf_op jit(solution)/shard_map/all_to_all | solution.py:328
  75.7 5.1 %shard_map.66.query = f32[512,256]{1,0:T(8,128)S(1)} custom-call(s32[5]{0:T(128)S(1)} %stack.23.place, bf16[528,512]{1,0:T(8,128)(2,1)} %copy-done.3, bf16[528,512]{1,0:T(8,128)(2,1)} %copy-done.7, bf16[528,512]{1,0:T(8,128)(2,1)} %copy-done.8, bf16[528,512]{1,0:T(8,128)(2,1)} %copy-done.4, bf16[528,256]{1,0:T(8,128)(2,1)} %copy-done.12, ...), custom_call_target="tpu_custom_call" | custom-call | flops 1073741824 | bytes 2684354 | tf_op jit(solution)/shard_map/pallas_call | solution.py:223
  80.8 2.3 %all-to-all-done.states = f32[16,16,256]{2,1,0:T(8,128)S(1)} async-done(((f32[16,16,256]{2,1,0:T(8,128)}), f32[16,16,256]{2,1,0:T(8,128)S(1)}, u32[]{:S(2)}, u32[]{:S(2)}) %all-to-all-start) | async-done | bytes 262176 | tf_op jit(solution)/shard_map/all_to_all | solution.py:328
  83.0 2.7 %shard_map.67 = (bf16[512,256]{1,0:T(8,128)(2,1)S(1)}, bf16[512,4096]{1,0:T(8,128)(2,1)S(1)}) custom-call(s32[5]{0:T(128)S(1)} %stack.23.place, bf16[512,4096]{1,0:T(8,128)(2,1)} %out_weight.1, f32[2,512,128]{2,1,0:T(8,128)S(1)} %get-tuple-element.43.signal, f32[512,256]{1,0:T(8,128)S(1)} %shard_map.66.query, ...), custom_call_target="tpu_custom_call" | custom-call | flops 8388608 | bytes 20971 | tf_op jit(solution)/shard_map/pallas_call | solution.py:223
  85.9 1.5 %collective-permute-done.22.given = bf16[512,256]{1,0:T(8,128)(2,1)S(1)} collective-permute-done((bf16[512,256]{1,0:T(8,128)(2,1)S(1)}, bf16[512,256]{1,0:T(8,128)(2,1)S(1)}, u32[]{:S(2)}, u32[]{:S(2)}) %collective-permute-start.22) | collective-permute-done | bytes 262176 | tf_op jit(solution)/shard_map/ppermute | solution.py:14
  87.4 1.8 %shard_map.68 = (bf16[512,256]{1,0:T(8,128)(2,1)S(1)}, bf16[512,512]{1,0:T(8,128)(2,1)S(1)}, bf16[512,512]{1,0:T(8,128)(2,1)S(1)}, bf16[512,512]{1,0:T(8,128)(2,1)S(1)}, bf16[256,512]{1,0:T(8,128)(2,1)S(1)}) custom-call(s32[5]{0:T(128)S(1)} %stack.23.place, bf16[512,256]{1,0:T(8,128)(2,1)S(1)} %get-tuple-element.48.mine, ...), custom_call_target="tpu_custom_call" | custom-call | flops 1610612736 | bytes 4026531 | tf_op jit(solution)/shard_map/pallas_call | solution.py:223
  89.2 2.7 %collective-permute-start.25 = (bf16[512,256]{1,0:T(8,128)(2,1)S(1)}, bf16[512,256]{1,0:T(8,128)(2,1)S(1)}, u32[]{:S(2)}, u32[]{:S(2)}) collective-permute-start(bf16[512,256]{1,0:T(8,128)(2,1)S(1)} %get-tuple-element.54), channel_id=1, source_target_pairs={{0,2},{1,3},{2,4},{3,5},{4,6},{5,7},{6,0},{7,1},{8,14},{9,15},{10,... | collective-permute-start | bytes 786440 | tf_op jit(solution)/shard_map/ppermute | solution.py:34
  91.9 2.6 %collective-permute-start.24 = (bf16[256,512]{1,0:T(8,128)(2,1)S(1)}, bf16[256,512]{1,0:T(8,128)(2,1)S(1)}, u32[]{:S(2)}, u32[]{:S(2)}) collective-permute-start(bf16[256,512]{1,0:T(8,128)(2,1)S(1)} %get-tuple-element.59), channel_id=1, source_target_pairs={{0,1},{1,2},{2,3},{3,4},{4,5},{5,6},{6,7},{7,0},{8,15},{9,8},{10,9... | collective-permute-start | bytes 786440 | tf_op jit(solution)/shard_map/ppermute | solution.py:34
  94.5 2.5 %collective-permute-start.23 = (bf16[256,512]{1,0:T(8,128)(2,1)S(1)}, bf16[256,512]{1,0:T(8,128)(2,1)S(1)}, u32[]{:S(2)}, u32[]{:S(2)}) collective-permute-start(bf16[256,512]{1,0:T(8,128)(2,1)S(1)} %get-tuple-element.60), channel_id=1, source_target_pairs={{0,1},{1,2},{2,3},{3,4},{4,5},{5,6},{6,7},{7,0},{8,15},{9,8},{10,9... | collective-permute-start | bytes 786440 | tf_op jit(solution)/shard_map/ppermute | solution.py:34
  97.1 2.8 %collective-permute-done.25 = bf16[512,256]{1,0:T(8,128)(2,1)S(1)} collective-permute-done((bf16[512,256]{1,0:T(8,128)(2,1)S(1)}, bf16[512,256]{1,0:T(8,128)(2,1)S(1)}, u32[]{:S(2)}, u32[]{:S(2)}) %collective-permute-start.25) | collective-permute-done | bytes 262176 | tf_op jit(solution)/shard_map/ppermute | solution.py:34
  100.0 4.5 %collective-permute-done.24 = bf16[256,512]{1,0:T(8,128)(2,1)S(1)} collective-permute-done((bf16[256,512]{1,0:T(8,128)(2,1)S(1)}, bf16[256,512]{1,0:T(8,128)(2,1)S(1)}, u32[]{:S(2)}, u32[]{:S(2)}) %collective-permute-start.24) | collective-permute-done | bytes 262176 | tf_op jit(solution)/shard_map/ppermute | solution.py:34
  104.5 0.3 collective-permute-start.27
  104.8 2.5 %collective-permute-done.23 = bf16[256,512]{1,0:T(8,128)(2,1)S(1)} collective-permute-done((bf16[256,512]{1,0:T(8,128)(2,1)S(1)}, bf16[256,512]{1,0:T(8,128)(2,1)S(1)}, u32[]{:S(2)}, u32[]{:S(2)}) %collective-permute-start.23) | collective-permute-done | bytes 262176 | tf_op jit(solution)/shard_map/ppermute | solution.py:34
  107.4 5.0 %collective-permute-done.27 = bf16[256,512]{1,0:T(8,128)(2,1)S(1)} collective-permute-done((bf16[256,512]{1,0:T(8,128)(2,1)S(1)}, bf16[256,512]{1,0:T(8,128)(2,1)S(1)}, u32[]{:S(2)}, u32[]{:S(2)}) %collective-permute-start.27) | collective-permute-done | bytes 262176 | tf_op jit(solution)/shard_map/ppermute | solution.py:34
  112.5 2.7 %collective-permute-done.26 = bf16[256,512]{1,0:T(8,128)(2,1)S(1)} collective-permute-done((bf16[256,512]{1,0:T(8,128)(2,1)S(1)}, bf16[256,512]{1,0:T(8,128)(2,1)S(1)}, u32[]{:S(2)}, u32[]{:S(2)}) %collective-permute-start.26) | collective-permute-done | bytes 262176 | tf_op jit(solution)/shard_map/ppermute | solution.py:34
  115.3 4.8 %collective-permute-done.29 = bf16[256,512]{1,0:T(8,128)(2,1)S(1)} collective-permute-done((bf16[256,512]{1,0:T(8,128)(2,1)S(1)}, bf16[256,512]{1,0:T(8,128)(2,1)S(1)}, u32[]{:S(2)}, u32[]{:S(2)}) %collective-permute-start.29) | collective-permute-done | bytes 262176 | tf_op jit(solution)/shard_map/ppermute | solution.py:34
  120.1 2.8 %collective-permute-done.28 = bf16[256,512]{1,0:T(8,128)(2,1)S(1)} collective-permute-done((bf16[256,512]{1,0:T(8,128)(2,1)S(1)}, bf16[256,512]{1,0:T(8,128)(2,1)S(1)}, u32[]{:S(2)}, u32[]{:S(2)}) %collective-permute-start.28) | collective-permute-done | bytes 262176 | tf_op jit(solution)/shard_map/ppermute | solution.py:34
  122.9 0.8 add_convert_fusion
  (83 shorter events, 1.9 us)
Async XLA Ops:
  0.0 58.3 %copy-start = (f32[3,3,512]{2,1,0:T(4,128)S(1)}, f32[3,3,512]{2,1,0:T(4,128)}, u32[]{:S(2)}) copy-start(f32[3,3,512]{2,1,0:T(4,128)} %param.8) | copy-start | bytes 55300
  0.0 1.7 %collective-permute-start = (bf16[256,512]{1,0:T(8,128)(2,1)}, bf16[256,512]{1,0:T(8,128)(2,1)S(1)}, u32[]{:S(2)}, u32[]{:S(2)}) collective-permute-start(bf16[256,512]{1,0:T(8,128)(2,1)} %param.6), channel_id=1, source_target_pairs={{0,8},{8,0},{1,9},{9,1},{2,10},{10,2},{3,11},{11,3},{4,12},{12,4},... | collective-permute-start | bytes 786440 | tf_op jit(solution)/shard_map/ppermute | solution.py:14
  1.8 4.7 %collective-permute-start.3 = (bf16[3,128,256]{2,1,0:T(8,128)(2,1)S(1)}, bf16[3,128,256]{2,1,0:T(8,128)(2,1)S(1)}, u32[]{:S(2)}, u32[]{:S(2)}) collective-permute-start(bf16[3,128,256]{2,1,0:T(8,128)(2,1)S(1)} %get-tuple-element.32), channel_id=1, source_target_pairs={{0,8},{8,0},{1,9},{9,1},{2,10},{10,2},{3,11},{11,3},{4,12},{12,4},... | collective-permute-start | bytes 589832 | tf_op jit(solution)/shard_map/ppermute | solution.py:14
  3.1 5.8 %collective-permute-start.1 = (bf16[16,512]{1,0:T(8,128)(2,1)S(1)}, bf16[16,512]{1,0:T(8,128)(2,1)S(1)}, u32[]{:S(2)}, u32[]{:S(2)}) collective-permute-start(bf16[16,512]{1,0:T(8,128)(2,1)S(1)} %slice.64), channel_id=1, source_target_pairs={{0,16},{8,24},{16,32},{24,40},{32,48},{40,56},{48,64},{56,72},{64,... | collective-permute-start | bytes 49160 | tf_op jit(solution)/shard_map/ppermute | solution.py:259
  6.7 7.9 %collective-permute-start.4 = (bf16[256,768]{1,0:T(8,128)(2,1)S(1)}, bf16[256,768]{1,0:T(8,128)(2,1)S(1)}, u32[]{:S(2)}, u32[]{:S(2)}) collective-permute-start(bf16[256,768]{1,0:T(8,128)(2,1)S(1)} %pad_maximum_fusion.1.own), channel_id=1, source_target_pairs={{0,16},{8,72},{16,32},{24,88},{32,48},{40,104},{48,0},{56,120},{64... | collective-permute-start | bytes 1179656 | tf_op jit(solution)/shard_map/ppermute | solution.py:25
  8.0 7.9 %collective-permute-start.5 = (bf16[256,768]{1,0:T(8,128)(2,1)S(1)}, bf16[256,768]{1,0:T(8,128)(2,1)S(1)}, u32[]{:S(2)}, u32[]{:S(2)}) collective-permute-start(bf16[256,768]{1,0:T(8,128)(2,1)S(1)} %pad_maximum_fusion.1.own), channel_id=1, source_target_pairs={{0,48},{8,200},{16,0},{24,216},{32,16},{40,232},{48,32},{56,248},{... | collective-permute-start | bytes 1179656 | tf_op jit(solution)/shard_map/ppermute | solution.py:25
  8.9 13.4 %copy-start.3 = (bf16[528,512]{1,0:T(8,128)(2,1)}, bf16[528,512]{1,0:T(8,128)(2,1)S(1)}, u32[]{:S(2)}) copy-start(bf16[528,512]{1,0:T(8,128)(2,1)S(1)} %pad_maximum_fusion.refs_0_) | copy-start | bytes 1622020
  8.9 13.3 %collective-permute-start.2 = (bf16[528,512]{1,0:T(8,128)(2,1)S(1)}, bf16[528,512]{1,0:T(8,128)(2,1)S(1)}, u32[]{:S(2)}, u32[]{:S(2)}) collective-permute-start(bf16[528,512]{1,0:T(8,128)(2,1)S(1)} %pad_maximum_fusion.refs_0_), channel_id=1, source_target_pairs={{0,1},{1,2},{2,3},{3,4},{4,5},{5,6},{6,7},{7,0},{8,15},{9,8},{10,9... | collective-permute-start | bytes 1622024 | tf_op jit(solution)/shard_map/ppermute | solution.py:34
  14.6 7.6 %collective-permute-start.11 = (bf16[128,768]{1,0:T(8,128)(2,1)S(1)}, bf16[128,768]{1,0:T(8,128)(2,1)S(1)}, u32[]{:S(2)}, u32[]{:S(2)}) collective-permute-start(bf16[128,768]{1,0:T(8,128)(2,1)S(1)} %slice.68), channel_id=1, source_target_pairs={{0,16},{8,72},{16,32},{24,88},{32,48},{40,104},{48,0},{56,120},{64... | collective-permute-start | bytes 589832 | tf_op jit(solution)/shard_map/ppermute | solution.py:25
  15.9 6.3 %collective-permute-start.12 = (bf16[128,768]{1,0:T(8,128)(2,1)S(1)}, bf16[128,768]{1,0:T(8,128)(2,1)S(1)}, u32[]{:S(2)}, u32[]{:S(2)}) collective-permute-start(bf16[128,768]{1,0:T(8,128)(2,1)S(1)} %slice.69), channel_id=1, source_target_pairs={{0,48},{8,200},{16,0},{24,216},{32,16},{40,232},{48,32},{56,248},{... | collective-permute-start | bytes 589832 | tf_op jit(solution)/shard_map/ppermute | solution.py:25
  22.2 16.7 %copy-start.7 = (bf16[528,512]{1,0:T(8,128)(2,1)}, bf16[528,512]{1,0:T(8,128)(2,1)S(1)}, u32[]{:S(2)}) copy-start(bf16[528,512]{1,0:T(8,128)(2,1)S(1)} %collective-permute-done.2.refs_1_) | copy-start | bytes 1622020
  22.2 10.6 %collective-permute-start.6 = (bf16[528,512]{1,0:T(8,128)(2,1)S(1)}, bf16[528,512]{1,0:T(8,128)(2,1)S(1)}, u32[]{:S(2)}, u32[]{:S(2)}) collective-permute-start(bf16[528,512]{1,0:T(8,128)(2,1)S(1)} %collective-permute-done.2.refs_1_), channel_id=1, source_target_pairs={{0,1},{1,2},{2,3},{3,4},{4,5},{5,6},{6,7},{7,0},{8,15},{9,8},{10,9... | collective-permute-start | bytes 1622024 | tf_op jit(solution)/shard_map/ppermute | solution.py:34
  22.3 24.0 %copy-start.1 = (bf16[1024,512]{1,0:T(8,128)(2,1)}, bf16[1024,512]{1,0:T(8,128)(2,1)S(1)}, u32[]{:S(2)}) copy-start(bf16[1024,512]{1,0:T(8,128)(2,1)S(1)} %get-tuple-element.37.refs_9_) | copy-start | bytes 3145732
  22.3 34.7 %copy-start.2 = (bf16[1024,256]{1,0:T(8,128)(2,1)}, bf16[1024,256]{1,0:T(8,128)(2,1)S(1)}, u32[]{:S(2)}) copy-start(bf16[1024,256]{1,0:T(8,128)(2,1)S(1)} %get-tuple-element.38.refs_9_) | copy-start | bytes 1572868
  22.3 16.1 %collective-permute-start.13 = (bf16[1024,512]{1,0:T(8,128)(2,1)S(1)}, bf16[1024,512]{1,0:T(8,128)(2,1)S(1)}, u32[]{:S(2)}, u32[]{:S(2)}) collective-permute-start(bf16[1024,512]{1,0:T(8,128)(2,1)S(1)} %get-tuple-element.37.refs_9_), channel_id=1, source_target_pairs={{0,64},{8,24},{16,80},{24,40},{32,96},{40,56},{48,112},{56,8},{64,... | collective-permute-start | bytes 3145736 | tf_op jit(solution)/shard_map/ppermute | solution.py:25
  24.0 14.9 %collective-permute-start.15 = (bf16[1024,512]{1,0:T(8,128)(2,1)S(1)}, bf16[1024,512]{1,0:T(8,128)(2,1)S(1)}, u32[]{:S(2)}, u32[]{:S(2)}) collective-permute-start(bf16[1024,512]{1,0:T(8,128)(2,1)S(1)} %get-tuple-element.37.refs_9_), channel_id=1, source_target_pairs={{0,192},{8,56},{16,208},{24,8},{32,224},{40,24},{48,240},{56,40},{... | collective-permute-start | bytes 3145736 | tf_op jit(solution)/shard_map/ppermute | solution.py:25
  25.6 16.2 %collective-permute-start.8 = (bf16[528,512]{1,0:T(8,128)(2,1)S(1)}, bf16[528,512]{1,0:T(8,128)(2,1)S(1)}, u32[]{:S(2)}, u32[]{:S(2)}) collective-permute-start(bf16[528,512]{1,0:T(8,128)(2,1)S(1)} %collective-permute-done.2.refs_1_), channel_id=1, source_target_pairs={{0,8},{8,0},{1,9},{9,1},{2,10},{10,2},{3,11},{11,3},{4,12},{12,4},... | collective-permute-start | bytes 1622024 | tf_op jit(solution)/shard_map/ppermute | solution.py:14
  32.7 13.6 %copy-start.8 = (bf16[528,512]{1,0:T(8,128)(2,1)}, bf16[528,512]{1,0:T(8,128)(2,1)S(1)}, u32[]{:S(2)}) copy-start(bf16[528,512]{1,0:T(8,128)(2,1)S(1)} %collective-permute-done.6.refs_2_) | copy-start | bytes 1622020
  32.7 10.6 %collective-permute-start.7 = (bf16[528,512]{1,0:T(8,128)(2,1)S(1)}, bf16[528,512]{1,0:T(8,128)(2,1)S(1)}, u32[]{:S(2)}, u32[]{:S(2)}) collective-permute-start(bf16[528,512]{1,0:T(8,128)(2,1)S(1)} %collective-permute-done.6.refs_2_), channel_id=1, source_target_pairs={{0,1},{1,2},{2,3},{3,4},{4,5},{5,6},{6,7},{7,0},{8,15},{9,8},{10,9... | collective-permute-start | bytes 1622024 | tf_op jit(solution)/shard_map/ppermute | solution.py:34
  32.7 13.6 %collective-permute-start.9 = (bf16[528,512]{1,0:T(8,128)(2,1)S(1)}, bf16[528,512]{1,0:T(8,128)(2,1)S(1)}, u32[]{:S(2)}, u32[]{:S(2)}) collective-permute-start(bf16[528,512]{1,0:T(8,128)(2,1)S(1)} %collective-permute-done.6.refs_2_), channel_id=1, source_target_pairs={{0,8},{8,0},{1,9},{9,1},{2,10},{10,2},{3,11},{11,3},{4,12},{12,4},... | collective-permute-start | bytes 1622024 | tf_op jit(solution)/shard_map/ppermute | solution.py:14
  38.4 16.9 %copy-start.5 = (bf16[1024,512]{1,0:T(8,128)(2,1)}, bf16[1024,512]{1,0:T(8,128)(2,1)S(1)}, u32[]{:S(2)}) copy-start(bf16[1024,512]{1,0:T(8,128)(2,1)S(1)} %collective-permute-done.13.refs_10_) | copy-start | bytes 3145732
  38.4 10.4 %collective-permute-start.17 = (bf16[1024,256]{1,0:T(8,128)(2,1)S(1)}, bf16[1024,256]{1,0:T(8,128)(2,1)S(1)}, u32[]{:S(2)}, u32[]{:S(2)}) collective-permute-start(bf16[1024,256]{1,0:T(8,128)(2,1)S(1)} %get-tuple-element.38.refs_9_), channel_id=1, source_target_pairs={{0,64},{8,24},{16,80},{24,40},{32,96},{40,56},{48,112},{56,8},{64,... | collective-permute-start | bytes 1572872 | tf_op jit(solution)/shard_map/ppermute | solution.py:25
  38.8 19.5 %copy-start.18 = (f32[16,512]{1,0:T(8,128)S(1)}, f32[16,512]{1,0:T(8,128)}, u32[]{:S(2)}) copy-start(f32[16,512]{1,0:T(8,128)} %param.9) | copy-start | bytes 98308
  38.8 19.5 %copy-start.19 = (f32[16,512]{1,0:T(8,128)S(1)}, f32[16,512]{1,0:T(8,128)}, u32[]{:S(2)}) copy-start(f32[16,512]{1,0:T(8,128)} %param.10) | copy-start | bytes 98308
  38.9 17.2 %copy-start.6 = (bf16[1024,512]{1,0:T(8,128)(2,1)}, bf16[1024,512]{1,0:T(8,128)(2,1)S(1)}, u32[]{:S(2)}) copy-start(bf16[1024,512]{1,0:T(8,128)(2,1)S(1)} %collective-permute-done.15.refs_11_) | copy-start | bytes 3145732
  38.9 9.9 %collective-permute-start.18 = (bf16[1024,256]{1,0:T(8,128)(2,1)S(1)}, bf16[1024,256]{1,0:T(8,128)(2,1)S(1)}, u32[]{:S(2)}, u32[]{:S(2)}) collective-permute-start(bf16[1024,256]{1,0:T(8,128)(2,1)S(1)} %get-tuple-element.38.refs_9_), channel_id=1, source_target_pairs={{0,192},{8,56},{16,208},{24,8},{32,224},{40,24},{48,240},{56,40},{... | collective-permute-start | bytes 1572872 | tf_op jit(solution)/shard_map/ppermute | solution.py:25
  41.9 14.3 %copy-start.9 = (bf16[528,512]{1,0:T(8,128)(2,1)}, bf16[528,512]{1,0:T(8,128)(2,1)S(1)}, u32[]{:S(2)}) copy-start(bf16[528,512]{1,0:T(8,128)(2,1)S(1)} %collective-permute-done.8.refs_5_) | copy-start | bytes 1622020
  41.9 13.4 %collective-permute-start.14 = (bf16[512,512]{1,0:T(8,128)(2,1)S(1)}, bf16[512,512]{1,0:T(8,128)(2,1)S(1)}, u32[]{:S(2)}, u32[]{:S(2)}) collective-permute-start(bf16[512,512]{1,0:T(8,128)(2,1)S(1)} %slice.70), channel_id=1, source_target_pairs={{0,64},{8,24},{16,80},{24,40},{32,96},{40,56},{48,112},{56,8},{64,... | collective-permute-start | bytes 1572872 | tf_op jit(solution)/shard_map/ppermute | solution.py:25
  43.3 15.2 %copy-start.4 = (bf16[528,512]{1,0:T(8,128)(2,1)}, bf16[528,512]{1,0:T(8,128)(2,1)S(1)}, u32[]{:S(2)}) copy-start(bf16[528,512]{1,0:T(8,128)(2,1)S(1)} %collective-permute-done.7.refs_3_) | copy-start | bytes 1622020
  43.3 12.8 %collective-permute-start.16 = (bf16[512,512]{1,0:T(8,128)(2,1)S(1)}, bf16[512,512]{1,0:T(8,128)(2,1)S(1)}, u32[]{:S(2)}, u32[]{:S(2)}) collective-permute-start(bf16[512,512]{1,0:T(8,128)(2,1)S(1)} %slice.71), channel_id=1, source_target_pairs={{0,192},{8,56},{16,208},{24,8},{32,224},{40,24},{48,240},{56,40},{... | collective-permute-start | bytes 1572872 | tf_op jit(solution)/shard_map/ppermute | solution.py:25
  46.4 9.9 %copy-start.10 = (bf16[528,512]{1,0:T(8,128)(2,1)}, bf16[528,512]{1,0:T(8,128)(2,1)S(1)}, u32[]{:S(2)}) copy-start(bf16[528,512]{1,0:T(8,128)(2,1)S(1)} %collective-permute-done.9.refs_6_) | copy-start | bytes 1622020
  46.4 8.9 %collective-permute-start.10 = (bf16[528,256]{1,0:T(8,128)(2,1)S(1)}, bf16[528,256]{1,0:T(8,128)(2,1)S(1)}, u32[]{:S(2)}, u32[]{:S(2)}) collective-permute-start(bf16[528,256]{1,0:T(8,128)(2,1)S(1)} %constant_dynamic-slice_fusion.1), channel_id=1, source_target_pairs={{0,1},{1,2},{2,3},{3,4},{4,5},{5,6},{6,7},{7,0},{8,15},{9,8},{10,9... | collective-permute-start | bytes 811016 | tf_op jit(solution)/shard_map/ppermute | solution.py:34
  48.8 9.7 %copy-start.14 = (bf16[1024,256]{1,0:T(8,128)(2,1)}, bf16[1024,256]{1,0:T(8,128)(2,1)S(1)}, u32[]{:S(2)}) copy-start(bf16[1024,256]{1,0:T(8,128)(2,1)S(1)} %collective-permute-done.17.refs_10_) | copy-start | bytes 1572868
  48.8 7.4 %copy-start.15 = (bf16[1024,256]{1,0:T(8,128)(2,1)}, bf16[1024,256]{1,0:T(8,128)(2,1)S(1)}, u32[]{:S(2)}) copy-start(bf16[1024,256]{1,0:T(8,128)(2,1)S(1)} %collective-permute-done.18.refs_11_) | copy-start | bytes 1572868
  55.3 3.3 %copy-start.12 = (bf16[528,256]{1,0:T(8,128)(2,1)}, bf16[528,256]{1,0:T(8,128)(2,1)S(1)}, u32[]{:S(2)}) copy-start(bf16[528,256]{1,0:T(8,128)(2,1)S(1)} %collective-permute-done.10.refs_4_) | copy-start | bytes 811012
  56.1 2.4 %collective-permute-start.19 = (bf16[528,512]{1,0:T(8,128)(2,1)S(1)}, bf16[528,512]{1,0:T(8,128)(2,1)S(1)}, u32[]{:S(2)}, u32[]{:S(2)}) collective-permute-start(bf16[528,512]{1,0:T(8,128)(2,1)S(1)} %collective-permute-done.7.refs_3_), channel_id=1, source_target_pairs={{0,8},{8,0},{1,9},{9,1},{2,10},{10,2},{3,11},{11,3},{4,12},{12,4},... | collective-permute-start | bytes 1622024 | tf_op jit(solution)/shard_map/ppermute | solution.py:14
  56.9 1.6 %collective-permute-start.20 = (bf16[528,256]{1,0:T(8,128)(2,1)S(1)}, bf16[528,256]{1,0:T(8,128)(2,1)S(1)}, u32[]{:S(2)}, u32[]{:S(2)}) collective-permute-start(bf16[528,256]{1,0:T(8,128)(2,1)S(1)} %collective-permute-done.10.refs_4_), channel_id=1, source_target_pairs={{0,8},{8,0},{1,9},{9,1},{2,10},{10,2},{3,11},{11,3},{4,12},{12,4},... | collective-permute-start | bytes 811016 | tf_op jit(solution)/shard_map/ppermute | solution.py:14
  57.0 18.7 %collective-permute-start.21 = (bf16[1024,256]{1,0:T(8,128)(2,1)S(1)}, bf16[1024,256]{1,0:T(8,128)(2,1)}, u32[]{:S(2)}, u32[]{:S(2)}) collective-permute-start(bf16[1024,256]{1,0:T(8,128)(2,1)S(1)} %get-tuple-element.38.refs_9_), channel_id=1, source_target_pairs={{0,128},{8,40},{16,144},{24,56},{32,160},{40,8},{48,176},{56,24},{... | collective-permute-start | bytes 1572872 | tf_op jit(solution)/shard_map/ppermute | solution.py:25
  67.9 15.2 %all-to-all-start = ((f32[16,16,256]{2,1,0:T(8,128)}), f32[16,16,256]{2,1,0:T(8,128)S(1)}, u32[]{:S(2)}, u32[]{:S(2)}) async-start(f32[16,16,256]{2,1,0:T(8,128)} %get-tuple-element.47), calls=%async_computation | async-start | bytes 524288 | tf_op jit(solution)/shard_map/all_to_all | solution.py:328
  85.8 1.6 %collective-permute-start.22 = (bf16[512,256]{1,0:T(8,128)(2,1)S(1)}, bf16[512,256]{1,0:T(8,128)(2,1)S(1)}, u32[]{:S(2)}, u32[]{:S(2)}) collective-permute-start(bf16[512,256]{1,0:T(8,128)(2,1)S(1)} %get-tuple-element.48.mine), channel_id=1, source_target_pairs={{0,8},{8,0},{1,9},{9,1},{2,10},{10,2},{3,11},{11,3},{4,12},{12,4},... | collective-permute-start | bytes 786440 | tf_op jit(solution)/shard_map/ppermute | solution.py:14
  89.2 10.6 %collective-permute-start.25 = (bf16[512,256]{1,0:T(8,128)(2,1)S(1)}, bf16[512,256]{1,0:T(8,128)(2,1)S(1)}, u32[]{:S(2)}, u32[]{:S(2)}) collective-permute-start(bf16[512,256]{1,0:T(8,128)(2,1)S(1)} %get-tuple-element.54), channel_id=1, source_target_pairs={{0,2},{1,3},{2,4},{3,5},{4,6},{5,7},{6,0},{7,1},{8,14},{9,15},{10,... | collective-permute-start | bytes 786440 | tf_op jit(solution)/shard_map/ppermute | solution.py:34
  91.9 12.5 %collective-permute-start.24 = (bf16[256,512]{1,0:T(8,128)(2,1)S(1)}, bf16[256,512]{1,0:T(8,128)(2,1)S(1)}, u32[]{:S(2)}, u32[]{:S(2)}) collective-permute-start(bf16[256,512]{1,0:T(8,128)(2,1)S(1)} %get-tuple-element.59), channel_id=1, source_target_pairs={{0,1},{1,2},{2,3},{3,4},{4,5},{5,6},{6,7},{7,0},{8,15},{9,8},{10,9... | collective-permute-start | bytes 786440 | tf_op jit(solution)/shard_map/ppermute | solution.py:34
  94.5 12.7 %collective-permute-start.23 = (bf16[256,512]{1,0:T(8,128)(2,1)S(1)}, bf16[256,512]{1,0:T(8,128)(2,1)S(1)}, u32[]{:S(2)}, u32[]{:S(2)}) collective-permute-start(bf16[256,512]{1,0:T(8,128)(2,1)S(1)} %get-tuple-element.60), channel_id=1, source_target_pairs={{0,1},{1,2},{2,3},{3,4},{4,5},{5,6},{6,7},{7,0},{8,15},{9,8},{10,9... | collective-permute-start | bytes 786440 | tf_op jit(solution)/shard_map/ppermute | solution.py:34
  104.5 7.9 %collective-permute-start.27 = (bf16[256,512]{1,0:T(8,128)(2,1)S(1)}, bf16[256,512]{1,0:T(8,128)(2,1)S(1)}, u32[]{:S(2)}, u32[]{:S(2)}) collective-permute-start(bf16[256,512]{1,0:T(8,128)(2,1)S(1)} %slice_add_fusion.1), channel_id=1, source_target_pairs={{0,1},{1,2},{2,3},{3,4},{4,5},{5,6},{6,7},{7,0},{8,15},{9,8},{10,9... | collective-permute-start | bytes 786440 | tf_op jit(solution)/shard_map/ppermute | solution.py:34
  107.3 7.9 %collective-permute-start.26 = (bf16[256,512]{1,0:T(8,128)(2,1)S(1)}, bf16[256,512]{1,0:T(8,128)(2,1)S(1)}, u32[]{:S(2)}, u32[]{:S(2)}) collective-permute-start(bf16[256,512]{1,0:T(8,128)(2,1)S(1)} %slice_add_fusion), channel_id=1, source_target_pairs={{0,1},{1,2},{2,3},{3,4},{4,5},{5,6},{6,7},{7,0},{8,15},{9,8},{10,9... | collective-permute-start | bytes 786440 | tf_op jit(solution)/shard_map/ppermute | solution.py:34
  112.4 7.7 %collective-permute-start.29 = (bf16[256,512]{1,0:T(8,128)(2,1)S(1)}, bf16[256,512]{1,0:T(8,128)(2,1)S(1)}, u32[]{:S(2)}, u32[]{:S(2)}) collective-permute-start(bf16[256,512]{1,0:T(8,128)(2,1)S(1)} %slice_add_fusion.2), channel_id=1, source_target_pairs={{0,1},{1,2},{2,3},{3,4},{4,5},{5,6},{6,7},{7,0},{8,15},{9,8},{10,9... | collective-permute-start | bytes 786440 | tf_op jit(solution)/shard_map/ppermute | solution.py:34
  115.2 7.7 %collective-permute-start.28 = (bf16[256,512]{1,0:T(8,128)(2,1)S(1)}, bf16[256,512]{1,0:T(8,128)(2,1)S(1)}, u32[]{:S(2)}, u32[]{:S(2)}) collective-permute-start(bf16[256,512]{1,0:T(8,128)(2,1)S(1)} %slice_add_fusion.3), channel_id=1, source_target_pairs={{0,1},{1,2},{2,3},{3,4},{4,5},{5,6},{6,7},{7,0},{8,15},{9,8},{10,9... | collective-permute-start | bytes 786440 | tf_op jit(solution)/shard_map/ppermute | solution.py:34
  120.1 2.8 %collective-permute-start.30 = (bf16[256,512]{1,0:T(8,128)(2,1)S(1)}, bf16[256,512]{1,0:T(8,128)(2,1)S(1)}, u32[]{:S(2)}, u32[]{:S(2)}) collective-permute-start(bf16[256,512]{1,0:T(8,128)(2,1)S(1)} %collective-permute-done.29), channel_id=1, source_target_pairs={{0,8},{8,0},{1,9},{9,1},{2,10},{10,2},{3,11},{11,3},{4,12},{12,4},... | collective-permute-start | bytes 786440 | tf_op jit(solution)/shard_map/ppermute | solution.py:14
  (4 other events, 3.2 us)

commit v5 on v4

--- a/solution.py
+++ b/solution.py
@@ -322,7 +322,7 @@
         ],
         4 * positions * features * width,
         20,
-        14,
+        12,
         place, *gathered, *weights, taps, rates,
     )
     states = lax.all_to_all(end_state, ("y", "x"), 0, 0, tiled=True)

time: 125 us -> 124 us (level)
  local copies, waits for them, and re-layouts: 3.73 us -> 2.17 us
    unnamed x40 -> x34, local copies, waits for them, and re-layouts: 2.41 us -> 0.85 us
where the time goes in v5:
time: 124 us; the launch traced here: 123 us
  waiting for transfers between devices  58.7 us (47%)
  starting transfers between devices  41.7 us (34%)
  Pallas kernels  17.9 us (14%)
  other arithmetic  2.48 us (2%)
  local copies, waits for them, and re-layouts  2.17 us (2%)
    ppermute x11, waiting for transfers between devices, group_ring(): return lax.ppermute(block, ('core', 'chan'), pairs)  44.1 us
    pallas_call x4, Pallas kernels, on_device(): pl.pallas_call(kernel, out_shape=outs, in_specs=[smem] + [hbm] * copied +...  17.8 us
    ppermute x11, starting transfers between devices, chip_ring(): return lax.ppermute(block, ('y', 'x', 'core'), pairs)  15.5 us
    ppermute x11, starting transfers between devices, group_ring(): return lax.ppermute(block, ('core', 'chan'), pairs)  11.6 us
    ppermute x11, waiting for transfers between devices, chip_ring(): return lax.ppermute(block, ('y', 'x', 'core'), pairs)  9.49 us
    all_to_all x1, starting transfers between devices, shards(): states = lax.all_to_all(end_state, ('y', 'x'), 0, 0, tiled=True)  7.64 us
    ppermute x8, starting transfers between devices, swap_cores(): return lax.ppermute(block, 'core', [(0, 1), (1, 0)])  3.59 us
    ppermute x1, starting transfers between devices, shards(): lax.ppermute(block[-HALO:], ('y', 'x', 'core'), [(i, i + 2) for i in rang...  3.41 us
  transfers between devices with their start and end apart: 32, of which 18 were waited for; matrix products, arithmetic and copies ran while one was open for 2% of the time, Pallas kernels for 11%

profile of v5, /device:TPU:2, one launch (start us, length us, event | category | flops | bytes accessed | tf_op | source)
XLA Modules:
  0.0 123.4 jit_solution(16801151921704616821)
XLA Ops:
  0.0 1.1 constant_dynamic-slice_fusion.3
  1.1 0.7 collective-permute-done
  1.9 1.2 maximum_select_fusion
  3.1 3.4 %collective-permute-start.1 = (bf16[16,512]{1,0:T(8,128)(2,1)S(1)}, bf16[16,512]{1,0:T(8,128)(2,1)S(1)}, u32[]{:S(2)}, u32[]{:S(2)}) collective-permute-start(bf16[16,512]{1,0:T(8,128)(2,1)S(1)} %slice.64), channel_id=1, source_target_pairs={{0,16},{8,24},{16,32},{24,40},{32,48},{40,56},{48,64},{56,72},{64,... | collective-permute-start | bytes 49160 | tf_op jit(solution)/shard_map/ppermute | solution.py:259
  6.7 1.3 %collective-permute-start.4 = (bf16[256,768]{1,0:T(8,128)(2,1)S(1)}, bf16[256,768]{1,0:T(8,128)(2,1)S(1)}, u32[]{:S(2)}, u32[]{:S(2)}) collective-permute-start(bf16[256,768]{1,0:T(8,128)(2,1)S(1)} %pad_maximum_fusion.1.own), channel_id=1, source_target_pairs={{0,16},{8,72},{16,32},{24,88},{32,48},{40,104},{48,0},{56,120},{64... | collective-permute-start | bytes 1179656 | tf_op jit(solution)/shard_map/ppermute | solution.py:25
  8.0 0.8 collective-permute-start.5
  8.9 2.0 %collective-permute-start.2 = (bf16[528,512]{1,0:T(8,128)(2,1)S(1)}, bf16[528,512]{1,0:T(8,128)(2,1)S(1)}, u32[]{:S(2)}, u32[]{:S(2)}) collective-permute-start(bf16[528,512]{1,0:T(8,128)(2,1)S(1)} %pad_maximum_fusion.refs_0_), channel_id=1, source_target_pairs={{0,1},{1,2},{2,3},{3,4},{4,5},{5,6},{6,7},{7,0},{8,15},{9,8},{10,9... | collective-permute-start | bytes 1622024 | tf_op jit(solution)/shard_map/ppermute | solution.py:34
  10.9 3.7 %collective-permute-done.4.before = bf16[256,768]{1,0:T(8,128)(2,1)S(1)} collective-permute-done((bf16[256,768]{1,0:T(8,128)(2,1)S(1)}, bf16[256,768]{1,0:T(8,128)(2,1)S(1)}, u32[]{:S(2)}, u32[]{:S(2)}) %collective-permute-start.4) | collective-permute-done | bytes 393248 | tf_op jit(solution)/shard_map/ppermute | solution.py:25
  14.6 1.3 %collective-permute-start.11 = (bf16[128,768]{1,0:T(8,128)(2,1)S(1)}, bf16[128,768]{1,0:T(8,128)(2,1)S(1)}, u32[]{:S(2)}, u32[]{:S(2)}) collective-permute-start(bf16[128,768]{1,0:T(8,128)(2,1)S(1)} %slice.68), channel_id=1, source_target_pairs={{0,16},{8,72},{16,32},{24,88},{32,48},{40,104},{48,0},{56,120},{64... | collective-permute-start | bytes 589832 | tf_op jit(solution)/shard_map/ppermute | solution.py:25
  15.9 0.9 collective-permute-start.12
  16.8 5.4 %collective-permute-done.2.refs_1_ = bf16[528,512]{1,0:T(8,128)(2,1)S(1)} collective-permute-done((bf16[528,512]{1,0:T(8,128)(2,1)S(1)}, bf16[528,512]{1,0:T(8,128)(2,1)S(1)}, u32[]{:S(2)}, u32[]{:S(2)}) %collective-permute-start.2) | collective-permute-done | bytes 540704 | tf_op jit(solution)/shard_map/ppermute | solution.py:34
  22.3 1.7 %collective-permute-start.13 = (bf16[1024,512]{1,0:T(8,128)(2,1)S(1)}, bf16[1024,512]{1,0:T(8,128)(2,1)S(1)}, u32[]{:S(2)}, u32[]{:S(2)}) collective-permute-start(bf16[1024,512]{1,0:T(8,128)(2,1)S(1)} %get-tuple-element.37.refs_9_), channel_id=1, source_target_pairs={{0,64},{8,24},{16,80},{24,40},{32,96},{40,56},{48,112},{56,8},{64,... | collective-permute-start | bytes 3145736 | tf_op jit(solution)/shard_map/ppermute | solution.py:25
  24.0 1.7 %collective-permute-start.15 = (bf16[1024,512]{1,0:T(8,128)(2,1)S(1)}, bf16[1024,512]{1,0:T(8,128)(2,1)S(1)}, u32[]{:S(2)}, u32[]{:S(2)}) collective-permute-start(bf16[1024,512]{1,0:T(8,128)(2,1)S(1)} %get-tuple-element.37.refs_9_), channel_id=1, source_target_pairs={{0,192},{8,56},{16,208},{24,8},{32,224},{40,24},{48,240},{56,40},{... | collective-permute-start | bytes 3145736 | tf_op jit(solution)/shard_map/ppermute | solution.py:25
  25.6 0.9 collective-permute-start.8
  26.5 6.2 %collective-permute-done.6.refs_2_ = bf16[528,512]{1,0:T(8,128)(2,1)S(1)} collective-permute-done((bf16[528,512]{1,0:T(8,128)(2,1)S(1)}, bf16[528,512]{1,0:T(8,128)(2,1)S(1)}, u32[]{:S(2)}, u32[]{:S(2)}) %collective-permute-start.6) | collective-permute-done | bytes 540704 | tf_op jit(solution)/shard_map/ppermute | solution.py:34
  32.7 1.8 %collective-permute-start.9 = (bf16[528,512]{1,0:T(8,128)(2,1)S(1)}, bf16[528,512]{1,0:T(8,128)(2,1)S(1)}, u32[]{:S(2)}, u32[]{:S(2)}) collective-permute-start(bf16[528,512]{1,0:T(8,128)(2,1)S(1)} %collective-permute-done.6.refs_2_), channel_id=1, source_target_pairs={{0,8},{8,0},{1,9},{9,1},{2,10},{10,2},{3,11},{11,3},{4,12},{12,4},... | collective-permute-start | bytes 1622024 | tf_op jit(solution)/shard_map/ppermute | solution.py:14
  34.6 3.9 %collective-permute-done.13.refs_10_ = bf16[1024,512]{1,0:T(8,128)(2,1)S(1)} collective-permute-done((bf16[1024,512]{1,0:T(8,128)(2,1)S(1)}, bf16[1024,512]{1,0:T(8,128)(2,1)S(1)}, u32[]{:S(2)}, u32[]{:S(2)}) %collective-permute-start.13) | collective-permute-done | bytes 1048608 | tf_op jit(solution)/shard_map/ppermute | solution.py:25
  38.4 0.4 collective-permute-start.17
  38.9 2.9 %collective-permute-start.18 = (bf16[1024,256]{1,0:T(8,128)(2,1)S(1)}, bf16[1024,256]{1,0:T(8,128)(2,1)S(1)}, u32[]{:S(2)}, u32[]{:S(2)}) collective-permute-start(bf16[1024,256]{1,0:T(8,128)(2,1)S(1)} %get-tuple-element.38.refs_9_), channel_id=1, source_target_pairs={{0,192},{8,56},{16,208},{24,8},{32,224},{40,24},{48,240},{56,40},{... | collective-permute-start | bytes 1572872 | tf_op jit(solution)/shard_map/ppermute | solution.py:25
  41.9 0.3 collective-permute-start.14
  42.2 1.1 collective-permute-done.7.refs_3_
  43.3 3.0 %collective-permute-start.16 = (bf16[512,512]{1,0:T(8,128)(2,1)S(1)}, bf16[512,512]{1,0:T(8,128)(2,1)S(1)}, u32[]{:S(2)}, u32[]{:S(2)}) collective-permute-start(bf16[512,512]{1,0:T(8,128)(2,1)S(1)} %slice.71), channel_id=1, source_target_pairs={{0,192},{8,56},{16,208},{24,8},{32,224},{40,24},{48,240},{56,40},{... | collective-permute-start | bytes 1572872 | tf_op jit(solution)/shard_map/ppermute | solution.py:25
  46.4 0.5 collective-permute-start.10
  46.9 1.9 %collective-permute-done.17.refs_10_ = bf16[1024,256]{1,0:T(8,128)(2,1)S(1)} collective-permute-done((bf16[1024,256]{1,0:T(8,128)(2,1)S(1)}, bf16[1024,256]{1,0:T(8,128)(2,1)S(1)}, u32[]{:S(2)}, u32[]{:S(2)}) %collective-permute-start.17) | collective-permute-done | bytes 524320 | tf_op jit(solution)/shard_map/ppermute | solution.py:25
  48.8 6.5 %collective-permute-done.10.refs_4_ = bf16[528,256]{1,0:T(8,128)(2,1)S(1)} collective-permute-done((bf16[528,256]{1,0:T(8,128)(2,1)S(1)}, bf16[528,256]{1,0:T(8,128)(2,1)S(1)}, u32[]{:S(2)}, u32[]{:S(2)}) %collective-permute-start.10) | collective-permute-done | bytes 270368 | tf_op jit(solution)/shard_map/ppermute | solution.py:34
  55.4 0.6 collective-permute-start.20
  56.1 1.3 %collective-permute-start.21 = (bf16[1024,256]{1,0:T(8,128)(2,1)S(1)}, bf16[1024,256]{1,0:T(8,128)(2,1)}, u32[]{:S(2)}, u32[]{:S(2)}) collective-permute-start(bf16[1024,256]{1,0:T(8,128)(2,1)S(1)} %get-tuple-element.38.refs_9_), channel_id=1, source_target_pairs={{0,128},{8,40},{16,144},{24,56},{32,160},{40,8},{48,176},{56,24},{... | collective-permute-start | bytes 1572872 | tf_op jit(solution)/shard_map/ppermute | solution.py:25
  57.4 0.4 collective-permute-done.20.refs_8_
  57.9 0.8 copy-done.11
  58.6 8.2 %shard_map.65 = (f32[2,512,128]{2,1,0:T(8,128)S(1)}, f32[16,8,256]{2,1,0:T(8,128)S(1)}, f32[16,16,256]{2,1,0:T(8,128)}) custom-call(s32[5]{0:T(128)S(1)} %stack.23.place, bf16[528,512]{1,0:T(8,128)(2,1)} %copy-done.3, bf16[528,512]{1,0:T(8,128)(2,1)} %copy-done.7, bf16[528,512]{1,0:T(8,128)(2,1)} %copy-done.8, bf16[528,512]{1,0:T(8,128)(2,1)} %copy-done.4, ...), custom_call_target="tpu_custom_call" | custom-call | flops 2147483648 | bytes 5368709 | tf_op jit(solution)/shard_map/pallas_call | solution.py:223
  66.8 7.6 %all-to-all-start = ((f32[16,16,256]{2,1,0:T(8,128)}), f32[16,16,256]{2,1,0:T(8,128)S(1)}, u32[]{:S(2)}, u32[]{:S(2)}) async-start(f32[16,16,256]{2,1,0:T(8,128)} %get-tuple-element.47), calls=%async_computation | async-start | bytes 524288 | tf_op jit(solution)/shard_map/all_to_all | solution.py:328
  74.5 5.1 %shard_map.66.query = f32[512,256]{1,0:T(8,128)S(1)} custom-call(s32[5]{0:T(128)S(1)} %stack.23.place, bf16[528,512]{1,0:T(8,128)(2,1)} %copy-done.3, bf16[528,512]{1,0:T(8,128)(2,1)} %copy-done.7, bf16[528,512]{1,0:T(8,128)(2,1)} %copy-done.8, bf16[528,512]{1,0:T(8,128)(2,1)} %copy-done.4, bf16[528,256]{1,0:T(8,128)(2,1)} %copy-done.12, ...), custom_call_target="tpu_custom_call" | custom-call | flops 1073741824 | bytes 2684354 | tf_op jit(solution)/shard_map/pallas_call | solution.py:223
  79.5 2.6 %all-to-all-done.states = f32[16,16,256]{2,1,0:T(8,128)S(1)} async-done(((f32[16,16,256]{2,1,0:T(8,128)}), f32[16,16,256]{2,1,0:T(8,128)S(1)}, u32[]{:S(2)}, u32[]{:S(2)}) %all-to-all-start) | async-done | bytes 262176 | tf_op jit(solution)/shard_map/all_to_all | solution.py:328
  82.1 2.7 %shard_map.67 = (bf16[512,256]{1,0:T(8,128)(2,1)S(1)}, bf16[512,4096]{1,0:T(8,128)(2,1)S(1)}) custom-call(s32[5]{0:T(128)S(1)} %stack.23.place, bf16[512,4096]{1,0:T(8,128)(2,1)} %out_weight.1, f32[2,512,128]{2,1,0:T(8,128)S(1)} %get-tuple-element.43.signal, f32[512,256]{1,0:T(8,128)S(1)} %shard_map.66.query, ...), custom_call_target="tpu_custom_call" | custom-call | flops 8388608 | bytes 20971 | tf_op jit(solution)/shard_map/pallas_call | solution.py:223
  84.9 1.5 %collective-permute-done.22.given = bf16[512,256]{1,0:T(8,128)(2,1)S(1)} collective-permute-done((bf16[512,256]{1,0:T(8,128)(2,1)S(1)}, bf16[512,256]{1,0:T(8,128)(2,1)S(1)}, u32[]{:S(2)}, u32[]{:S(2)}) %collective-permute-start.22) | collective-permute-done | bytes 262176 | tf_op jit(solution)/shard_map/ppermute | solution.py:14
  86.4 1.8 %shard_map.68 = (bf16[512,256]{1,0:T(8,128)(2,1)S(1)}, bf16[512,512]{1,0:T(8,128)(2,1)S(1)}, bf16[512,512]{1,0:T(8,128)(2,1)S(1)}, bf16[512,512]{1,0:T(8,128)(2,1)S(1)}, bf16[256,512]{1,0:T(8,128)(2,1)S(1)}) custom-call(s32[5]{0:T(128)S(1)} %stack.23.place, bf16[512,256]{1,0:T(8,128)(2,1)S(1)} %get-tuple-element.48.mine, ...), custom_call_target="tpu_custom_call" | custom-call | flops 1610612736 | bytes 4026531 | tf_op jit(solution)/shard_map/pallas_call | solution.py:223
  88.3 3.3 %collective-permute-start.25 = (bf16[512,256]{1,0:T(8,128)(2,1)S(1)}, bf16[512,256]{1,0:T(8,128)(2,1)S(1)}, u32[]{:S(2)}, u32[]{:S(2)}) collective-permute-start(bf16[512,256]{1,0:T(8,128)(2,1)S(1)} %get-tuple-element.54), channel_id=1, source_target_pairs={{0,2},{1,3},{2,4},{3,5},{4,6},{5,7},{6,0},{7,1},{8,14},{9,15},{10,... | collective-permute-start | bytes 786440 | tf_op jit(solution)/shard_map/ppermute | solution.py:34
  91.7 2.0 %collective-permute-start.24 = (bf16[256,512]{1,0:T(8,128)(2,1)S(1)}, bf16[256,512]{1,0:T(8,128)(2,1)S(1)}, u32[]{:S(2)}, u32[]{:S(2)}) collective-permute-start(bf16[256,512]{1,0:T(8,128)(2,1)S(1)} %get-tuple-element.59), channel_id=1, source_target_pairs={{0,1},{1,2},{2,3},{3,4},{4,5},{5,6},{6,7},{7,0},{8,15},{9,8},{10,9... | collective-permute-start | bytes 786440 | tf_op jit(solution)/shard_map/ppermute | solution.py:34
  93.6 3.1 %collective-permute-start.23 = (bf16[256,512]{1,0:T(8,128)(2,1)S(1)}, bf16[256,512]{1,0:T(8,128)(2,1)S(1)}, u32[]{:S(2)}, u32[]{:S(2)}) collective-permute-start(bf16[256,512]{1,0:T(8,128)(2,1)S(1)} %get-tuple-element.60), channel_id=1, source_target_pairs={{0,1},{1,2},{2,3},{3,4},{4,5},{5,6},{6,7},{7,0},{8,15},{9,8},{10,9... | collective-permute-start | bytes 786440 | tf_op jit(solution)/shard_map/ppermute | solution.py:34
  96.8 2.8 %collective-permute-done.25 = bf16[512,256]{1,0:T(8,128)(2,1)S(1)} collective-permute-done((bf16[512,256]{1,0:T(8,128)(2,1)S(1)}, bf16[512,256]{1,0:T(8,128)(2,1)S(1)}, u32[]{:S(2)}, u32[]{:S(2)}) %collective-permute-start.25) | collective-permute-done | bytes 262176 | tf_op jit(solution)/shard_map/ppermute | solution.py:34
  99.7 4.5 %collective-permute-done.24 = bf16[256,512]{1,0:T(8,128)(2,1)S(1)} collective-permute-done((bf16[256,512]{1,0:T(8,128)(2,1)S(1)}, bf16[256,512]{1,0:T(8,128)(2,1)S(1)}, u32[]{:S(2)}, u32[]{:S(2)}) %collective-permute-start.24) | collective-permute-done | bytes 262176 | tf_op jit(solution)/shard_map/ppermute | solution.py:34
  104.2 0.3 collective-permute-start.27
  104.5 2.5 %collective-permute-done.23 = bf16[256,512]{1,0:T(8,128)(2,1)S(1)} collective-permute-done((bf16[256,512]{1,0:T(8,128)(2,1)S(1)}, bf16[256,512]{1,0:T(8,128)(2,1)S(1)}, u32[]{:S(2)}, u32[]{:S(2)}) %collective-permute-start.23) | collective-permute-done | bytes 262176 | tf_op jit(solution)/shard_map/ppermute | solution.py:34
  107.1 5.0 %collective-permute-done.27 = bf16[256,512]{1,0:T(8,128)(2,1)S(1)} collective-permute-done((bf16[256,512]{1,0:T(8,128)(2,1)S(1)}, bf16[256,512]{1,0:T(8,128)(2,1)S(1)}, u32[]{:S(2)}, u32[]{:S(2)}) %collective-permute-start.27) | collective-permute-done | bytes 262176 | tf_op jit(solution)/shard_map/ppermute | solution.py:34
  112.2 2.7 %collective-permute-done.26 = bf16[256,512]{1,0:T(8,128)(2,1)S(1)} collective-permute-done((bf16[256,512]{1,0:T(8,128)(2,1)S(1)}, bf16[256,512]{1,0:T(8,128)(2,1)S(1)}, u32[]{:S(2)}, u32[]{:S(2)}) %collective-permute-start.26) | collective-permute-done | bytes 262176 | tf_op jit(solution)/shard_map/ppermute | solution.py:34
  115.0 4.8 %collective-permute-done.29 = bf16[256,512]{1,0:T(8,128)(2,1)S(1)} collective-permute-done((bf16[256,512]{1,0:T(8,128)(2,1)S(1)}, bf16[256,512]{1,0:T(8,128)(2,1)S(1)}, u32[]{:S(2)}, u32[]{:S(2)}) %collective-permute-start.29) | collective-permute-done | bytes 262176 | tf_op jit(solution)/shard_map/ppermute | solution.py:34
  119.8 2.8 %collective-permute-done.28 = bf16[256,512]{1,0:T(8,128)(2,1)S(1)} collective-permute-done((bf16[256,512]{1,0:T(8,128)(2,1)S(1)}, bf16[256,512]{1,0:T(8,128)(2,1)S(1)}, u32[]{:S(2)}, u32[]{:S(2)}) %collective-permute-start.28) | collective-permute-done | bytes 262176 | tf_op jit(solution)/shard_map/ppermute | solution.py:34
  122.6 0.8 add_convert_fusion
  (77 shorter events, 1.6 us)
Async XLA Ops:
  0.0 57.4 %copy-start = (f32[3,3,512]{2,1,0:T(4,128)S(1)}, f32[3,3,512]{2,1,0:T(4,128)}, u32[]{:S(2)}) copy-start(f32[3,3,512]{2,1,0:T(4,128)} %param.8) | copy-start | bytes 55300
  0.0 1.7 %collective-permute-start = (bf16[256,512]{1,0:T(8,128)(2,1)}, bf16[256,512]{1,0:T(8,128)(2,1)S(1)}, u32[]{:S(2)}, u32[]{:S(2)}) collective-permute-start(bf16[256,512]{1,0:T(8,128)(2,1)} %param.6), channel_id=1, source_target_pairs={{0,8},{8,0},{1,9},{9,1},{2,10},{10,2},{3,11},{11,3},{4,12},{12,4},... | collective-permute-start | bytes 786440 | tf_op jit(solution)/shard_map/ppermute | solution.py:14
  1.8 4.7 %collective-permute-start.3 = (bf16[3,128,256]{2,1,0:T(8,128)(2,1)S(1)}, bf16[3,128,256]{2,1,0:T(8,128)(2,1)S(1)}, u32[]{:S(2)}, u32[]{:S(2)}) collective-permute-start(bf16[3,128,256]{2,1,0:T(8,128)(2,1)S(1)} %get-tuple-element.32), channel_id=1, source_target_pairs={{0,8},{8,0},{1,9},{9,1},{2,10},{10,2},{3,11},{11,3},{4,12},{12,4},... | collective-permute-start | bytes 589832 | tf_op jit(solution)/shard_map/ppermute | solution.py:14
  3.1 5.8 %collective-permute-start.1 = (bf16[16,512]{1,0:T(8,128)(2,1)S(1)}, bf16[16,512]{1,0:T(8,128)(2,1)S(1)}, u32[]{:S(2)}, u32[]{:S(2)}) collective-permute-start(bf16[16,512]{1,0:T(8,128)(2,1)S(1)} %slice.64), channel_id=1, source_target_pairs={{0,16},{8,24},{16,32},{24,40},{32,48},{40,56},{48,64},{56,72},{64,... | collective-permute-start | bytes 49160 | tf_op jit(solution)/shard_map/ppermute | solution.py:259
  6.7 7.9 %collective-permute-start.4 = (bf16[256,768]{1,0:T(8,128)(2,1)S(1)}, bf16[256,768]{1,0:T(8,128)(2,1)S(1)}, u32[]{:S(2)}, u32[]{:S(2)}) collective-permute-start(bf16[256,768]{1,0:T(8,128)(2,1)S(1)} %pad_maximum_fusion.1.own), channel_id=1, source_target_pairs={{0,16},{8,72},{16,32},{24,88},{32,48},{40,104},{48,0},{56,120},{64... | collective-permute-start | bytes 1179656 | tf_op jit(solution)/shard_map/ppermute | solution.py:25
  8.0 7.9 %collective-permute-start.5 = (bf16[256,768]{1,0:T(8,128)(2,1)S(1)}, bf16[256,768]{1,0:T(8,128)(2,1)S(1)}, u32[]{:S(2)}, u32[]{:S(2)}) collective-permute-start(bf16[256,768]{1,0:T(8,128)(2,1)S(1)} %pad_maximum_fusion.1.own), channel_id=1, source_target_pairs={{0,48},{8,200},{16,0},{24,216},{32,16},{40,232},{48,32},{56,248},{... | collective-permute-start | bytes 1179656 | tf_op jit(solution)/shard_map/ppermute | solution.py:25
  8.9 13.4 %copy-start.3 = (bf16[528,512]{1,0:T(8,128)(2,1)}, bf16[528,512]{1,0:T(8,128)(2,1)S(1)}, u32[]{:S(2)}) copy-start(bf16[528,512]{1,0:T(8,128)(2,1)S(1)} %pad_maximum_fusion.refs_0_) | copy-start | bytes 1622020
  8.9 13.3 %collective-permute-start.2 = (bf16[528,512]{1,0:T(8,128)(2,1)S(1)}, bf16[528,512]{1,0:T(8,128)(2,1)S(1)}, u32[]{:S(2)}, u32[]{:S(2)}) collective-permute-start(bf16[528,512]{1,0:T(8,128)(2,1)S(1)} %pad_maximum_fusion.refs_0_), channel_id=1, source_target_pairs={{0,1},{1,2},{2,3},{3,4},{4,5},{5,6},{6,7},{7,0},{8,15},{9,8},{10,9... | collective-permute-start | bytes 1622024 | tf_op jit(solution)/shard_map/ppermute | solution.py:34
  14.6 7.6 %collective-permute-start.11 = (bf16[128,768]{1,0:T(8,128)(2,1)S(1)}, bf16[128,768]{1,0:T(8,128)(2,1)S(1)}, u32[]{:S(2)}, u32[]{:S(2)}) collective-permute-start(bf16[128,768]{1,0:T(8,128)(2,1)S(1)} %slice.68), channel_id=1, source_target_pairs={{0,16},{8,72},{16,32},{24,88},{32,48},{40,104},{48,0},{56,120},{64... | collective-permute-start | bytes 589832 | tf_op jit(solution)/shard_map/ppermute | solution.py:25
  15.9 6.3 %collective-permute-start.12 = (bf16[128,768]{1,0:T(8,128)(2,1)S(1)}, bf16[128,768]{1,0:T(8,128)(2,1)S(1)}, u32[]{:S(2)}, u32[]{:S(2)}) collective-permute-start(bf16[128,768]{1,0:T(8,128)(2,1)S(1)} %slice.69), channel_id=1, source_target_pairs={{0,48},{8,200},{16,0},{24,216},{32,16},{40,232},{48,32},{56,248},{... | collective-permute-start | bytes 589832 | tf_op jit(solution)/shard_map/ppermute | solution.py:25
  22.2 16.7 %copy-start.7 = (bf16[528,512]{1,0:T(8,128)(2,1)}, bf16[528,512]{1,0:T(8,128)(2,1)S(1)}, u32[]{:S(2)}) copy-start(bf16[528,512]{1,0:T(8,128)(2,1)S(1)} %collective-permute-done.2.refs_1_) | copy-start | bytes 1622020
  22.2 10.6 %collective-permute-start.6 = (bf16[528,512]{1,0:T(8,128)(2,1)S(1)}, bf16[528,512]{1,0:T(8,128)(2,1)S(1)}, u32[]{:S(2)}, u32[]{:S(2)}) collective-permute-start(bf16[528,512]{1,0:T(8,128)(2,1)S(1)} %collective-permute-done.2.refs_1_), channel_id=1, source_target_pairs={{0,1},{1,2},{2,3},{3,4},{4,5},{5,6},{6,7},{7,0},{8,15},{9,8},{10,9... | collective-permute-start | bytes 1622024 | tf_op jit(solution)/shard_map/ppermute | solution.py:34
  22.3 24.0 %copy-start.1 = (bf16[1024,512]{1,0:T(8,128)(2,1)}, bf16[1024,512]{1,0:T(8,128)(2,1)S(1)}, u32[]{:S(2)}) copy-start(bf16[1024,512]{1,0:T(8,128)(2,1)S(1)} %get-tuple-element.37.refs_9_) | copy-start | bytes 3145732
  22.3 33.8 %copy-start.2 = (bf16[1024,256]{1,0:T(8,128)(2,1)}, bf16[1024,256]{1,0:T(8,128)(2,1)S(1)}, u32[]{:S(2)}) copy-start(bf16[1024,256]{1,0:T(8,128)(2,1)S(1)} %get-tuple-element.38.refs_9_) | copy-start | bytes 1572868
  22.3 16.1 %collective-permute-start.13 = (bf16[1024,512]{1,0:T(8,128)(2,1)S(1)}, bf16[1024,512]{1,0:T(8,128)(2,1)S(1)}, u32[]{:S(2)}, u32[]{:S(2)}) collective-permute-start(bf16[1024,512]{1,0:T(8,128)(2,1)S(1)} %get-tuple-element.37.refs_9_), channel_id=1, source_target_pairs={{0,64},{8,24},{16,80},{24,40},{32,96},{40,56},{48,112},{56,8},{64,... | collective-permute-start | bytes 3145736 | tf_op jit(solution)/shard_map/ppermute | solution.py:25
  24.0 14.9 %collective-permute-start.15 = (bf16[1024,512]{1,0:T(8,128)(2,1)S(1)}, bf16[1024,512]{1,0:T(8,128)(2,1)S(1)}, u32[]{:S(2)}, u32[]{:S(2)}) collective-permute-start(bf16[1024,512]{1,0:T(8,128)(2,1)S(1)} %get-tuple-element.37.refs_9_), channel_id=1, source_target_pairs={{0,192},{8,56},{16,208},{24,8},{32,224},{40,24},{48,240},{56,40},{... | collective-permute-start | bytes 3145736 | tf_op jit(solution)/shard_map/ppermute | solution.py:25
  25.6 16.2 %collective-permute-start.8 = (bf16[528,512]{1,0:T(8,128)(2,1)S(1)}, bf16[528,512]{1,0:T(8,128)(2,1)S(1)}, u32[]{:S(2)}, u32[]{:S(2)}) collective-permute-start(bf16[528,512]{1,0:T(8,128)(2,1)S(1)} %collective-permute-done.2.refs_1_), channel_id=1, source_target_pairs={{0,8},{8,0},{1,9},{9,1},{2,10},{10,2},{3,11},{11,3},{4,12},{12,4},... | collective-permute-start | bytes 1622024 | tf_op jit(solution)/shard_map/ppermute | solution.py:14
  32.7 22.7 %copy-start.8 = (bf16[528,512]{1,0:T(8,128)(2,1)}, bf16[528,512]{1,0:T(8,128)(2,1)S(1)}, u32[]{:S(2)}) copy-start(bf16[528,512]{1,0:T(8,128)(2,1)S(1)} %collective-permute-done.6.refs_2_) | copy-start | bytes 1622020
  32.7 10.6 %collective-permute-start.7 = (bf16[528,512]{1,0:T(8,128)(2,1)S(1)}, bf16[528,512]{1,0:T(8,128)(2,1)S(1)}, u32[]{:S(2)}, u32[]{:S(2)}) collective-permute-start(bf16[528,512]{1,0:T(8,128)(2,1)S(1)} %collective-permute-done.6.refs_2_), channel_id=1, source_target_pairs={{0,1},{1,2},{2,3},{3,4},{4,5},{5,6},{6,7},{7,0},{8,15},{9,8},{10,9... | collective-permute-start | bytes 1622024 | tf_op jit(solution)/shard_map/ppermute | solution.py:34
  32.7 13.6 %collective-permute-start.9 = (bf16[528,512]{1,0:T(8,128)(2,1)S(1)}, bf16[528,512]{1,0:T(8,128)(2,1)S(1)}, u32[]{:S(2)}, u32[]{:S(2)}) collective-permute-start(bf16[528,512]{1,0:T(8,128)(2,1)S(1)} %collective-permute-done.6.refs_2_), channel_id=1, source_target_pairs={{0,8},{8,0},{1,9},{9,1},{2,10},{10,2},{3,11},{11,3},{4,12},{12,4},... | collective-permute-start | bytes 1622024 | tf_op jit(solution)/shard_map/ppermute | solution.py:14
  38.4 3.4 %copy-start.5 = (bf16[1024,512]{1,0:T(8,128)(2,1)}, bf16[1024,512]{1,0:T(8,128)(2,1)S(1)}, u32[]{:S(2)}) copy-start(bf16[1024,512]{1,0:T(8,128)(2,1)S(1)} %collective-permute-done.13.refs_10_) | copy-start | bytes 3145732
  38.4 10.4 %collective-permute-start.17 = (bf16[1024,256]{1,0:T(8,128)(2,1)S(1)}, bf16[1024,256]{1,0:T(8,128)(2,1)S(1)}, u32[]{:S(2)}, u32[]{:S(2)}) collective-permute-start(bf16[1024,256]{1,0:T(8,128)(2,1)S(1)} %get-tuple-element.38.refs_9_), channel_id=1, source_target_pairs={{0,64},{8,24},{16,80},{24,40},{32,96},{40,56},{48,112},{56,8},{64,... | collective-permute-start | bytes 1572872 | tf_op jit(solution)/shard_map/ppermute | solution.py:25
  38.8 18.6 %copy-start.15 = (f32[16,512]{1,0:T(8,128)S(1)}, f32[16,512]{1,0:T(8,128)}, u32[]{:S(2)}) copy-start(f32[16,512]{1,0:T(8,128)} %param.9) | copy-start | bytes 98308
  38.8 18.6 %copy-start.16 = (f32[16,512]{1,0:T(8,128)S(1)}, f32[16,512]{1,0:T(8,128)}, u32[]{:S(2)}) copy-start(f32[16,512]{1,0:T(8,128)} %param.10) | copy-start | bytes 98308
  38.9 16.4 %copy-start.6 = (bf16[1024,512]{1,0:T(8,128)(2,1)}, bf16[1024,512]{1,0:T(8,128)(2,1)S(1)}, u32[]{:S(2)}) copy-start(bf16[1024,512]{1,0:T(8,128)(2,1)S(1)} %collective-permute-done.15.refs_11_) | copy-start | bytes 3145732
  38.9 9.9 %collective-permute-start.18 = (bf16[1024,256]{1,0:T(8,128)(2,1)S(1)}, bf16[1024,256]{1,0:T(8,128)(2,1)S(1)}, u32[]{:S(2)}, u32[]{:S(2)}) collective-permute-start(bf16[1024,256]{1,0:T(8,128)(2,1)S(1)} %get-tuple-element.38.refs_9_), channel_id=1, source_target_pairs={{0,192},{8,56},{16,208},{24,8},{32,224},{40,24},{48,240},{56,40},{... | collective-permute-start | bytes 1572872 | tf_op jit(solution)/shard_map/ppermute | solution.py:25
  41.9 13.5 %copy-start.9 = (bf16[528,512]{1,0:T(8,128)(2,1)}, bf16[528,512]{1,0:T(8,128)(2,1)S(1)}, u32[]{:S(2)}) copy-start(bf16[528,512]{1,0:T(8,128)(2,1)S(1)} %collective-permute-done.8.refs_5_) | copy-start | bytes 1622020
  41.9 13.4 %collective-permute-start.14 = (bf16[512,512]{1,0:T(8,128)(2,1)S(1)}, bf16[512,512]{1,0:T(8,128)(2,1)S(1)}, u32[]{:S(2)}, u32[]{:S(2)}) collective-permute-start(bf16[512,512]{1,0:T(8,128)(2,1)S(1)} %slice.70), channel_id=1, source_target_pairs={{0,64},{8,24},{16,80},{24,40},{32,96},{40,56},{48,112},{56,8},{64,... | collective-permute-start | bytes 1572872 | tf_op jit(solution)/shard_map/ppermute | solution.py:25
  43.3 14.5 %copy-start.4 = (bf16[528,512]{1,0:T(8,128)(2,1)}, bf16[528,512]{1,0:T(8,128)(2,1)S(1)}, u32[]{:S(2)}) copy-start(bf16[528,512]{1,0:T(8,128)(2,1)S(1)} %collective-permute-done.7.refs_3_) | copy-start | bytes 1622020
  43.3 12.0 %collective-permute-start.16 = (bf16[512,512]{1,0:T(8,128)(2,1)S(1)}, bf16[512,512]{1,0:T(8,128)(2,1)S(1)}, u32[]{:S(2)}, u32[]{:S(2)}) collective-permute-start(bf16[512,512]{1,0:T(8,128)(2,1)S(1)} %slice.71), channel_id=1, source_target_pairs={{0,192},{8,56},{16,208},{24,8},{32,224},{40,24},{48,240},{56,40},{... | collective-permute-start | bytes 1572872 | tf_op jit(solution)/shard_map/ppermute | solution.py:25
  46.4 9.1 %copy-start.10 = (bf16[528,512]{1,0:T(8,128)(2,1)}, bf16[528,512]{1,0:T(8,128)(2,1)S(1)}, u32[]{:S(2)}) copy-start(bf16[528,512]{1,0:T(8,128)(2,1)S(1)} %collective-permute-done.9.refs_6_) | copy-start | bytes 1622020
  46.4 8.9 %collective-permute-start.10 = (bf16[528,256]{1,0:T(8,128)(2,1)S(1)}, bf16[528,256]{1,0:T(8,128)(2,1)S(1)}, u32[]{:S(2)}, u32[]{:S(2)}) collective-permute-start(bf16[528,256]{1,0:T(8,128)(2,1)S(1)} %constant_dynamic-slice_fusion.1), channel_id=1, source_target_pairs={{0,1},{1,2},{2,3},{3,4},{4,5},{5,6},{6,7},{7,0},{8,15},{9,8},{10,9... | collective-permute-start | bytes 811016 | tf_op jit(solution)/shard_map/ppermute | solution.py:34
  48.8 6.6 %copy-start.13 = (bf16[1024,256]{1,0:T(8,128)(2,1)}, bf16[1024,256]{1,0:T(8,128)(2,1)S(1)}, u32[]{:S(2)}) copy-start(bf16[1024,256]{1,0:T(8,128)(2,1)S(1)} %collective-permute-done.17.refs_10_) | copy-start | bytes 1572868
  48.8 6.6 %copy-start.14 = (bf16[1024,256]{1,0:T(8,128)(2,1)}, bf16[1024,256]{1,0:T(8,128)(2,1)S(1)}, u32[]{:S(2)}) copy-start(bf16[1024,256]{1,0:T(8,128)(2,1)S(1)} %collective-permute-done.18.refs_11_) | copy-start | bytes 1572868
  55.3 2.6 %copy-start.12 = (bf16[528,256]{1,0:T(8,128)(2,1)}, bf16[528,256]{1,0:T(8,128)(2,1)S(1)}, u32[]{:S(2)}) copy-start(bf16[528,256]{1,0:T(8,128)(2,1)S(1)} %collective-permute-done.10.refs_4_) | copy-start | bytes 811012
  55.3 2.5 %collective-permute-start.19 = (bf16[528,512]{1,0:T(8,128)(2,1)S(1)}, bf16[528,512]{1,0:T(8,128)(2,1)S(1)}, u32[]{:S(2)}, u32[]{:S(2)}) collective-permute-start(bf16[528,512]{1,0:T(8,128)(2,1)S(1)} %collective-permute-done.7.refs_3_), channel_id=1, source_target_pairs={{0,8},{8,0},{1,9},{9,1},{2,10},{10,2},{3,11},{11,3},{4,12},{12,4},... | collective-permute-start | bytes 1622024 | tf_op jit(solution)/shard_map/ppermute | solution.py:14
  55.4 2.4 %collective-permute-start.20 = (bf16[528,256]{1,0:T(8,128)(2,1)S(1)}, bf16[528,256]{1,0:T(8,128)(2,1)}, u32[]{:S(2)}, u32[]{:S(2)}) collective-permute-start(bf16[528,256]{1,0:T(8,128)(2,1)S(1)} %collective-permute-done.10.refs_4_), channel_id=1, source_target_pairs={{0,8},{8,0},{1,9},{9,1},{2,10},{10,2},{3,11},{11,3},{4,12},{12,4},... | collective-permute-start | bytes 811016 | tf_op jit(solution)/shard_map/ppermute | solution.py:14
  56.1 18.4 %collective-permute-start.21 = (bf16[1024,256]{1,0:T(8,128)(2,1)S(1)}, bf16[1024,256]{1,0:T(8,128)(2,1)}, u32[]{:S(2)}, u32[]{:S(2)}) collective-permute-start(bf16[1024,256]{1,0:T(8,128)(2,1)S(1)} %get-tuple-element.38.refs_9_), channel_id=1, source_target_pairs={{0,128},{8,40},{16,144},{24,56},{32,160},{40,8},{48,176},{56,24},{... | collective-permute-start | bytes 1572872 | tf_op jit(solution)/shard_map/ppermute | solution.py:25
  66.8 15.3 %all-to-all-start = ((f32[16,16,256]{2,1,0:T(8,128)}), f32[16,16,256]{2,1,0:T(8,128)S(1)}, u32[]{:S(2)}, u32[]{:S(2)}) async-start(f32[16,16,256]{2,1,0:T(8,128)} %get-tuple-element.47), calls=%async_computation | async-start | bytes 524288 | tf_op jit(solution)/shard_map/all_to_all | solution.py:328
  84.8 1.6 %collective-permute-start.22 = (bf16[512,256]{1,0:T(8,128)(2,1)S(1)}, bf16[512,256]{1,0:T(8,128)(2,1)S(1)}, u32[]{:S(2)}, u32[]{:S(2)}) collective-permute-start(bf16[512,256]{1,0:T(8,128)(2,1)S(1)} %get-tuple-element.48.mine), channel_id=1, source_target_pairs={{0,8},{8,0},{1,9},{9,1},{2,10},{10,2},{3,11},{11,3},{4,12},{12,4},... | collective-permute-start | bytes 786440 | tf_op jit(solution)/shard_map/ppermute | solution.py:14
  88.3 11.3 %collective-permute-start.25 = (bf16[512,256]{1,0:T(8,128)(2,1)S(1)}, bf16[512,256]{1,0:T(8,128)(2,1)S(1)}, u32[]{:S(2)}, u32[]{:S(2)}) collective-permute-start(bf16[512,256]{1,0:T(8,128)(2,1)S(1)} %get-tuple-element.54), channel_id=1, source_target_pairs={{0,2},{1,3},{2,4},{3,5},{4,6},{5,7},{6,0},{7,1},{8,14},{9,15},{10,... | collective-permute-start | bytes 786440 | tf_op jit(solution)/shard_map/ppermute | solution.py:34
  91.7 12.5 %collective-permute-start.24 = (bf16[256,512]{1,0:T(8,128)(2,1)S(1)}, bf16[256,512]{1,0:T(8,128)(2,1)S(1)}, u32[]{:S(2)}, u32[]{:S(2)}) collective-permute-start(bf16[256,512]{1,0:T(8,128)(2,1)S(1)} %get-tuple-element.59), channel_id=1, source_target_pairs={{0,1},{1,2},{2,3},{3,4},{4,5},{5,6},{6,7},{7,0},{8,15},{9,8},{10,9... | collective-permute-start | bytes 786440 | tf_op jit(solution)/shard_map/ppermute | solution.py:34
  93.6 13.3 %collective-permute-start.23 = (bf16[256,512]{1,0:T(8,128)(2,1)S(1)}, bf16[256,512]{1,0:T(8,128)(2,1)S(1)}, u32[]{:S(2)}, u32[]{:S(2)}) collective-permute-start(bf16[256,512]{1,0:T(8,128)(2,1)S(1)} %get-tuple-element.60), channel_id=1, source_target_pairs={{0,1},{1,2},{2,3},{3,4},{4,5},{5,6},{6,7},{7,0},{8,15},{9,8},{10,9... | collective-permute-start | bytes 786440 | tf_op jit(solution)/shard_map/ppermute | solution.py:34
  104.2 7.9 %collective-permute-start.27 = (bf16[256,512]{1,0:T(8,128)(2,1)S(1)}, bf16[256,512]{1,0:T(8,128)(2,1)S(1)}, u32[]{:S(2)}, u32[]{:S(2)}) collective-permute-start(bf16[256,512]{1,0:T(8,128)(2,1)S(1)} %slice_add_fusion.1), channel_id=1, source_target_pairs={{0,1},{1,2},{2,3},{3,4},{4,5},{5,6},{6,7},{7,0},{8,15},{9,8},{10,9... | collective-permute-start | bytes 786440 | tf_op jit(solution)/shard_map/ppermute | solution.py:34
  107.0 7.9 %collective-permute-start.26 = (bf16[256,512]{1,0:T(8,128)(2,1)S(1)}, bf16[256,512]{1,0:T(8,128)(2,1)S(1)}, u32[]{:S(2)}, u32[]{:S(2)}) collective-permute-start(bf16[256,512]{1,0:T(8,128)(2,1)S(1)} %slice_add_fusion), channel_id=1, source_target_pairs={{0,1},{1,2},{2,3},{3,4},{4,5},{5,6},{6,7},{7,0},{8,15},{9,8},{10,9... | collective-permute-start | bytes 786440 | tf_op jit(solution)/shard_map/ppermute | solution.py:34
  112.1 7.7 %collective-permute-start.29 = (bf16[256,512]{1,0:T(8,128)(2,1)S(1)}, bf16[256,512]{1,0:T(8,128)(2,1)S(1)}, u32[]{:S(2)}, u32[]{:S(2)}) collective-permute-start(bf16[256,512]{1,0:T(8,128)(2,1)S(1)} %slice_add_fusion.2), channel_id=1, source_target_pairs={{0,1},{1,2},{2,3},{3,4},{4,5},{5,6},{6,7},{7,0},{8,15},{9,8},{10,9... | collective-permute-start | bytes 786440 | tf_op jit(solution)/shard_map/ppermute | solution.py:34
  114.9 7.7 %collective-permute-start.28 = (bf16[256,512]{1,0:T(8,128)(2,1)S(1)}, bf16[256,512]{1,0:T(8,128)(2,1)S(1)}, u32[]{:S(2)}, u32[]{:S(2)}) collective-permute-start(bf16[256,512]{1,0:T(8,128)(2,1)S(1)} %slice_add_fusion.3), channel_id=1, source_target_pairs={{0,1},{1,2},{2,3},{3,4},{4,5},{5,6},{6,7},{7,0},{8,15},{9,8},{10,9... | collective-permute-start | bytes 786440 | tf_op jit(solution)/shard_map/ppermute | solution.py:34
  119.8 2.8 %collective-permute-start.30 = (bf16[256,512]{1,0:T(8,128)(2,1)S(1)}, bf16[256,512]{1,0:T(8,128)(2,1)S(1)}, u32[]{:S(2)}, u32[]{:S(2)}) collective-permute-start(bf16[256,512]{1,0:T(8,128)(2,1)S(1)} %collective-permute-done.29), channel_id=1, source_target_pairs={{0,8},{8,0},{1,9},{9,1},{2,10},{10,2},{3,11},{11,3},{4,12},{12,4},... | collective-permute-start | bytes 786440 | tf_op jit(solution)/shard_map/ppermute | solution.py:14
  (1 other events, 0.8 us)
